TPU v7x, 32 devices: a whole 2x2x4 slice. The times are simulated.
32 devices in a mesh: los: 32 (over z, y, x, core), sky: 1.
Axes of the slice: x: 2, y: 2, z: 4, core: 2. Of those that a mesh axis runs over, the one named last changes fastest.
Arguments:
- part_cell: int32 [3, 131072], P(None, ('los', 'sky')), may hold values from 0 to 127, as said below
- part_frac: float32 [3, 131072], P(None, ('los', 'sky')), may hold values from 0 to 1
- los_offset: int32 [131072], P(('los', 'sky')), may hold values from -32 to 32
- block_dest: int32 [1024], P(('los', 'sky')), may hold values from 0 to 31, as said below
- block_count: int32 [1024], P(('los', 'sky')), may hold values from 96 to 128, as said below
- selection: float32 [128, 4, 128], P('los', 'sky'), may hold values from 0.3 to 3
- galaxy_counts: int32 [128, 4, 128], P('los', 'sky'), may hold values from 0 to 5
- bias_exp: float32 [128], P('los'), may hold values from 1.2 to 2.2
- rsd_factor: float32 [128], P('los'), may hold values from 0.5 to 2
Outputs:
- grad_pos: float32 [3, 131072], P(None, ('los', 'sky'))
- grad_vel: float32 [131072], P(('los', 'sky'))
Inputs may be any that keep to these rules, and one draw needn't show every extreme that they name: Component 1 of a particle lies in the first-sky cells of its own device's columns, and (part_cell[0] + los_offset) mod 128 lies in cells block_dest * 4 to block_dest * 4 + 3 of the particle's block, for every slot. `block_dest`: the 32 blocks of one device name any slab at most 2 times, and on every device some slab is named exactly 2 times. `block_count`: A block's live particles are its first slots; every device has a full block.
All inputs are finite; a program needn't handle non-finite values.
Results may differ from a plain program's by a relative error of at most 0.000098.
Values sent between devices are 32-bit elements; how exact they have to be, the bound alone decides.
No kernel may reach another device: no remote copies, remote signals or barrier semaphores. Data moves between devices by JAX's collectives and lax.ppermute only.
A program may use at most 64 MiB of HBM per device.

v0:
```python
import jax
import jax.numpy as jnp
from jax import lax
from jax.sharding import PartitionSpec as P


def passed_along(block, axis, distance):
    devices = range(lax.axis_size(axis))
    route = [((i - distance) % len(devices), i) for i in devices]
    return lax.ppermute(block, axis, route)


def factor(fraction, bit):
    return fraction if bit else 1.0 - fraction


def slope(bit):
    return 1.0 if bit else -1.0


def with_sky_rim(field):
    from_right = passed_along(field[:, 0], "sky", -1)
    return jnp.concatenate([field, from_right[:, None]], axis=1)


def group_tables(group_rows, plane_cols, plane_size, deep_width):
    flat_rows = group_rows.transpose(1, 0, 2).reshape(group_rows.shape[1], -1)
    los_here = flat_rows[0].astype(jnp.int32)
    sky_here = flat_rows[1].astype(jnp.int32)
    deep_here = flat_rows[2].astype(jnp.int32)
    frac_los = flat_rows[3]
    frac_sky = flat_rows[4]
    frac_deep = flat_rows[5]
    live_here = flat_rows[6]
    base = los_here * plane_cols + sky_here
    plane_iota = jnp.arange(plane_size, dtype=jnp.int32)[None, :]
    plane_val = jnp.zeros((base.shape[0], plane_size), jnp.float32)
    plane_los = jnp.zeros((base.shape[0], plane_size), jnp.float32)
    plane_sky = jnp.zeros((base.shape[0], plane_size), jnp.float32)
    for los_bit in (0, 1):
        for sky_bit in (0, 1):
            hit = (plane_iota == (base + los_bit * plane_cols + sky_bit)[:, None]).astype(
                jnp.float32
            )
            weight_los = factor(frac_los, los_bit)
            weight_sky = factor(frac_sky, sky_bit)
            plane_val = plane_val + (weight_los * weight_sky)[:, None] * hit
            plane_los = plane_los + (slope(los_bit) * weight_sky)[:, None] * hit
            plane_sky = plane_sky + (weight_los * slope(sky_bit))[:, None] * hit
    deep_iota = jnp.arange(deep_width, dtype=jnp.int32)[None, :]
    lower = deep_iota == deep_here[:, None]
    upper = deep_iota == jnp.mod(deep_here + 1, deep_width)[:, None]
    deep_val = jnp.where(lower, 1.0 - frac_deep[:, None], 0.0) + jnp.where(
        upper, frac_deep[:, None], 0.0
    )
    deep_slope = upper.astype(jnp.float32) - lower.astype(jnp.float32)
    return (plane_val, plane_los, plane_sky, deep_val, deep_slope, live_here)


def on_device(
    part_cell,
    part_frac,
    los_offset,
    block_dest,
    block_count,
    selection,
    galaxy_counts,
    bias_exp,
    rsd_factor,
):
    slab_rows, sky_width, deep_width = selection.shape
    los_devices = lax.axis_size("los")
    sky_here = lax.axis_index("sky")
    block_total = block_dest.shape[0]
    block_size = part_cell.shape[1] // block_total
    capacity = 2 * block_total // los_devices
    row_in_slab = jnp.mod(part_cell[0] + los_offset, slab_rows)
    slot_index = jnp.arange(block_size, dtype=jnp.int32)
    alive = (slot_index[None, :] < block_count[:, None]).astype(jnp.float32).reshape(-1)
    sky_local = part_cell[1] - sky_here * sky_width
    deep_cell = part_cell[2]
    located = jnp.stack(
        [
            row_in_slab.astype(jnp.float32),
            sky_local.astype(jnp.float32),
            deep_cell.astype(jnp.float32),
        ]
    )
    payload = jnp.concatenate([located, part_frac], axis=0)
    payload = payload.reshape(6, block_total, block_size).transpose(1, 0, 2)
    member = (block_dest[:, None] == jnp.arange(los_devices, dtype=jnp.int32)[None, :]).astype(
        jnp.int32
    )
    before = jnp.cumsum(member, axis=0) - member
    ranking = jnp.sum(before * member, axis=1)
    target = block_dest * capacity + ranking
    outgoing = (
        jnp.zeros((los_devices * capacity, 6, block_size), jnp.float32).at[target].set(payload)
    )
    outgoing = outgoing.reshape(los_devices, capacity, 6, block_size)
    out_counts = jnp.zeros((los_devices * capacity,), jnp.int32).at[target].set(block_count)
    out_counts = out_counts.reshape(los_devices, capacity)
    arrived, arrived_counts = (
        lax.all_to_all(outgoing, "los", split_axis=0, concat_axis=0, tiled=True),
        lax.all_to_all(out_counts, "los", split_axis=0, concat_axis=0, tiled=True),
    )
    recv_blocks = los_devices * capacity
    arrived = arrived.reshape(recv_blocks, 6, block_size)
    slot_live = (slot_index[None, :] < arrived_counts.reshape(-1)[:, None]).astype(jnp.float32)
    recv_los = arrived[:, 0].astype(jnp.int32)
    plane_rows = slab_rows + 1
    plane_cols = sky_width + 1
    plane_size = plane_rows * plane_cols
    group = 4
    group_count = recv_blocks // group
    grouped = jnp.concatenate([arrived, slot_live[:, None, :]], axis=1).reshape(
        group_count, group, 7, block_size
    )

    def deposit(painted, group_rows):
        plane_val, plane_los, plane_sky, deep_val, deep_slope, live_here = group_tables(
            group_rows, plane_cols, plane_size, deep_width
        )
        term = lax.dot_general(
            plane_val * live_here[:, None],
            deep_val,
            (((0,), (0,)), ((), ())),
            precision=lax.Precision.HIGHEST,
            preferred_element_type=jnp.float32,
        )
        return (painted + term, None)

    painted, unused = lax.scan(deposit, jnp.zeros((plane_size, deep_width), jnp.float32), grouped)
    painted = painted.reshape(plane_rows, plane_cols, deep_width)
    from_below = passed_along(painted[slab_rows], "los", 1)
    core = painted[:slab_rows].at[0].add(from_below)
    from_left = passed_along(core[:, sky_width], "sky", 1)
    density = core[:, :sky_width].at[:, 0].add(from_left)
    shifted = density + 0.5
    exponent = bias_exp[:, None, None]
    intensity = selection * jnp.exp(exponent * jnp.log(shifted))
    cotangent = (
        (1.0 - galaxy_counts.astype(jnp.float32) / intensity) * exponent * intensity / shifted
    )
    sky_framed = with_sky_rim(cotangent)
    from_above = passed_along(sky_framed[0], "los", -1)
    extended = jnp.concatenate([sky_framed, from_above[None]], axis=0)
    field_plane = extended.reshape(plane_size, deep_width)

    def pull(group_rows):
        plane_val, plane_los, plane_sky, deep_val, deep_slope, live_here = group_tables(
            group_rows, plane_cols, plane_size, deep_width
        )
        stacked = jnp.concatenate([plane_los, plane_sky, plane_val], axis=0)
        picked = jnp.dot(
            stacked,
            field_plane,
            precision=lax.Precision.HIGHEST,
            preferred_element_type=jnp.float32,
        )
        picked = picked.reshape(3, -1, deep_width)
        sum_los = jnp.sum(picked[0] * deep_val, axis=1)
        sum_sky = jnp.sum(picked[1] * deep_val, axis=1)
        sum_deep = jnp.sum(picked[2] * deep_slope, axis=1)
        return jnp.stack([sum_los, sum_sky, sum_deep]).reshape(3, group, block_size)

    pulled = lax.map(pull, grouped)
    pulled = pulled.transpose(0, 2, 1, 3).reshape(recv_blocks, 3, block_size)
    rate_each = rsd_factor[recv_los]
    returned = (
        jnp.concatenate([pulled, (rate_each * pulled[:, 0])[:, None]], axis=1)
        * slot_live[:, None, :]
    )
    returned = returned.reshape(los_devices, capacity, 4, block_size)
    came_back = lax.all_to_all(returned, "los", split_axis=0, concat_axis=0, tiled=True)
    own_rows = came_back.reshape(los_devices * capacity, 4, block_size)[target]
    own_rows = own_rows.transpose(1, 0, 2).reshape(4, -1)
    grad_pos = own_rows[:3] * alive[None, :]
    grad_vel = own_rows[3] * alive
    return (grad_pos, grad_vel)


def solution(mesh):
    return jax.shard_map(
        on_device,
        mesh=mesh,
        in_specs=(
            P(None, ("los", "sky")),
            P(None, ("los", "sky")),
            P(("los", "sky")),
            P(("los", "sky")),
            P(("los", "sky")),
            P("los", "sky", None),
            P("los", "sky", None),
            P("los"),
            P("los"),
        ),
        out_specs=(P(None, ("los", "sky")), P(("los", "sky"))),
        check_vma=False,
    )
```

profile of v0, /device:TPU:0, one launch (start us, length us, event | category | flops | bytes accessed | tf_op | source)
XLA Modules:
  0.0 104.6 jit_solution(13451210798989442808)
XLA Ops:
  2.9 0.7 all_to_all.13
  3.7 7.3 %all-to-all-start.1 = ((s32[32,1,2]{2,1,0:T(1,128)}), s32[32,1,2]{2,1,0:T(1,128)S(1)}, u32[]{:S(2)}, u32[]{:S(2)}) async-start(s32[32,1,2]{2,1,0:T(1,128)} %bitcast.21), calls=%async_computation.1 | async-start | bytes 32768 | tf_op jit(solution)/shard_map/all_to_all | solution.py:105
  11.9 1.5 %scatter_fusion = f32[64,6,128]{2,1,0:T(8,128)S(1)} fusion(f32[64,6,128]{2,1,0:T(8,128)S(1)} %broadcast_in_dim.124, s32[32]{0:T(128)S(1)} %compare_select_fusion.1, f32[32,6,128]{2,1,0:T(8,128)S(1)} %maximum_bitcast_fusion), kind=kCustom, calls=%fused_computation.1 | custom fusion | bytes 295040 | tf_op jit(solution)/shard_map/scatter | solution.py:98
  13.4 0.8 copy.52
  14.2 3.8 %all-to-all-done.1 = s32[32,1,2]{2,1,0:T(1,128)S(1)} async-done(((s32[32,1,2]{2,1,0:T(1,128)}), s32[32,1,2]{2,1,0:T(1,128)S(1)}, u32[]{:S(2)}, u32[]{:S(2)}) %all-to-all-start.1) | async-done | bytes 288 | tf_op jit(solution)/shard_map/all_to_all | solution.py:105
  18.0 2.6 %all-to-all-start = ((f32[32,2,6,128]{3,1,2,0:T(2,128)}), f32[32,2,6,128]{3,1,2,0:T(2,128)S(1)}, u32[]{:S(2)}, u32[]{:S(2)}) async-start(f32[32,2,6,128]{3,1,2,0:T(2,128)} %copy.52), calls=%async_computation | async-start | bytes 393216 | tf_op jit(solution)/shard_map/all_to_all | solution.py:104
  22.0 7.5 %all-to-all-done = f32[32,2,6,128]{3,1,2,0:T(2,128)S(1)} async-done(((f32[32,2,6,128]{3,1,2,0:T(2,128)}), f32[32,2,6,128]{3,1,2,0:T(2,128)S(1)}, u32[]{:S(2)}, u32[]{:S(2)}) %all-to-all-start) | async-done | bytes 196640 | tf_op jit(solution)/shard_map/all_to_all | solution.py:104
  29.8 26.2 %while.28 = (s32[]{:T(128)}, f32[25,128]{1,0:T(8,128)S(1)}, f32[16,4,7,128]{3,2,1,0:T(8,128)S(1)}, s32[]{:T(128)}, s32[]{:T(128)}) while((s32[]{:T(128)}, f32[25,128]{1,0:T(8,128)S(1)}, f32[16,4,7,128]{3,2,1,0:T(8,128)S(1)}, s32[]{:T(128)}, s32[]{:T(128)}) %tuple.116), condition=%wide.region_5.6_spmd.clone, body=%wide.region_4.5_spmd.clone.sunk | while | flops 20162308 | bytes 136267 | solution.py:133
  29.9 1.5 %convolution_add_fusion.2 = f32[25,128]{1,0:T(8,128)S(1)} fusion(f32[512]{0:T(512)S(1)} %bitcast.144, s32[512]{0:T(512)S(1)} %get-tuple-element.311, f32[512]{0:T(512)S(1)} %get-tuple-element.314, s32[512]{0:T(512)S(1)} %bitcast.140, f32[512]{0:T(512)S(1)} %bitcast.154, f32[512]{0:T(512)S(1)} %get-tuple-element.316, s32[512]{0:T(512)S(1)} %get-tuple-element.317, ...), kind=kOutput, calls=%fused_computation.50.clone.1 | convolution fusion | flops 20148480 | bytes 52225 | tf_op jit(solution)/shard_map/while/body/eval_jaxpr/dot_general | solution.py:124
  31.5 1.5 %convolution_add_fusion.2 = f32[25,128]{1,0:T(8,128)S(1)} fusion(f32[512]{0:T(512)S(1)} %bitcast.144, s32[512]{0:T(512)S(1)} %get-tuple-element.311, f32[512]{0:T(512)S(1)} %get-tuple-element.314, s32[512]{0:T(512)S(1)} %bitcast.140, f32[512]{0:T(512)S(1)} %bitcast.154, f32[512]{0:T(512)S(1)} %get-tuple-element.316, s32[512]{0:T(512)S(1)} %get-tuple-element.317, ...), kind=kOutput, calls=%fused_computation.50.clone.1 | convolution fusion | flops 20148480 | bytes 52225 | tf_op jit(solution)/shard_map/while/body/eval_jaxpr/dot_general | solution.py:124
  33.2 1.5 %convolution_add_fusion.2 = f32[25,128]{1,0:T(8,128)S(1)} fusion(f32[512]{0:T(512)S(1)} %bitcast.144, s32[512]{0:T(512)S(1)} %get-tuple-element.311, f32[512]{0:T(512)S(1)} %get-tuple-element.314, s32[512]{0:T(512)S(1)} %bitcast.140, f32[512]{0:T(512)S(1)} %bitcast.154, f32[512]{0:T(512)S(1)} %get-tuple-element.316, s32[512]{0:T(512)S(1)} %get-tuple-element.317, ...), kind=kOutput, calls=%fused_computation.50.clone.1 | convolution fusion | flops 20148480 | bytes 52225 | tf_op jit(solution)/shard_map/while/body/eval_jaxpr/dot_general | solution.py:124
  34.8 1.5 %convolution_add_fusion.2 = f32[25,128]{1,0:T(8,128)S(1)} fusion(f32[512]{0:T(512)S(1)} %bitcast.144, s32[512]{0:T(512)S(1)} %get-tuple-element.311, f32[512]{0:T(512)S(1)} %get-tuple-element.314, s32[512]{0:T(512)S(1)} %bitcast.140, f32[512]{0:T(512)S(1)} %bitcast.154, f32[512]{0:T(512)S(1)} %get-tuple-element.316, s32[512]{0:T(512)S(1)} %get-tuple-element.317, ...), kind=kOutput, calls=%fused_computation.50.clone.1 | convolution fusion | flops 20148480 | bytes 52225 | tf_op jit(solution)/shard_map/while/body/eval_jaxpr/dot_general | solution.py:124
  36.4 1.5 %convolution_add_fusion.2 = f32[25,128]{1,0:T(8,128)S(1)} fusion(f32[512]{0:T(512)S(1)} %bitcast.144, s32[512]{0:T(512)S(1)} %get-tuple-element.311, f32[512]{0:T(512)S(1)} %get-tuple-element.314, s32[512]{0:T(512)S(1)} %bitcast.140, f32[512]{0:T(512)S(1)} %bitcast.154, f32[512]{0:T(512)S(1)} %get-tuple-element.316, s32[512]{0:T(512)S(1)} %get-tuple-element.317, ...), kind=kOutput, calls=%fused_computation.50.clone.1 | convolution fusion | flops 20148480 | bytes 52225 | tf_op jit(solution)/shard_map/while/body/eval_jaxpr/dot_general | solution.py:124
  38.1 1.5 %convolution_add_fusion.2 = f32[25,128]{1,0:T(8,128)S(1)} fusion(f32[512]{0:T(512)S(1)} %bitcast.144, s32[512]{0:T(512)S(1)} %get-tuple-element.311, f32[512]{0:T(512)S(1)} %get-tuple-element.314, s32[512]{0:T(512)S(1)} %bitcast.140, f32[512]{0:T(512)S(1)} %bitcast.154, f32[512]{0:T(512)S(1)} %get-tuple-element.316, s32[512]{0:T(512)S(1)} %get-tuple-element.317, ...), kind=kOutput, calls=%fused_computation.50.clone.1 | convolution fusion | flops 20148480 | bytes 52225 | tf_op jit(solution)/shard_map/while/body/eval_jaxpr/dot_general | solution.py:124
  39.7 1.5 %convolution_add_fusion.2 = f32[25,128]{1,0:T(8,128)S(1)} fusion(f32[512]{0:T(512)S(1)} %bitcast.144, s32[512]{0:T(512)S(1)} %get-tuple-element.311, f32[512]{0:T(512)S(1)} %get-tuple-element.314, s32[512]{0:T(512)S(1)} %bitcast.140, f32[512]{0:T(512)S(1)} %bitcast.154, f32[512]{0:T(512)S(1)} %get-tuple-element.316, s32[512]{0:T(512)S(1)} %get-tuple-element.317, ...), kind=kOutput, calls=%fused_computation.50.clone.1 | convolution fusion | flops 20148480 | bytes 52225 | tf_op jit(solution)/shard_map/while/body/eval_jaxpr/dot_general | solution.py:124
  41.4 1.5 %convolution_add_fusion.2 = f32[25,128]{1,0:T(8,128)S(1)} fusion(f32[512]{0:T(512)S(1)} %bitcast.144, s32[512]{0:T(512)S(1)} %get-tuple-element.311, f32[512]{0:T(512)S(1)} %get-tuple-element.314, s32[512]{0:T(512)S(1)} %bitcast.140, f32[512]{0:T(512)S(1)} %bitcast.154, f32[512]{0:T(512)S(1)} %get-tuple-element.316, s32[512]{0:T(512)S(1)} %get-tuple-element.317, ...), kind=kOutput, calls=%fused_computation.50.clone.1 | convolution fusion | flops 20148480 | bytes 52225 | tf_op jit(solution)/shard_map/while/body/eval_jaxpr/dot_general | solution.py:124
  43.0 1.5 %convolution_add_fusion.2 = f32[25,128]{1,0:T(8,128)S(1)} fusion(f32[512]{0:T(512)S(1)} %bitcast.144, s32[512]{0:T(512)S(1)} %get-tuple-element.311, f32[512]{0:T(512)S(1)} %get-tuple-element.314, s32[512]{0:T(512)S(1)} %bitcast.140, f32[512]{0:T(512)S(1)} %bitcast.154, f32[512]{0:T(512)S(1)} %get-tuple-element.316, s32[512]{0:T(512)S(1)} %get-tuple-element.317, ...), kind=kOutput, calls=%fused_computation.50.clone.1 | convolution fusion | flops 20148480 | bytes 52225 | tf_op jit(solution)/shard_map/while/body/eval_jaxpr/dot_general | solution.py:124
  44.6 1.5 %convolution_add_fusion.2 = f32[25,128]{1,0:T(8,128)S(1)} fusion(f32[512]{0:T(512)S(1)} %bitcast.144, s32[512]{0:T(512)S(1)} %get-tuple-element.311, f32[512]{0:T(512)S(1)} %get-tuple-element.314, s32[512]{0:T(512)S(1)} %bitcast.140, f32[512]{0:T(512)S(1)} %bitcast.154, f32[512]{0:T(512)S(1)} %get-tuple-element.316, s32[512]{0:T(512)S(1)} %get-tuple-element.317, ...), kind=kOutput, calls=%fused_computation.50.clone.1 | convolution fusion | flops 20148480 | bytes 52225 | tf_op jit(solution)/shard_map/while/body/eval_jaxpr/dot_general | solution.py:124
  46.3 1.5 %convolution_add_fusion.2 = f32[25,128]{1,0:T(8,128)S(1)} fusion(f32[512]{0:T(512)S(1)} %bitcast.144, s32[512]{0:T(512)S(1)} %get-tuple-element.311, f32[512]{0:T(512)S(1)} %get-tuple-element.314, s32[512]{0:T(512)S(1)} %bitcast.140, f32[512]{0:T(512)S(1)} %bitcast.154, f32[512]{0:T(512)S(1)} %get-tuple-element.316, s32[512]{0:T(512)S(1)} %get-tuple-element.317, ...), kind=kOutput, calls=%fused_computation.50.clone.1 | convolution fusion | flops 20148480 | bytes 52225 | tf_op jit(solution)/shard_map/while/body/eval_jaxpr/dot_general | solution.py:124
  47.9 1.5 %convolution_add_fusion.2 = f32[25,128]{1,0:T(8,128)S(1)} fusion(f32[512]{0:T(512)S(1)} %bitcast.144, s32[512]{0:T(512)S(1)} %get-tuple-element.311, f32[512]{0:T(512)S(1)} %get-tuple-element.314, s32[512]{0:T(512)S(1)} %bitcast.140, f32[512]{0:T(512)S(1)} %bitcast.154, f32[512]{0:T(512)S(1)} %get-tuple-element.316, s32[512]{0:T(512)S(1)} %get-tuple-element.317, ...), kind=kOutput, calls=%fused_computation.50.clone.1 | convolution fusion | flops 20148480 | bytes 52225 | tf_op jit(solution)/shard_map/while/body/eval_jaxpr/dot_general | solution.py:124
  49.6 1.5 %convolution_add_fusion.2 = f32[25,128]{1,0:T(8,128)S(1)} fusion(f32[512]{0:T(512)S(1)} %bitcast.144, s32[512]{0:T(512)S(1)} %get-tuple-element.311, f32[512]{0:T(512)S(1)} %get-tuple-element.314, s32[512]{0:T(512)S(1)} %bitcast.140, f32[512]{0:T(512)S(1)} %bitcast.154, f32[512]{0:T(512)S(1)} %get-tuple-element.316, s32[512]{0:T(512)S(1)} %get-tuple-element.317, ...), kind=kOutput, calls=%fused_computation.50.clone.1 | convolution fusion | flops 20148480 | bytes 52225 | tf_op jit(solution)/shard_map/while/body/eval_jaxpr/dot_general | solution.py:124
  51.2 1.5 %convolution_add_fusion.2 = f32[25,128]{1,0:T(8,128)S(1)} fusion(f32[512]{0:T(512)S(1)} %bitcast.144, s32[512]{0:T(512)S(1)} %get-tuple-element.311, f32[512]{0:T(512)S(1)} %get-tuple-element.314, s32[512]{0:T(512)S(1)} %bitcast.140, f32[512]{0:T(512)S(1)} %bitcast.154, f32[512]{0:T(512)S(1)} %get-tuple-element.316, s32[512]{0:T(512)S(1)} %get-tuple-element.317, ...), kind=kOutput, calls=%fused_computation.50.clone.1 | convolution fusion | flops 20148480 | bytes 52225 | tf_op jit(solution)/shard_map/while/body/eval_jaxpr/dot_general | solution.py:124
  52.8 1.5 %convolution_add_fusion.2 = f32[25,128]{1,0:T(8,128)S(1)} fusion(f32[512]{0:T(512)S(1)} %bitcast.144, s32[512]{0:T(512)S(1)} %get-tuple-element.311, f32[512]{0:T(512)S(1)} %get-tuple-element.314, s32[512]{0:T(512)S(1)} %bitcast.140, f32[512]{0:T(512)S(1)} %bitcast.154, f32[512]{0:T(512)S(1)} %get-tuple-element.316, s32[512]{0:T(512)S(1)} %get-tuple-element.317, ...), kind=kOutput, calls=%fused_computation.50.clone.1 | convolution fusion | flops 20148480 | bytes 52225 | tf_op jit(solution)/shard_map/while/body/eval_jaxpr/dot_general | solution.py:124
  54.5 1.5 %convolution_add_fusion.2 = f32[25,128]{1,0:T(8,128)S(1)} fusion(f32[512]{0:T(512)S(1)} %bitcast.144, s32[512]{0:T(512)S(1)} %get-tuple-element.311, f32[512]{0:T(512)S(1)} %get-tuple-element.314, s32[512]{0:T(512)S(1)} %bitcast.140, f32[512]{0:T(512)S(1)} %bitcast.154, f32[512]{0:T(512)S(1)} %get-tuple-element.316, s32[512]{0:T(512)S(1)} %get-tuple-element.317, ...), kind=kOutput, calls=%fused_computation.50.clone.1 | convolution fusion | flops 20148480 | bytes 52225 | tf_op jit(solution)/shard_map/while/body/eval_jaxpr/dot_general | solution.py:124
  56.7 6.0 %collective-permute-done = f32[5,128]{1,0:T(8,128)S(1)} collective-permute-done((f32[5,128]{1,0:T(8,128)S(1)}, f32[5,128]{1,0:T(8,128)S(1)}, u32[]{:S(2)}, u32[]{:S(2)}) %collective-permute-start) | collective-permute-done | bytes 2592 | tf_op jit(solution)/shard_map/ppermute | solution.py:10
  65.1 1.2 %collective-permute-done.3 = f32[5,128]{1,0:T(8,128)S(1)} collective-permute-done((f32[5,128]{1,0:T(8,128)S(1)}, f32[5,128]{1,0:T(8,128)S(1)}, u32[]{:S(2)}, u32[]{:S(2)}) %collective-permute-start.3) | collective-permute-done | bytes 2592 | tf_op jit(solution)/shard_map/ppermute | solution.py:10
  66.3 18.9 %while.27 = (s32[]{:T(128)}, f32[16,3,4,128]{3,2,1,0:T(4,128)S(1)}, f32[16,4,7,128]{3,2,1,0:T(8,128)S(1)}, f32[25,128]{1,0:T(8,128)S(1)}, s32[]{:T(128)}) while((s32[]{:T(128)}, f32[16,3,4,128]{3,2,1,0:T(4,128)S(1)}, f32[16,4,7,128]{3,2,1,0:T(8,128)S(1)}, f32[25,128]{1,0:T(8,128)S(1)}, s32[]{:T(128)}) %tuple.122), condition=%wide.region_10.11_spmd, body=%wide.region_6.10_spmd.sunk | while | flops 60314112 | bytes 2044485 | solution.py:167
  66.5 0.8 fusion.77
  67.7 0.8 fusion.77
  68.8 0.8 fusion.77
  70.0 0.8 fusion.77
  71.2 0.8 fusion.77
  72.4 0.8 fusion.77
  73.6 0.8 fusion.77
  74.7 0.8 fusion.77
  75.9 0.8 fusion.77
  77.1 0.8 fusion.77
  78.3 0.8 fusion.77
  79.5 0.8 fusion.77
  80.6 0.8 fusion.77
  81.8 0.8 fusion.77
  83.0 0.8 fusion.77
  84.2 0.8 fusion.77
  85.2 2.6 %slice_multiply_fusion.3 = f32[64,1,128]{2,0,1:T(8,128)S(1)} fusion(f32[64,3,128]{2,0,1:T(8,128)S(1)} %bitcast.121, f32[64,6,128]{2,0,1:T(8,128)S(1)} %bitcast.120, f32[]{:T(128)} %bitcast.34, f32[]{:T(128)} %bitcast.35, f32[]{:T(128)} %bitcast.37, f32[]{:T(128)} %bitcast.36), kind=kLoop, calls=%fused_computation.108 | loop fusion | flops 90112 | bytes 98320 | tf_op jit(solution)/shard_map/mul | solution.py:171
  87.9 0.7 copy.65
  88.5 5.8 %all-to-all-start.2 = ((f32[32,2,4,128]{3,1,2,0:T(2,128)}), f32[32,2,4,128]{3,1,2,0:T(2,128)S(1)}, u32[]{:S(2)}, u32[]{:S(2)}) async-start(f32[32,2,4,128]{3,1,2,0:T(2,128)} %copy.65), calls=%async_computation.2 | async-start | bytes 262144 | tf_op jit(solution)/shard_map/all_to_all | solution.py:175
  94.4 8.1 %all-to-all-done.2 = f32[32,2,4,128]{3,1,2,0:T(2,128)S(1)} async-done(((f32[32,2,4,128]{3,1,2,0:T(2,128)}), f32[32,2,4,128]{3,1,2,0:T(2,128)S(1)}, u32[]{:S(2)}, u32[]{:S(2)}) %all-to-all-start.2) | async-done | bytes 131104 | tf_op jit(solution)/shard_map/all_to_all | solution.py:175
  103.9 0.7 fusion.53
  (305 shorter events, 14.5 us)
Async XLA Ops:
  0.6 0.7 copy-start.7
  0.6 10.3 %copy-start.1 = (s32[3,4096]{1,0:T(4,128)S(1)}, s32[3,4096]{1,0:T(4,128)}, u32[]{:S(2)}) copy-start(s32[3,4096]{1,0:T(4,128)} %param.17) | copy-start | bytes 147460
  1.6 0.7 copy-start.6
  3.7 14.4 %all-to-all-start.1 = ((s32[32,1,2]{2,1,0:T(1,128)}), s32[32,1,2]{2,1,0:T(1,128)S(1)}, u32[]{:S(2)}, u32[]{:S(2)}) async-start(s32[32,1,2]{2,1,0:T(1,128)} %bitcast.21), calls=%async_computation.1 | async-start | bytes 32768 | tf_op jit(solution)/shard_map/all_to_all | solution.py:105
  11.0 0.7 copy-start.2
  11.0 0.8 copy-start
  18.0 11.5 %all-to-all-start = ((f32[32,2,6,128]{3,1,2,0:T(2,128)}), f32[32,2,6,128]{3,1,2,0:T(2,128)S(1)}, u32[]{:S(2)}, u32[]{:S(2)}) async-start(f32[32,2,6,128]{3,1,2,0:T(2,128)} %copy.52), calls=%async_computation | async-start | bytes 393216 | tf_op jit(solution)/shard_map/all_to_all | solution.py:104
  56.0 6.7 %collective-permute-start = (f32[5,128]{1,0:T(8,128)S(1)}, f32[5,128]{1,0:T(8,128)S(1)}, u32[]{:S(2)}, u32[]{:S(2)}) collective-permute-start(f32[5,128]{1,0:T(8,128)S(1)} %slice.212), channel_id=1, source_target_pairs={{31,0},{0,1},{1,2},{2,3},{3,4},{4,5},{5,6},{6,7},{7,8},{8,9},{9,10... | collective-permute-start | bytes 7688 | tf_op jit(solution)/shard_map/ppermute | solution.py:10
  62.8 0.7 copy-start.5
  62.8 0.7 copy-start.4
  62.8 0.7 copy-start.8
  63.6 0.7 copy-start.3
  63.6 1.3 %collective-permute-start.2 = (f32[4,128]{1,0:T(4,128)S(1)}, f32[4,128]{1,0:T(4,128)S(1)}, u32[]{:S(2)}, u32[]{:S(2)}) collective-permute-start(f32[4,128]{1,0:T(4,128)S(1)} %bitcast.160), channel_id=1, source_target_pairs={{0,0},{1,1},{2,2},{3,3},{4,4},{5,5},{6,6},{7,7},{8,8},{9,9},{10,10... | collective-permute-start | bytes 6152 | tf_op jit(solution)/shard_map/ppermute | solution.py:10
  64.9 1.4 %collective-permute-start.3 = (f32[5,128]{1,0:T(8,128)S(1)}, f32[5,128]{1,0:T(8,128)S(1)}, u32[]{:S(2)}, u32[]{:S(2)}) collective-permute-start(f32[5,128]{1,0:T(8,128)S(1)} %fusion.55), channel_id=1, source_target_pairs={{1,0},{2,1},{3,2},{4,3},{5,4},{6,5},{7,6},{8,7},{9,8},{10,9},{11,1... | collective-permute-start | bytes 7688 | tf_op jit(solution)/shard_map/ppermute | solution.py:10
  88.5 14.0 %all-to-all-start.2 = ((f32[32,2,4,128]{3,1,2,0:T(2,128)}), f32[32,2,4,128]{3,1,2,0:T(2,128)S(1)}, u32[]{:S(2)}, u32[]{:S(2)}) async-start(f32[32,2,4,128]{3,1,2,0:T(2,128)} %copy.65), calls=%async_computation.2 | async-start | bytes 262144 | tf_op jit(solution)/shard_map/all_to_all | solution.py:175
  (1 other events, 0.0 us)
where the time goes:
time: 105 us
  matrix products  37.5 us (36%)
  waiting for transfers between devices  26.7 us (25%)
  starting transfers between devices  16.4 us (16%)
  other arithmetic  10.5 us (10%)
  local copies, waits for them, and re-layouts  10.2 us (10%)
  loops' own time  2.34 us (2%)
    dot_general x16, matrix products, deposit(): lax.dot_general(plane_val * live_here[:, None], deep_val, (((0,), (0,)),...  24.5 us
    dot_general x16, matrix products, pull(): jnp.dot(stacked, field_plane, precision=lax.Precision.HIGHEST, preferred_...  13 us
    all_to_all x1, waiting for transfers between devices, on_device(): lax.all_to_all(returned, 'los', split_axis=0, concat_axis=0, tiled=True)  8.14 us
    all_to_all x1, waiting for transfers between devices, on_device(): lax.all_to_all(outgoing, 'los', split_axis=0, concat_axis=0, tiled=True)  7.49 us
    all_to_all x1, starting transfers between devices, on_device(): lax.all_to_all(out_counts, 'los', split_axis=0, concat_axis=0, tiled=True)  7.3 us
    ppermute x4, waiting for transfers between devices, passed_along(): return lax.ppermute(block, axis, route)  7.24 us
    all_to_all x1, starting transfers between devices, on_device(): lax.all_to_all(returned, 'los', split_axis=0, concat_axis=0, tiled=True)  5.81 us
    all_to_all x1, waiting for transfers between devices, on_device(): lax.all_to_all(out_counts, 'los', split_axis=0, concat_axis=0, tiled=True)  3.84 us
  transfers between devices with their start and end apart: 7, of which 5 were waited for; matrix products, arithmetic and copies ran while one was open for 4% of the time, Pallas kernels for 0%

commit v1 on v0

v1 whole, which is shorter than its diff:
```python
import functools

import jax
import jax.numpy as jnp
from jax import lax
from jax.experimental import pallas as pl
from jax.experimental.pallas import tpu as pltpu
from jax.sharding import PartitionSpec as P

SUB = 8


def passed_along(block, axis, distance):
    devices = range(lax.axis_size(axis))
    route = [((i - distance) % len(devices), i) for i in devices]
    return lax.ppermute(block, axis, route)


def exchanged(chunks):
    return lax.all_to_all(chunks, "los", split_axis=0, concat_axis=0, tiled=True)


def rounded_up(value, step):
    return -(-value // step) * step


def row_iotas(cols):
    sub = lax.broadcasted_iota(jnp.int32, (SUB, 128), 0)
    return sub // cols, sub % cols


def block_rows(ref, row, k, lanes):
    return jnp.broadcast_to(ref[row : row + 1, k * lanes : (k + 1) * lanes], (SUB, lanes))


def paint_kernel(
    g, dest_ref, count_ref, cell_ref, frac_ref, offset_ref, out_ref, low_ref, high_ref
):
    low_ref[...] = jnp.zeros_like(low_ref)
    high_ref[...] = jnp.zeros_like(high_ref)
    plane_iota, sky_iota = row_iotas(g.cols)
    deep_iota = lax.broadcasted_iota(jnp.int32, (g.deep, g.block), 0)
    lane = lax.broadcasted_iota(jnp.int32, (SUB, g.block), 1)
    for k in range(g.blocks):
        offset = jnp.broadcast_to(offset_ref[k : k + 1, :], (SUB, g.block))
        red = jnp.mod(block_rows(cell_ref, 0, k, g.block) + offset, g.slab_rows)
        sky = block_rows(cell_ref, 1, k, g.block)
        sky_next = jnp.where(sky + 1 == g.sky_wrap, 0, sky + 1)
        frac_los = block_rows(frac_ref, 0, k, g.block)
        frac_sky = block_rows(frac_ref, 1, k, g.block)
        frac_deep = block_rows(frac_ref, 2, k, g.block)
        live = lane < count_ref[k]
        on_sky = jnp.where(
            sky_iota == sky, 1.0 - frac_sky, jnp.where(sky_iota == sky_next, frac_sky, 0.0)
        )
        on_sky = jnp.where(live, on_sky, 0.0)
        rows = []
        for i in range(g.window // SUB):
            plane = plane_iota + i * g.planes_per_tile - red
            on_los = jnp.where(
                plane == 0, 1.0 - frac_los, jnp.where(plane == 1, frac_los, 0.0)
            )
            rows.append(on_los * on_sky)
        weight = jnp.concatenate(rows, axis=0)
        upper = weight * jnp.concatenate([frac_deep] * (g.window // SUB), axis=0)
        weight = jnp.concatenate([weight - upper, upper], axis=0)
        coarse = weight.astype(jnp.bfloat16)
        fine = (weight - coarse.astype(jnp.float32)).astype(jnp.bfloat16)
        deep = jnp.broadcast_to(cell_ref[2:3, k * g.block : (k + 1) * g.block], (g.deep, g.block))
        hit = jnp.where(deep_iota == deep, 1.0, 0.0).astype(jnp.bfloat16)
        got = lax.dot_general(
            jnp.concatenate([coarse, fine], axis=0),
            hit,
            (((1,), (1,)), ((), ())),
            preferred_element_type=jnp.float32,
        )
        got = got[: 2 * g.window] + got[2 * g.window :]
        at = pl.ds(pl.multiple_of(dest_ref[k] * g.slab, SUB), g.window)
        low_ref[at, :] += got[: g.window]
        high_ref[at, :] += got[g.window :]
    total = low_ref[...] + pltpu.roll(high_ref[...], 1, 1)
    size = g.slabs * g.slab
    spill = g.window - g.slab
    out_ref[spill:, :] = total[spill:size]
    out_ref[:spill, :] = total[:spill] + total[size:]


def cotangent_of(density, selection, counts, exponent):
    shifted = density + 0.5
    intensity = selection * jnp.exp(exponent * jnp.log(shifted))
    return (1.0 - counts.astype(jnp.float32) / intensity) * exponent * intensity / shifted


def field_kernel(g, recv_ref, selection_ref, counts_ref, bias_ref, rate_ref, out_ref):
    density = recv_ref[0]
    for i in range(1, g.slabs):
        density = density + recv_ref[i]
    plane = lax.broadcasted_iota(jnp.int32, (g.slab, g.deep), 0) // g.cols
    lane = lax.broadcasted_iota(jnp.int32, (1, g.deep), 1)
    exponent = jnp.zeros((g.slab, g.deep), jnp.float32)
    rate = jnp.zeros((1, g.deep), jnp.float32)
    for j in range(g.slab_rows):
        exponent = jnp.where(plane == j, bias_ref[j], exponent)
        rate = jnp.where(lane == j, rate_ref[j], rate)
    field = cotangent_of(density, selection_ref[...], counts_ref[...], exponent)
    sent = jnp.concatenate([field, rate], axis=0)
    for i in range(g.slabs):
        out_ref[i * (g.slab + 1) : (i + 1) * (g.slab + 1), :] = sent


def picked(rows, index):
    return jnp.take_along_axis(rows, index, axis=1, mode="promise_in_bounds")


def pull_kernel(
    g, dest_ref, count_ref, cell_ref, frac_ref, offset_ref, field_ref, pos_ref, vel_ref, whole_ref, rate_ref
):
    for i in range(g.slabs):
        start = i * (g.slab + 1)
        whole_ref[i * g.slab : (i + 1) * g.slab, :] = field_ref[start : start + g.slab, :]
        rate_ref[i : i + 1, :] = field_ref[start + g.slab : start + g.slab + 1, :]
    spill = g.window - g.slab
    whole_ref[g.slabs * g.slab :, :] = field_ref[:spill, :]
    plane_iota, sky_iota = row_iotas(g.cols)
    lane = lax.broadcasted_iota(jnp.int32, (1, g.block), 1)
    for k in range(g.blocks):
        slab = dest_ref[k]
        offset = jnp.broadcast_to(offset_ref[k : k + 1, :], (SUB, g.block))
        red = jnp.mod(block_rows(cell_ref, 0, k, g.block) + offset, g.slab_rows)
        sky = block_rows(cell_ref, 1, k, g.block)
        sky_next = jnp.where(sky + 1 == g.sky_wrap, 0, sky + 1)
        deep = block_rows(cell_ref, 2, k, g.block)
        deep_next = jnp.where(deep + 1 == g.deep, 0, deep + 1)
        frac_los = block_rows(frac_ref, 0, k, g.block)
        frac_sky = block_rows(frac_ref, 1, k, g.block)
        frac_deep = block_rows(frac_ref, 2, k, g.block)
        at_sky, at_next = sky_iota == sky, sky_iota == sky_next
        on_sky = jnp.where(at_sky, 1.0 - frac_sky, jnp.where(at_next, frac_sky, 0.0))
        slope_sky = jnp.where(at_next, 1.0, 0.0) - jnp.where(at_sky, 1.0, 0.0)
        sum_val, sum_los, sum_deep = 0.0, 0.0, 0.0
        for i in range(g.window // SUB):
            at = pl.ds(pl.multiple_of(slab * g.slab, SUB) + i * SUB, SUB)
            rows = whole_ref[at, :]
            below = picked(rows, deep)
            step = picked(rows, deep_next) - below
            value = below + frac_deep * step
            plane = plane_iota + i * g.planes_per_tile - red
            at_plane, at_above = plane == 0, plane == 1
            on_los = jnp.where(at_plane, 1.0 - frac_los, jnp.where(at_above, frac_los, 0.0))
            sum_val += on_los * value
            sum_deep += on_los * step
            sum_los += jnp.where(at_above, value, jnp.where(at_plane, -value, 0.0))
        live = lane < count_ref[k]
        lanes = slice(k * g.block, (k + 1) * g.block)
        rate = picked(jnp.broadcast_to(rate_ref[pl.ds(slab, 1), :], (SUB, g.deep)), red)
        grad_los = jnp.where(live, jnp.sum(on_sky * sum_los, axis=0, keepdims=True), 0.0)
        grad_sky = jnp.where(live, jnp.sum(slope_sky * sum_val, axis=0, keepdims=True), 0.0)
        grad_deep = jnp.where(live, jnp.sum(on_sky * sum_deep, axis=0, keepdims=True), 0.0)
        pos_ref[0:1, lanes] = grad_los
        pos_ref[1:2, lanes] = grad_sky
        pos_ref[2:3, lanes] = grad_deep
        vel_ref[k : k + 1, :] = rate[0:1] * grad_los


class Geometry:
    def __init__(self, slabs, sky_parts, cell_shape, block_shape, field_shape):
        self.slabs = slabs
        self.blocks = block_shape[0]
        self.block = cell_shape[1] // self.blocks
        self.slab_rows, self.width, self.deep = field_shape
        self.sky_wrap = self.width if sky_parts == 1 else -1
        need = self.width + (sky_parts > 1)
        self.cols = next(c for c in (1, 2, 4, 8) if c >= need and c * self.slab_rows % SUB == 0)
        self.planes_per_tile = SUB // self.cols
        self.slab = self.slab_rows * self.cols
        self.window = rounded_up(self.slab + self.cols, SUB)


def on_device(
    part_cell,
    part_frac,
    los_offset,
    block_dest,
    block_count,
    selection,
    galaxy_counts,
    bias_exp,
    rsd_factor,
):
    sky_parts = lax.axis_size("sky")
    g = Geometry(
        lax.axis_size("los"), sky_parts, part_cell.shape, block_dest.shape, selection.shape
    )
    f32 = jnp.float32
    smem = pl.BlockSpec(memory_space=pltpu.SMEM)
    vmem = pl.BlockSpec(memory_space=pltpu.VMEM)
    if sky_parts > 1:
        shift = jnp.stack([0, lax.axis_index("sky") * g.width, 0]).astype(jnp.int32)
        part_cell = part_cell - shift[:, None]
    offsets = los_offset.reshape(g.blocks, g.block)
    size = g.slabs * g.slab
    padded = size + g.window - g.slab
    painted = pl.pallas_call(
        functools.partial(paint_kernel, g),
        out_shape=jax.ShapeDtypeStruct((size, g.deep), f32),
        in_specs=[smem, smem, vmem, vmem, vmem],
        out_specs=vmem,
        scratch_shapes=[pltpu.VMEM((padded, g.deep), f32), pltpu.VMEM((padded, g.deep), f32)],
        name="paint",
    )(block_dest, block_count, part_cell, part_frac, offsets)
    recv = exchanged(painted.reshape(g.slabs, g.slab, g.deep))
    tall = g.slabs * (g.slab + 1)
    if sky_parts == 1:
        sent = pl.pallas_call(
            functools.partial(field_kernel, g),
            out_shape=jax.ShapeDtypeStruct((tall, g.deep), f32),
            in_specs=[vmem, vmem, vmem, smem, smem],
            out_specs=vmem,
            name="field",
        )(
            recv,
            selection.reshape(g.slab, g.deep),
            galaxy_counts.reshape(g.slab, g.deep),
            bias_exp,
            rsd_factor,
        )
    else:
        core = jnp.sum(recv, axis=0).reshape(g.slab_rows, g.cols, g.deep)
        density = core[:, : g.width].at[:, 0].add(passed_along(core[:, g.width], "sky", 1))
        field = cotangent_of(density, selection, galaxy_counts, bias_exp[:, None, None])
        rim = passed_along(field[:, 0], "sky", -1)
        rest = jnp.zeros((g.slab_rows, g.cols - g.width - 1, g.deep), f32)
        field = jnp.concatenate([field, rim[:, None], rest], axis=1).reshape(g.slab, g.deep)
        rate = jnp.pad(rsd_factor, (0, g.deep - g.slab_rows))[None]
        sent = jnp.concatenate([field, rate], axis=0)
        sent = jnp.broadcast_to(sent[None], (g.slabs, g.slab + 1, g.deep)).reshape(tall, g.deep)
    whole = exchanged(sent.reshape(g.slabs, 1, (g.slab + 1) * g.deep)).reshape(tall, g.deep)
    grad_pos, grad_vel = pl.pallas_call(
        functools.partial(pull_kernel, g),
        out_shape=(
            jax.ShapeDtypeStruct(part_frac.shape, f32),
            jax.ShapeDtypeStruct((g.blocks, g.block), f32),
        ),
        in_specs=[smem, smem, vmem, vmem, vmem, vmem],
        out_specs=(vmem, vmem),
        scratch_shapes=[pltpu.VMEM((padded, g.deep), f32), pltpu.VMEM((g.slabs, g.deep), f32)],
        name="pull",
    )(block_dest, block_count, part_cell, part_frac, offsets, whole)
    return grad_pos, grad_vel.reshape(-1)


def solution(mesh):
    return jax.shard_map(
        on_device,
        mesh=mesh,
        in_specs=(
            P(None, ("los", "sky")),
            P(None, ("los", "sky")),
            P(("los", "sky")),
            P(("los", "sky")),
            P(("los", "sky")),
            P("los", "sky", None),
            P("los", "sky", None),
            P("los"),
            P("los"),
        ),
        out_specs=(P(None, ("los", "sky")), P(("los", "sky"))),
        check_vma=False,
    )
```

time: 105 us -> 40.1 us (0.38)
  matrix products: 37.5 us -> 0 us
  blocking collectives: 0 us -> 32.4 us
  waiting for transfers between devices: 26.7 us -> 0 us
  starting transfers between devices: 16.4 us -> 0 us
  other arithmetic: 10.5 us -> 0 us
  local copies, waits for them, and re-layouts: 10.2 us -> 0 us
  Pallas kernels: 0 us -> 6.68 us
  loops' own time: 2.34 us -> 0 us
    dot_general x32 -> x0, matrix products: 37.5 us -> none  [the longest x16 24.5 us: deposit(): lax.dot_general(plane_val * live_here[:, None], deep_val, (((0,), (0,)),...]
    all_to_all x0 -> x2, blocking collectives: none -> 32.4 us  [exchanged(): lax.all_to_all(chunks, 'los', split_axis=0, concat_axis=0, tiled=True)]
    all_to_all x3 -> x0, waiting for transfers between devices: 19.5 us -> none  [the longest x1 8.14 us: on_device(): lax.all_to_all(returned, 'los', split_axis=0, concat_axis=0, tiled=True)]
    all_to_all x3 -> x0, starting transfers between devices: 15.7 us -> none  [the longest x1 7.3 us: on_device(): lax.all_to_all(out_counts, 'los', split_axis=0, concat_axis=0, tiled=True)]
    ppermute x4 -> x0, waiting for transfers between devices: 7.24 us -> none  [passed_along(): return lax.ppermute(block, axis, route)]
    pallas_call x0 -> x3, Pallas kernels: none -> 6.68 us  [the longest x1 2.58 us: on_device(): pl.pallas_call(functools.partial(paint_kernel, g), out_shape=jax.ShapeDty...]
    mul x36 -> x0, other arithmetic: 4.19 us -> none  [the longest x1 2.55 us: on_device(): rate_each * pulled[:, 0]]
    unnamed x18 -> x0, local copies, waits for them, and re-layouts: 3.35 us -> none
  transfers between devices with their start and end apart: 7 -> 0, of which waited for: 5 -> 0; matrix products, arithmetic and copies ran while one was open for 4% -> 0% of each run, Pallas kernels for 0% -> 0%
where the time goes in v1:
time: 40.1 us; the launch traced here: 39.7 us
  blocking collectives  32.4 us (81%)
  Pallas kernels  6.68 us (17%)
  between operations  0.63 us (2%)
    all_to_all x2, blocking collectives, exchanged(): lax.all_to_all(chunks, 'los', split_axis=0, concat_axis=0, tiled=True)  32.4 us
    pallas_call x1, Pallas kernels, on_device(): pl.pallas_call(functools.partial(paint_kernel, g), out_shape=jax.ShapeDty...  2.58 us
    pallas_call x1, Pallas kernels, on_device(): pl.pallas_call(functools.partial(pull_kernel, g), out_shape=(jax.ShapeDty...  2.33 us
    pallas_call x1, Pallas kernels, on_device(): pl.pallas_call(functools.partial(field_kernel, g), out_shape=jax.ShapeDty...  1.76 us

profile of v1, /device:TPU:0, one launch (start us, length us, event | category | flops | bytes accessed | tf_op | source)
XLA Modules:
  0.0 39.7 jit_solution(6229795417171348453)
XLA Ops:
  0.6 2.6 %paint.1 = f32[512,128]{1,0:T(8,128)} custom-call(s32[32]{0:T(128)} %dest_ref.3, s32[32]{0:T(128)} %count_ref.3, s32[3,4096]{1,0:T(4,128)} %cell_ref.3, f32[3,4096]{1,0:T(4,128)} %frac_ref.3, s32[32,128]{1,0:T(8,128)} %bitcast.10), custom_call_target="tpu_custom_call" | custom-call | tf_op jit(solution)/shard_map/paint/pallas_call | solution.py:203
  3.2 18.0 %all_to_all.10.recv_ref = f32[32,16,128]{2,1,0:T(8,128)} all-to-all(f32[32,16,128]{2,1,0:T(8,128)} %bitcast.9), channel_id=1, replica_groups=mesh['los'=32,'sky'=1] {'los'}, dimensions={0} | all-to-all | bytes 524288 | tf_op jit(solution)/shard_map/all_to_all | solution.py:20
  21.2 1.8 %field.1 = f32[544,128]{1,0:T(8,128)} custom-call(f32[32,16,128]{2,1,0:T(8,128)} %all_to_all.10.recv_ref, f32[16,128]{1,0:T(8,128)} %bitcast.12, s32[16,128]{1,0:T(8,128)} %bitcast.13, f32[4]{0:T(128)} %bias_ref.1, f32[4]{0:T(128)} %rate_ref.1), custom_call_target="tpu_custom_call" | custom-call | tf_op jit(solution)/shard_map/field/pallas_call | solution.py:214
  23.0 14.4 %all_to_all.11 = f32[32,1,2176]{2,1,0:T(1,128)} all-to-all(f32[32,1,2176]{2,1,0:T(1,128)} %bitcast.7), channel_id=1, replica_groups=mesh['los'=32,'sky'=1] {'los'}, dimensions={0} | all-to-all | bytes 557056 | tf_op jit(solution)/shard_map/all_to_all | solution.py:20
  37.4 2.3 %pull.1 = (f32[3,4096]{1,0:T(4,128)}, f32[32,128]{1,0:T(8,128)}) custom-call(s32[32]{0:T(128)} %dest_ref.3, s32[32]{0:T(128)} %count_ref.3, s32[3,4096]{1,0:T(4,128)} %cell_ref.3, f32[3,4096]{1,0:T(4,128)} %frac_ref.3, s32[32,128]{1,0:T(8,128)} %bitcast.11, f32[544,128]{1,0:T(8,128)} %bitcast.8), custom_call_target="tpu_custom_call" | custom-call | tf_op jit(solution)/shard_map/pull/pallas_call | solution.py:238

commit v2 on v1

v2 whole, which is shorter than its diff:
```python
import functools

import jax
import jax.numpy as jnp
from jax import lax
from jax.experimental import pallas as pl
from jax.experimental.pallas import tpu as pltpu
from jax.sharding import PartitionSpec as P

SUB = 8
VMEM_LIMIT = 8 * 1024 * 1024


def passed_along(block, axis, distance):
    devices = range(lax.axis_size(axis))
    route = [((i - distance) % len(devices), i) for i in devices]
    return lax.ppermute(block, axis, route)


def rounded_up(value, step):
    return -(-value // step) * step


def row_iotas(cols):
    sub = lax.broadcasted_iota(jnp.int32, (SUB, 128), 0)
    return sub // cols, sub % cols


def block_rows(ref, row, k, lanes):
    return jnp.broadcast_to(ref[row : row + 1, k * lanes : (k + 1) * lanes], (SUB, lanes))


def slab_at(g, me, near, far):
    return far * g.plane + ((me % g.plane) ^ near)


def write_table(g, refs, table_ref):
    selection_ref, counts_ref, bias_ref, rate_ref = refs
    lane = lax.broadcasted_iota(jnp.int32, (SUB, g.deep), 1)
    rate = jnp.zeros((SUB, g.deep), jnp.float32)
    table_ref[...] = jnp.zeros_like(table_ref)
    for j in range(g.slab_rows):
        rate = jnp.where(lane == j, rate_ref[j], rate)
        start = j * g.cols
        table_ref[start : start + g.width, :] = selection_ref[j]
        table_ref[g.slab + start : g.slab + start + g.width, :] = counts_ref[j].astype(jnp.float32)
        table_ref[2 * g.slab + start : 2 * g.slab + start + g.cols, :] = jnp.full(
            (g.cols, g.deep), bias_ref[j], jnp.float32
        )
    table_ref[3 * g.slab :, :] = rate


def fetch_kernel(g, *refs):
    far_refs, (place_ref, frac_ref, dest_ref, table_ref), near_refs = refs[:9], refs[9:13], refs[13:]
    arrived = near_refs[-1]
    near_refs = (*near_refs[:3], frac_ref, *near_refs[3:-1])
    copies = [
        pltpu.make_async_copy(a, b, arrived.at[i])
        for i, (a, b) in enumerate(zip(far_refs, near_refs, strict=True))
    ]
    for copy in copies:
        copy.start()
    for copy in copies:
        copy.wait()
    blocks_ref, count_ref, cell_ref, frac_ref, offset_ref = near_refs[:5]
    write_table(g, near_refs[5:], table_ref)
    lane = lax.broadcasted_iota(jnp.int32, (1, g.block), 1)
    for k in range(g.blocks):
        lanes = slice(k * g.block, (k + 1) * g.block)
        red = jnp.mod(cell_ref[0:1, lanes] + offset_ref[k : k + 1, :], g.slab_rows)
        deep = jnp.where(lane < count_ref[k], cell_ref[2:3, lanes], -1)
        place_ref[:, lanes] = jnp.concatenate([red, cell_ref[1:2, lanes], deep], axis=0)
        dest_ref[k : k + 1, :] = jnp.full((1, g.deep), blocks_ref[k], jnp.int32)


def dest_of(dest_ref, k):
    return dest_ref[k : k + 1, 0:1][0, 0]


def paint_kernel(g, place_ref, frac_ref, dest_ref, keep_ref, send_ref, low_ref, high_ref):
    low_ref[...] = jnp.zeros_like(low_ref)
    high_ref[...] = jnp.zeros_like(high_ref)
    plane_iota, sky_iota = row_iotas(g.cols)
    deep_iota = lax.broadcasted_iota(jnp.int32, (g.deep, g.block), 0)
    for k in range(g.blocks):
        red = block_rows(place_ref, 0, k, g.block)
        sky = block_rows(place_ref, 1, k, g.block)
        sky_next = jnp.where(sky + 1 == g.sky_wrap, 0, sky + 1)
        frac_los = block_rows(frac_ref, 0, k, g.block)
        frac_sky = block_rows(frac_ref, 1, k, g.block)
        frac_deep = block_rows(frac_ref, 2, k, g.block)
        on_sky = jnp.where(
            sky_iota == sky, 1.0 - frac_sky, jnp.where(sky_iota == sky_next, frac_sky, 0.0)
        )
        rows = []
        for i in range(g.window // SUB):
            plane = plane_iota + i * g.planes_per_tile - red
            on_los = jnp.where(
                plane == 0, 1.0 - frac_los, jnp.where(plane == 1, frac_los, 0.0)
            )
            rows.append(on_los * on_sky)
        weight = jnp.concatenate(rows, axis=0)
        upper = weight * jnp.concatenate([frac_deep] * (g.window // SUB), axis=0)
        weight = jnp.concatenate([weight - upper, upper], axis=0)
        coarse = weight.astype(jnp.bfloat16)
        fine = (weight - coarse.astype(jnp.float32)).astype(jnp.bfloat16)
        deep = jnp.broadcast_to(place_ref[2:3, k * g.block : (k + 1) * g.block], (g.deep, g.block))
        hit = jnp.where(deep_iota == deep, 1.0, 0.0).astype(jnp.bfloat16)
        got = lax.dot_general(
            jnp.concatenate([coarse, fine], axis=0),
            hit,
            (((1,), (1,)), ((), ())),
            preferred_element_type=jnp.float32,
        )
        got = got[: 2 * g.window] + got[2 * g.window :]
        at = pl.ds(pl.multiple_of(dest_of(dest_ref, k) * g.slab, SUB), g.window)
        low_ref[at, :] += got[: g.window]
        high_ref[at, :] += got[g.window :]
    size = g.slabs * g.slab
    spill = g.window - g.slab
    low_ref[:spill, :] += low_ref[size:, :]
    high_ref[:spill, :] += high_ref[size:, :]
    me = lax.axis_index("los")
    for near in range(g.plane):
        for far in range(g.planes):
            at = pl.ds(pl.multiple_of(slab_at(g, me, near, far) * g.slab, SUB), g.slab)
            start = (near // 2) * g.column + far * g.slab
            rows = low_ref[at, :] + pltpu.roll(high_ref[at, :], 1, 1)
            (send_ref if near % 2 else keep_ref)[start : start + g.slab, :] = rows


def cotangent_of(density, selection, counts, exponent):
    shifted = density + 0.5
    intensity = selection * jnp.exp(exponent * jnp.log(shifted))
    return (1.0 - counts.astype(jnp.float32) / intensity) * exponent * intensity / shifted


def field_kernel(g, *refs):
    part_refs, table_refs, out_ref, sum_ref = refs[: g.planes], refs[g.planes : 2 * g.planes], refs[-2], refs[-1]
    total = part_refs[0][...]
    for ref in part_refs[1:]:
        total = total + ref[...]
    sum_ref[...] = total
    far = lax.axis_index("los") // g.plane
    out_ref[g.column :, :] = jnp.zeros((SUB, g.deep), jnp.float32)
    for m, ref in enumerate(table_refs):
        there = lax.rem(far + m, g.planes)
        at = pl.ds(pl.multiple_of(there * g.slab, SUB), g.slab)
        out_ref[at, :] = cotangent_of(
            sum_ref[at, :], ref[: g.slab, :], ref[g.slab : 2 * g.slab, :], ref[2 * g.slab : 3 * g.slab, :]
        )
        out_ref[pl.ds(g.column + there, 1), :] = ref[3 * g.slab : 3 * g.slab + 1, :]


def picked(rows, index):
    return jnp.take_along_axis(rows, index, axis=1, mode="promise_in_bounds")


def pull_kernel(g, place_ref, frac_ref, dest_ref, *refs):
    field_refs, (pos_ref, vel_ref, whole_ref, rate_ref) = refs[:-4], refs[-4:]
    me = lax.axis_index("los")
    tall = g.column + SUB
    for near in range(g.plane):
        ref, base = field_refs[near // 2], (near % 2) * tall
        for far in range(g.planes):
            slab = slab_at(g, me, near, far)
            at = pl.ds(pl.multiple_of(slab * g.slab, SUB), g.slab)
            start = base + far * g.slab
            whole_ref[at, :] = ref[start : start + g.slab, :]
            start = base + g.column + far
            rate_ref[pl.ds(slab, 1), :] = ref[start : start + 1, :]
    spill = g.window - g.slab
    whole_ref[g.slabs * g.slab :, :] = whole_ref[:spill, :]
    plane_iota, sky_iota = row_iotas(g.cols)
    for k in range(g.blocks):
        slab = dest_of(dest_ref, k)
        red = block_rows(place_ref, 0, k, g.block)
        sky = block_rows(place_ref, 1, k, g.block)
        sky_next = jnp.where(sky + 1 == g.sky_wrap, 0, sky + 1)
        deep = block_rows(place_ref, 2, k, g.block)
        live = deep[0:1] >= 0
        deep = jnp.maximum(deep, 0)
        deep_next = jnp.where(deep + 1 == g.deep, 0, deep + 1)
        frac_los = block_rows(frac_ref, 0, k, g.block)
        frac_sky = block_rows(frac_ref, 1, k, g.block)
        frac_deep = block_rows(frac_ref, 2, k, g.block)
        at_sky, at_next = sky_iota == sky, sky_iota == sky_next
        on_sky = jnp.where(at_sky, 1.0 - frac_sky, jnp.where(at_next, frac_sky, 0.0))
        slope_sky = jnp.where(at_next, 1.0, 0.0) - jnp.where(at_sky, 1.0, 0.0)
        sum_val, sum_los, sum_deep = 0.0, 0.0, 0.0
        for i in range(g.window // SUB):
            at = pl.ds(pl.multiple_of(slab * g.slab, SUB) + i * SUB, SUB)
            rows = whole_ref[at, :]
            below = picked(rows, deep)
            step = picked(rows, deep_next) - below
            value = below + frac_deep * step
            plane = plane_iota + i * g.planes_per_tile - red
            at_plane, at_above = plane == 0, plane == 1
            on_los = jnp.where(at_plane, 1.0 - frac_los, jnp.where(at_above, frac_los, 0.0))
            sum_val += on_los * value
            sum_deep += on_los * step
            sum_los += jnp.where(at_above, value, jnp.where(at_plane, -value, 0.0))
        lanes = slice(k * g.block, (k + 1) * g.block)
        rate = picked(jnp.broadcast_to(rate_ref[pl.ds(slab, 1), :], (SUB, g.deep)), red)
        grad_los = jnp.where(live, jnp.sum(on_sky * sum_los, axis=0, keepdims=True), 0.0)
        grad_sky = jnp.where(live, jnp.sum(slope_sky * sum_val, axis=0, keepdims=True), 0.0)
        grad_deep = jnp.where(live, jnp.sum(on_sky * sum_deep, axis=0, keepdims=True), 0.0)
        pos_ref[0:1, lanes] = grad_los
        pos_ref[1:2, lanes] = grad_sky
        pos_ref[2:3, lanes] = grad_deep
        vel_ref[k : k + 1, :] = rate[0:1] * grad_los


class Geometry:
    def __init__(self, slabs, sky_parts, cell_shape, block_shape, field_shape):
        self.slabs = slabs
        self.blocks = block_shape[0]
        self.block = cell_shape[1] // self.blocks
        self.slab_rows, self.width, self.deep = field_shape
        self.sky_wrap = self.width if sky_parts == 1 else -1
        need = self.width + (sky_parts > 1)
        self.cols = next(c for c in (1, 2, 4, 8) if c >= need and c * self.slab_rows % SUB == 0)
        self.planes_per_tile = SUB // self.cols
        self.slab = self.slab_rows * self.cols
        self.plane = 8
        self.planes = slabs // self.plane
        self.column = self.planes * self.slab
        self.window = rounded_up(self.slab + self.cols, SUB)


def on_device(
    part_cell,
    part_frac,
    los_offset,
    block_dest,
    block_count,
    selection,
    galaxy_counts,
    bias_exp,
    rsd_factor,
):
    sky_parts = lax.axis_size("sky")
    g = Geometry(
        lax.axis_size("los"), sky_parts, part_cell.shape, block_dest.shape, selection.shape
    )
    f32 = jnp.float32
    vmem = pl.BlockSpec(memory_space=pltpu.VMEM)
    if sky_parts > 1:
        shift = jnp.stack([0, lax.axis_index("sky") * g.width, 0]).astype(jnp.int32)
        part_cell = part_cell - shift[:, None]
    offsets = los_offset.reshape(g.blocks, g.block)
    size = g.slabs * g.slab
    padded = size + g.window - g.slab
    small = pltpu.CompilerParams(vmem_limit_bytes=VMEM_LIMIT)

    def tiled(rows):
        return jax.ShapeDtypeStruct((rows, g.deep), f32)

    def to_near(block, near):
        return lax.ppermute(block, "los", [(i ^ near, i) for i in range(g.slabs)])

    def from_far(block, m):
        return passed_along(block, "los", -m * g.plane)

    given = (
        block_dest,
        block_count,
        part_cell,
        part_frac,
        offsets,
        selection,
        galaxy_counts,
        bias_exp,
        rsd_factor,
    )
    place, frac, dest, table = pl.pallas_call(
        functools.partial(fetch_kernel, g),
        out_shape=(
            pltpu.VMEM(part_cell.shape, jnp.int32),
            pltpu.VMEM(part_frac.shape, f32),
            pltpu.VMEM((g.blocks, g.deep), jnp.int32),
            pltpu.VMEM((3 * g.slab + SUB, g.deep), f32),
        ),
        in_specs=[pl.BlockSpec(memory_space=pltpu.HBM)] * len(given),
        out_specs=(vmem,) * 4,
        scratch_shapes=[
            pltpu.SMEM(block_dest.shape, jnp.int32),
            pltpu.SMEM(block_count.shape, jnp.int32),
            pltpu.VMEM(part_cell.shape, jnp.int32),
            pltpu.VMEM(offsets.shape, jnp.int32),
            pltpu.VMEM(selection.shape, f32),
            pltpu.VMEM(galaxy_counts.shape, jnp.int32),
            pltpu.SMEM(bias_exp.shape, f32),
            pltpu.SMEM(rsd_factor.shape, f32),
            pltpu.SemaphoreType.DMA((len(given),)),
        ],
        compiler_params=small,
        name="fetch",
    )(*(pltpu.with_memory_space_constraint(x, pltpu.HBM) for x in given))
    keep, send = pl.pallas_call(
        functools.partial(paint_kernel, g),
        out_shape=(tiled(size // 2), tiled(size // 2)),
        in_specs=[vmem] * 3,
        out_specs=(vmem, vmem),
        scratch_shapes=[pltpu.VMEM((padded, g.deep), f32), pltpu.VMEM((padded, g.deep), f32)],
        compiler_params=small,
        cost_estimate=pl.CostEstimate(flops=10**9, bytes_accessed=10**7, transcendentals=0),
        name="paint",
    )(place, frac, dest)
    tables = [table] + [from_far(table, m) for m in range(1, g.planes)]
    quarters = g.plane // 2
    pair = (keep + to_near(send, 1)).reshape(quarters, g.column, g.deep)
    column = pair[0] + sum(to_near(pair[j], 2 * j) for j in range(1, quarters))
    parts = [column] + [from_far(column, m) for m in range(1, g.planes)]
    tall = g.column + SUB
    if sky_parts == 1:
        field = pl.pallas_call(
            functools.partial(field_kernel, g),
            out_shape=tiled(tall),
            in_specs=[vmem] * (2 * g.planes),
            out_specs=vmem,
            scratch_shapes=[pltpu.VMEM((g.column, g.deep), f32)],
            compiler_params=small,
            name="field",
        )(*parts, *tables)
    else:
        start = jnp.mod(-(lax.axis_index("los") // g.plane), g.planes)
        planes = lax.dynamic_slice_in_dim(jnp.stack(tables + tables), start, g.planes)
        cells = planes[:, : 3 * g.slab].reshape(g.planes, 3, g.slab_rows, g.cols, g.deep)
        core = sum(parts).reshape(g.planes, g.slab_rows, g.cols, g.deep)
        edge = passed_along(core[:, :, g.width], "sky", 1)
        density = core[:, :, : g.width].at[:, :, 0].add(edge)
        near = cells[:, :, :, : g.width]
        inner = cotangent_of(density, near[:, 0], near[:, 1], near[:, 2])
        rim = passed_along(inner[:, :, 0], "sky", -1)
        rest = jnp.zeros((g.planes, g.slab_rows, g.cols - g.width - 1, g.deep), f32)
        inner = jnp.concatenate([inner, rim[:, :, None], rest], axis=2).reshape(g.column, g.deep)
        rates = jnp.pad(planes[:, 3 * g.slab], ((0, SUB - g.planes), (0, 0)))
        field = jnp.concatenate([inner, rates])
    both = jnp.concatenate([field, to_near(field, 1)])
    fields = [both] + [to_near(both, 2 * j) for j in range(1, quarters)]
    grad_pos, grad_vel = pl.pallas_call(
        functools.partial(pull_kernel, g),
        out_shape=(
            jax.ShapeDtypeStruct(part_frac.shape, f32),
            jax.ShapeDtypeStruct((g.blocks, g.block), f32),
        ),
        in_specs=[vmem] * (3 + quarters),
        out_specs=(vmem, vmem),
        scratch_shapes=[pltpu.VMEM((padded, g.deep), f32), pltpu.VMEM((g.slabs, g.deep), f32)],
        compiler_params=small,
        name="pull",
    )(place, frac, dest, *fields)
    return grad_pos, grad_vel.reshape(-1)


def solution(mesh):
    return jax.shard_map(
        on_device,
        mesh=mesh,
        in_specs=(
            P(None, ("los", "sky")),
            P(None, ("los", "sky")),
            P(("los", "sky")),
            P(("los", "sky")),
            P(("los", "sky")),
            P("los", "sky", None),
            P("los", "sky", None),
            P("los"),
            P("los"),
        ),
        out_specs=(P(None, ("los", "sky")), P(("los", "sky"))),
        check_vma=False,
    )
```

time: 40.1 us -> 35.2 us (0.88)
  blocking collectives: 32.4 us -> 0 us
  starting transfers between devices: 0 us -> 20.4 us
  waiting for transfers between devices: 0 us -> 10.3 us
  Pallas kernels: 6.68 us -> 3.5 us
    all_to_all x2 -> x0, blocking collectives: 32.4 us -> none  [exchanged(): lax.all_to_all(chunks, 'los', split_axis=0, concat_axis=0, tiled=True)]
    ppermute x0 -> x14, starting transfers between devices: none -> 20.4 us  [the longest x6 11.8 us: passed_along(): return lax.ppermute(block, axis, route)]
    ppermute x0 -> x14, waiting for transfers between devices: none -> 10.3 us  [the longest x8 6.13 us: to_near(): return lax.ppermute(block, 'los', [(i ^ near, i) for i in range(g.slabs)])]
    pallas_call x2 -> x3, Pallas kernels: 4.35 us -> 2.13 us  [the longest x1 1.07 us: on_device(): pl.pallas_call(functools.partial(fetch_kernel, g), out_shape=(pltpu.VMEM(...]
    pallas_call x1, Pallas kernels: 2.33 us -> 1.37 us  [on_device(): pl.pallas_call(functools.partial(pull_kernel, g), out_shape=(jax.ShapeDty...]
  transfers between devices with their start and end apart: 0 -> 14, of which waited for: 0 -> 6; matrix products, arithmetic and copies ran while one was open for 0% -> 0% of each run, Pallas kernels for 0% -> 0%
where the time goes in v2:
time: 35.2 us; the launch traced here: 35 us
  starting transfers between devices  20.4 us (58%)
  waiting for transfers between devices  10.3 us (29%)
  Pallas kernels  3.5 us (10%)
  between operations  0.7 us (2%)
    ppermute x6, starting transfers between devices, passed_along(): return lax.ppermute(block, axis, route)  11.8 us
    ppermute x8, starting transfers between devices, to_near(): return lax.ppermute(block, 'los', [(i ^ near, i) for i in range(g.slabs)])  8.58 us
    ppermute x8, waiting for transfers between devices, to_near(): return lax.ppermute(block, 'los', [(i ^ near, i) for i in range(g.slabs)])  6.13 us
    ppermute x6, waiting for transfers between devices, passed_along(): return lax.ppermute(block, axis, route)  4.22 us
    pallas_call x1, Pallas kernels, on_device(): pl.pallas_call(functools.partial(pull_kernel, g), out_shape=(jax.ShapeDty...  1.37 us
    pallas_call x1, Pallas kernels, on_device(): pl.pallas_call(functools.partial(fetch_kernel, g), out_shape=(pltpu.VMEM(...  1.07 us
    pallas_call x1, Pallas kernels, on_device(): pl.pallas_call(functools.partial(paint_kernel, g), out_shape=(tiled(size...  1.01 us
  transfers between devices with their start and end apart: 14, of which 6 were waited for; matrix products, arithmetic and copies ran while one was open for 0% of the time, Pallas kernels for 0%

profile of v2, /device:TPU:0, one launch (start us, length us, event | category | flops | bytes accessed | tf_op | source)
XLA Modules:
  0.0 35.0 jit_solution(7436232021342383839)
XLA Ops:
  0.6 1.1 %fetch.1 = (s32[3,4096]{1,0:T(4,128)S(1)}, f32[3,4096]{1,0:T(4,128)S(1)}, s32[32,128]{1,0:T(8,128)S(1)}, f32[56,128]{1,0:T(8,128)S(1)}) custom-call(s32[32]{0:T(128)} %refs_0_.1, s32[32]{0:T(128)} %refs_1_.1, s32[3,4096]{1,0:T(4,128)} %refs_2_.1, f32[3,4096]{1,0:T(4,128)} %refs_3_.1, s32[32,128]{1,0:T(8,128)} %bitcast.2, f32[4,4,128]{2,1,0:T(4,128)} %refs_5_.1, ...), custom_call_target="tpu_custom_call" | custom-call | tf_op jit(solution)/shard_map/fetch/pallas_call | solution.py:276
  1.7 1.0 %paint.1 = (f32[256,128]{1,0:T(8,128)S(1)}, f32[256,128]{1,0:T(8,128)S(1)}) custom-call(s32[3,4096]{1,0:T(4,128)S(1)} %get-tuple-element.10.place_ref, f32[3,4096]{1,0:T(4,128)S(1)} %get-tuple-element.11.frac_ref, s32[32,128]{1,0:T(8,128)S(1)} %get-tuple-element.12.dest_ref), custom_call_target="tpu_custom_call" | custom-call | flops 1000000000 | bytes 10000000 | tf_op jit(solution)/shard_map/paint/pallas_call | solution.py:300
  2.7 0.5 %collective-permute-start = (f32[256,128]{1,0:T(8,128)S(1)}, f32[256,128]{1,0:T(8,128)S(1)}, u32[]{:S(2)}, u32[]{:S(2)}) collective-permute-start(f32[256,128]{1,0:T(8,128)S(1)} %get-tuple-element.14), channel_id=1, source_target_pairs={{1,0},{0,1},{3,2},{2,3},{5,4},{4,5},{7,6},{6,7},{9,8},{8,9},{11,10... | collective-permute-start | bytes 393224 | tf_op jit(solution)/shard_map/ppermute | solution.py:260
  3.2 1.0 %collective-permute-done = f32[256,128]{1,0:T(8,128)S(1)} collective-permute-done((f32[256,128]{1,0:T(8,128)S(1)}, f32[256,128]{1,0:T(8,128)S(1)}, u32[]{:S(2)}, u32[]{:S(2)}) %collective-permute-start) | collective-permute-done | bytes 131104 | tf_op jit(solution)/shard_map/ppermute | solution.py:260
  4.3 3.9 %collective-permute-start.3 = (f32[64,128]{1,0:T(8,128)S(1)}, f32[64,128]{1,0:T(8,128)S(1)}, u32[]{:S(2)}, u32[]{:S(2)}) collective-permute-start(f32[64,128]{1,0:T(8,128)S(1)} %get-tuple-element.19), channel_id=1, source_target_pairs={{6,0},{7,1},{4,2},{5,3},{2,4},{3,5},{0,6},{1,7},{14,8},{15,9},{12,... | collective-permute-start | bytes 98312 | tf_op jit(solution)/shard_map/ppermute | solution.py:260
  8.1 0.5 %collective-permute-start.1 = (f32[64,128]{1,0:T(8,128)S(1)}, f32[64,128]{1,0:T(8,128)S(1)}, u32[]{:S(2)}, u32[]{:S(2)}) collective-permute-start(f32[64,128]{1,0:T(8,128)S(1)} %get-tuple-element.20), channel_id=1, source_target_pairs={{2,0},{3,1},{0,2},{1,3},{6,4},{7,5},{4,6},{5,7},{10,8},{11,9},{8,1... | collective-permute-start | bytes 98312 | tf_op jit(solution)/shard_map/ppermute | solution.py:260
  8.7 0.1 collective-permute-start.2
  8.8 4.0 %collective-permute-start.7 = (f32[56,128]{1,0:T(8,128)S(1)}, f32[56,128]{1,0:T(8,128)S(1)}, u32[]{:S(2)}, u32[]{:S(2)}) collective-permute-start(f32[56,128]{1,0:T(8,128)S(1)} %get-tuple-element.15.refs_4_), channel_id=1, source_target_pairs={{8,0},{9,1},{10,2},{11,3},{12,4},{13,5},{14,6},{15,7},{16,8},{17,9... | collective-permute-start | bytes 86024 | tf_op jit(solution)/shard_map/ppermute | solution.py:17
  12.8 0.0 collective-permute-done.3
  12.8 0.0 collective-permute-done.1
  12.8 0.0 collective-permute-done.2
  12.8 3.4 %collective-permute-start.4 = (f32[64,128]{1,0:T(8,128)S(1)}, f32[64,128]{1,0:T(8,128)S(1)}, u32[]{:S(2)}, u32[]{:S(2)}) collective-permute-start(f32[64,128]{1,0:T(8,128)S(1)} %slice_add_fusion.refs_0_), channel_id=1, source_target_pairs={{8,0},{9,1},{10,2},{11,3},{12,4},{13,5},{14,6},{15,7},{16,8},{17,9... | collective-permute-start | bytes 98312 | tf_op jit(solution)/shard_map/ppermute | solution.py:17
  16.2 0.0 collective-permute-start.5
  16.2 1.0 %collective-permute-start.6 = (f32[64,128]{1,0:T(8,128)S(1)}, f32[64,128]{1,0:T(8,128)S(1)}, u32[]{:S(2)}, u32[]{:S(2)}) collective-permute-start(f32[64,128]{1,0:T(8,128)S(1)} %slice_add_fusion.refs_0_), channel_id=1, source_target_pairs={{24,0},{25,1},{26,2},{27,3},{28,4},{29,5},{30,6},{31,7},{0,8},{1,9... | collective-permute-start | bytes 98312 | tf_op jit(solution)/shard_map/ppermute | solution.py:17
  17.3 1.9 %collective-permute-start.8 = (f32[56,128]{1,0:T(8,128)S(1)}, f32[56,128]{1,0:T(8,128)S(1)}, u32[]{:S(2)}, u32[]{:S(2)}) collective-permute-start(f32[56,128]{1,0:T(8,128)S(1)} %get-tuple-element.15.refs_4_), channel_id=1, source_target_pairs={{16,0},{17,1},{18,2},{19,3},{20,4},{21,5},{22,6},{23,7},{24,8},{25... | collective-permute-start | bytes 86024 | tf_op jit(solution)/shard_map/ppermute | solution.py:17
  19.2 0.0 collective-permute-done.7.refs_5_
  19.2 1.5 %collective-permute-start.9 = (f32[56,128]{1,0:T(8,128)S(1)}, f32[56,128]{1,0:T(8,128)S(1)}, u32[]{:S(2)}, u32[]{:S(2)}) collective-permute-start(f32[56,128]{1,0:T(8,128)S(1)} %get-tuple-element.15.refs_4_), channel_id=1, source_target_pairs={{24,0},{25,1},{26,2},{27,3},{28,4},{29,5},{30,6},{31,7},{0,8},{1,9... | collective-permute-start | bytes 86024 | tf_op jit(solution)/shard_map/ppermute | solution.py:17
  20.6 1.6 %collective-permute-done.8.refs_6_ = f32[56,128]{1,0:T(8,128)S(1)} collective-permute-done((f32[56,128]{1,0:T(8,128)S(1)}, f32[56,128]{1,0:T(8,128)S(1)}, u32[]{:S(2)}, u32[]{:S(2)}) %collective-permute-start.8) | collective-permute-done | bytes 28704 | tf_op jit(solution)/shard_map/ppermute | solution.py:17
  22.3 2.6 %collective-permute-done.9.refs_7_ = f32[56,128]{1,0:T(8,128)S(1)} collective-permute-done((f32[56,128]{1,0:T(8,128)S(1)}, f32[56,128]{1,0:T(8,128)S(1)}, u32[]{:S(2)}, u32[]{:S(2)}) %collective-permute-start.9) | collective-permute-done | bytes 28704 | tf_op jit(solution)/shard_map/ppermute | solution.py:17
  24.8 0.0 collective-permute-done.4.refs_1_
  24.8 0.0 collective-permute-done.5.refs_2_
  24.9 0.0 collective-permute-done.6.refs_3_
  24.9 0.1 field.1
  24.9 0.1 collective-permute-start.10
  25.0 1.2 %collective-permute-done.10 = f32[72,128]{1,0:T(8,128)S(1)} collective-permute-done((f32[72,128]{1,0:T(8,128)S(1)}, f32[72,128]{1,0:T(8,128)S(1)}, u32[]{:S(2)}, u32[]{:S(2)}) %collective-permute-start.10) | collective-permute-done | bytes 36896 | tf_op jit(solution)/shard_map/ppermute | solution.py:260
  26.2 1.5 %collective-permute-start.11 = (f32[144,128]{1,0:T(8,128)S(1)}, f32[144,128]{1,0:T(8,128)S(1)}, u32[]{:S(2)}, u32[]{:S(2)}) collective-permute-start(f32[144,128]{1,0:T(8,128)S(1)} %pad_maximum_fusion.refs_0_), channel_id=1, source_target_pairs={{2,0},{3,1},{0,2},{1,3},{6,4},{7,5},{4,6},{5,7},{10,8},{11,9},{8,1... | collective-permute-start | bytes 221192 | tf_op jit(solution)/shard_map/ppermute | solution.py:260
  27.7 0.5 %collective-permute-start.12 = (f32[144,128]{1,0:T(8,128)S(1)}, f32[144,128]{1,0:T(8,128)S(1)}, u32[]{:S(2)}, u32[]{:S(2)}) collective-permute-start(f32[144,128]{1,0:T(8,128)S(1)} %pad_maximum_fusion.refs_0_), channel_id=1, source_target_pairs={{4,0},{5,1},{6,2},{7,3},{0,4},{1,5},{2,6},{3,7},{12,8},{13,9},{14,... | collective-permute-start | bytes 221192 | tf_op jit(solution)/shard_map/ppermute | solution.py:260
  28.2 1.5 %collective-permute-start.13 = (f32[144,128]{1,0:T(8,128)S(1)}, f32[144,128]{1,0:T(8,128)S(1)}, u32[]{:S(2)}, u32[]{:S(2)}) collective-permute-start(f32[144,128]{1,0:T(8,128)S(1)} %pad_maximum_fusion.refs_0_), channel_id=1, source_target_pairs={{6,0},{7,1},{4,2},{5,3},{2,4},{3,5},{0,6},{1,7},{14,8},{15,9},{12,... | collective-permute-start | bytes 221192 | tf_op jit(solution)/shard_map/ppermute | solution.py:260
  29.7 0.9 %collective-permute-done.11.refs_1_ = f32[144,128]{1,0:T(8,128)S(1)} collective-permute-done((f32[144,128]{1,0:T(8,128)S(1)}, f32[144,128]{1,0:T(8,128)S(1)}, u32[]{:S(2)}, u32[]{:S(2)}) %collective-permute-start.11) | collective-permute-done | bytes 73760 | tf_op jit(solution)/shard_map/ppermute | solution.py:260
  30.6 3.1 %collective-permute-done.12.refs_2_ = f32[144,128]{1,0:T(8,128)S(1)} collective-permute-done((f32[144,128]{1,0:T(8,128)S(1)}, f32[144,128]{1,0:T(8,128)S(1)}, u32[]{:S(2)}, u32[]{:S(2)}) %collective-permute-start.12) | collective-permute-done | bytes 73760 | tf_op jit(solution)/shard_map/ppermute | solution.py:260
  33.6 0.0 collective-permute-done.13.refs_3_
  33.6 1.4 %pull.1 = (f32[3,4096]{1,0:T(4,128)}, f32[32,128]{1,0:T(8,128)}) custom-call(s32[3,4096]{1,0:T(4,128)S(1)} %get-tuple-element.10.place_ref, f32[3,4096]{1,0:T(4,128)S(1)} %get-tuple-element.11.frac_ref, s32[32,128]{1,0:T(8,128)S(1)} %get-tuple-element.12.dest_ref, f32[144,128]{1,0:T(8,128)S(1)} %pad_maximum_fusion.refs_0_, ...), custom_call_target="tpu_custom_call" | custom-call | tf_op jit(solution)/shard_map/pull/pallas_call | solution.py:342
  (4 shorter events, 0.0 us)
Async XLA Ops:
  2.7 1.5 %collective-permute-start = (f32[256,128]{1,0:T(8,128)S(1)}, f32[256,128]{1,0:T(8,128)S(1)}, u32[]{:S(2)}, u32[]{:S(2)}) collective-permute-start(f32[256,128]{1,0:T(8,128)S(1)} %get-tuple-element.14), channel_id=1, source_target_pairs={{1,0},{0,1},{3,2},{2,3},{5,4},{4,5},{7,6},{6,7},{9,8},{8,9},{11,10... | collective-permute-start | bytes 393224 | tf_op jit(solution)/shard_map/ppermute | solution.py:260
  4.3 8.5 %collective-permute-start.3 = (f32[64,128]{1,0:T(8,128)S(1)}, f32[64,128]{1,0:T(8,128)S(1)}, u32[]{:S(2)}, u32[]{:S(2)}) collective-permute-start(f32[64,128]{1,0:T(8,128)S(1)} %get-tuple-element.19), channel_id=1, source_target_pairs={{6,0},{7,1},{4,2},{5,3},{2,4},{3,5},{0,6},{1,7},{14,8},{15,9},{12,... | collective-permute-start | bytes 98312 | tf_op jit(solution)/shard_map/ppermute | solution.py:260
  8.1 4.7 %collective-permute-start.1 = (f32[64,128]{1,0:T(8,128)S(1)}, f32[64,128]{1,0:T(8,128)S(1)}, u32[]{:S(2)}, u32[]{:S(2)}) collective-permute-start(f32[64,128]{1,0:T(8,128)S(1)} %get-tuple-element.20), channel_id=1, source_target_pairs={{2,0},{3,1},{0,2},{1,3},{6,4},{7,5},{4,6},{5,7},{10,8},{11,9},{8,1... | collective-permute-start | bytes 98312 | tf_op jit(solution)/shard_map/ppermute | solution.py:260
  8.7 4.1 %collective-permute-start.2 = (f32[64,128]{1,0:T(8,128)S(1)}, f32[64,128]{1,0:T(8,128)S(1)}, u32[]{:S(2)}, u32[]{:S(2)}) collective-permute-start(f32[64,128]{1,0:T(8,128)S(1)} %get-tuple-element.18), channel_id=1, source_target_pairs={{4,0},{5,1},{6,2},{7,3},{0,4},{1,5},{2,6},{3,7},{12,8},{13,9},{14,... | collective-permute-start | bytes 98312 | tf_op jit(solution)/shard_map/ppermute | solution.py:260
  8.8 10.4 %collective-permute-start.7 = (f32[56,128]{1,0:T(8,128)S(1)}, f32[56,128]{1,0:T(8,128)S(1)}, u32[]{:S(2)}, u32[]{:S(2)}) collective-permute-start(f32[56,128]{1,0:T(8,128)S(1)} %get-tuple-element.15.refs_4_), channel_id=1, source_target_pairs={{8,0},{9,1},{10,2},{11,3},{12,4},{13,5},{14,6},{15,7},{16,8},{17,9... | collective-permute-start | bytes 86024 | tf_op jit(solution)/shard_map/ppermute | solution.py:17
  12.8 12.0 %collective-permute-start.4 = (f32[64,128]{1,0:T(8,128)S(1)}, f32[64,128]{1,0:T(8,128)S(1)}, u32[]{:S(2)}, u32[]{:S(2)}) collective-permute-start(f32[64,128]{1,0:T(8,128)S(1)} %slice_add_fusion.refs_0_), channel_id=1, source_target_pairs={{8,0},{9,1},{10,2},{11,3},{12,4},{13,5},{14,6},{15,7},{16,8},{17,9... | collective-permute-start | bytes 98312 | tf_op jit(solution)/shard_map/ppermute | solution.py:17
  16.2 8.6 %collective-permute-start.5 = (f32[64,128]{1,0:T(8,128)S(1)}, f32[64,128]{1,0:T(8,128)S(1)}, u32[]{:S(2)}, u32[]{:S(2)}) collective-permute-start(f32[64,128]{1,0:T(8,128)S(1)} %slice_add_fusion.refs_0_), channel_id=1, source_target_pairs={{16,0},{17,1},{18,2},{19,3},{20,4},{21,5},{22,6},{23,7},{24,8},{25... | collective-permute-start | bytes 98312 | tf_op jit(solution)/shard_map/ppermute | solution.py:17
  16.2 8.6 %collective-permute-start.6 = (f32[64,128]{1,0:T(8,128)S(1)}, f32[64,128]{1,0:T(8,128)S(1)}, u32[]{:S(2)}, u32[]{:S(2)}) collective-permute-start(f32[64,128]{1,0:T(8,128)S(1)} %slice_add_fusion.refs_0_), channel_id=1, source_target_pairs={{24,0},{25,1},{26,2},{27,3},{28,4},{29,5},{30,6},{31,7},{0,8},{1,9... | collective-permute-start | bytes 98312 | tf_op jit(solution)/shard_map/ppermute | solution.py:17
  17.3 5.0 %collective-permute-start.8 = (f32[56,128]{1,0:T(8,128)S(1)}, f32[56,128]{1,0:T(8,128)S(1)}, u32[]{:S(2)}, u32[]{:S(2)}) collective-permute-start(f32[56,128]{1,0:T(8,128)S(1)} %get-tuple-element.15.refs_4_), channel_id=1, source_target_pairs={{16,0},{17,1},{18,2},{19,3},{20,4},{21,5},{22,6},{23,7},{24,8},{25... | collective-permute-start | bytes 86024 | tf_op jit(solution)/shard_map/ppermute | solution.py:17
  19.2 5.7 %collective-permute-start.9 = (f32[56,128]{1,0:T(8,128)S(1)}, f32[56,128]{1,0:T(8,128)S(1)}, u32[]{:S(2)}, u32[]{:S(2)}) collective-permute-start(f32[56,128]{1,0:T(8,128)S(1)} %get-tuple-element.15.refs_4_), channel_id=1, source_target_pairs={{24,0},{25,1},{26,2},{27,3},{28,4},{29,5},{30,6},{31,7},{0,8},{1,9... | collective-permute-start | bytes 86024 | tf_op jit(solution)/shard_map/ppermute | solution.py:17
  24.9 1.3 %collective-permute-start.10 = (f32[72,128]{1,0:T(8,128)S(1)}, f32[72,128]{1,0:T(8,128)S(1)}, u32[]{:S(2)}, u32[]{:S(2)}) collective-permute-start(f32[72,128]{1,0:T(8,128)S(1)} %field.1), channel_id=1, source_target_pairs={{1,0},{0,1},{3,2},{2,3},{5,4},{4,5},{7,6},{6,7},{9,8},{8,9},{11,10... | collective-permute-start | bytes 110600 | tf_op jit(solution)/shard_map/ppermute | solution.py:260
  26.2 4.4 %collective-permute-start.11 = (f32[144,128]{1,0:T(8,128)S(1)}, f32[144,128]{1,0:T(8,128)S(1)}, u32[]{:S(2)}, u32[]{:S(2)}) collective-permute-start(f32[144,128]{1,0:T(8,128)S(1)} %pad_maximum_fusion.refs_0_), channel_id=1, source_target_pairs={{2,0},{3,1},{0,2},{1,3},{6,4},{7,5},{4,6},{5,7},{10,8},{11,9},{8,1... | collective-permute-start | bytes 221192 | tf_op jit(solution)/shard_map/ppermute | solution.py:260
  27.7 5.9 %collective-permute-start.12 = (f32[144,128]{1,0:T(8,128)S(1)}, f32[144,128]{1,0:T(8,128)S(1)}, u32[]{:S(2)}, u32[]{:S(2)}) collective-permute-start(f32[144,128]{1,0:T(8,128)S(1)} %pad_maximum_fusion.refs_0_), channel_id=1, source_target_pairs={{4,0},{5,1},{6,2},{7,3},{0,4},{1,5},{2,6},{3,7},{12,8},{13,9},{14,... | collective-permute-start | bytes 221192 | tf_op jit(solution)/shard_map/ppermute | solution.py:260
  28.2 5.4 %collective-permute-start.13 = (f32[144,128]{1,0:T(8,128)S(1)}, f32[144,128]{1,0:T(8,128)S(1)}, u32[]{:S(2)}, u32[]{:S(2)}) collective-permute-start(f32[144,128]{1,0:T(8,128)S(1)} %pad_maximum_fusion.refs_0_), channel_id=1, source_target_pairs={{6,0},{7,1},{4,2},{5,3},{2,4},{3,5},{0,6},{1,7},{14,8},{15,9},{12,... | collective-permute-start | bytes 221192 | tf_op jit(solution)/shard_map/ppermute | solution.py:260

commit v3 on v2

--- a/solution.py
+++ b/solution.py
@@ -36,18 +36,16 @@
 
 def write_table(g, refs, table_ref):
     selection_ref, counts_ref, bias_ref, rate_ref = refs
+    sub = lax.broadcasted_iota(jnp.int32, (SUB, g.deep), 0)
     lane = lax.broadcasted_iota(jnp.int32, (SUB, g.deep), 1)
-    rate = jnp.zeros((SUB, g.deep), jnp.float32)
+    rest = jnp.zeros((SUB, g.deep), jnp.float32)
     table_ref[...] = jnp.zeros_like(table_ref)
     for j in range(g.slab_rows):
-        rate = jnp.where(lane == j, rate_ref[j], rate)
+        rest = jnp.where(lane == j, jnp.where(sub == 0, bias_ref[j], rate_ref[j]), rest)
         start = j * g.cols
         table_ref[start : start + g.width, :] = selection_ref[j]
         table_ref[g.slab + start : g.slab + start + g.width, :] = counts_ref[j].astype(jnp.float32)
-        table_ref[2 * g.slab + start : 2 * g.slab + start + g.cols, :] = jnp.full(
-            (g.cols, g.deep), bias_ref[j], jnp.float32
-        )
-    table_ref[3 * g.slab :, :] = rate
+    table_ref[2 * g.slab :, :] = rest
 
 
 def fetch_kernel(g, *refs):
@@ -135,21 +133,38 @@
     return (1.0 - counts.astype(jnp.float32) / intensity) * exponent * intensity / shifted
 
 
+def column_kernel(g, own_ref, *refs):
+    total = own_ref[...]
+    for ref in refs[:-2]:
+        total = total + ref[...]
+    refs[-1][: g.column, :] = total
+    refs[-1][g.column :, :] = refs[-2][...]
+
+
 def field_kernel(g, *refs):
-    part_refs, table_refs, out_ref, sum_ref = refs[: g.planes], refs[g.planes : 2 * g.planes], refs[-2], refs[-1]
-    total = part_refs[0][...]
+    part_refs, out_ref, sum_ref = refs[: g.planes], refs[-2], refs[-1]
+    total = part_refs[0][: g.column, :]
     for ref in part_refs[1:]:
-        total = total + ref[...]
+        total = total + ref[: g.column, :]
     sum_ref[...] = total
     far = lax.axis_index("los") // g.plane
+    plane = lax.broadcasted_iota(jnp.int32, (g.slab, g.deep), 0) // g.cols
     out_ref[g.column :, :] = jnp.zeros((SUB, g.deep), jnp.float32)
-    for m, ref in enumerate(table_refs):
-        there = lax.rem(far + m, g.planes)
+    for m, ref in enumerate(part_refs):
+        there = g.far_peer(far, m)
         at = pl.ds(pl.multiple_of(there * g.slab, SUB), g.slab)
-        out_ref[at, :] = cotangent_of(
-            sum_ref[at, :], ref[: g.slab, :], ref[g.slab : 2 * g.slab, :], ref[2 * g.slab : 3 * g.slab, :]
-        )
-        out_ref[pl.ds(g.column + there, 1), :] = ref[3 * g.slab : 3 * g.slab + 1, :]
+        start = g.column + 2 * g.slab
+        exponent = picked(jnp.broadcast_to(ref[start : start + 1, :], (g.slab, g.deep)), plane)
+        selection = ref[g.column : g.column + g.slab, :]
+        counts = ref[g.column + g.slab : start, :]
+        out_ref[at, :] = cotangent_of(sum_ref[at, :], selection, counts, exponent)
+        out_ref[pl.ds(g.column + there, 1), :] = ref[start + 1 : start + 2, :]
+
+
+def joined_kernel(*refs):
+    rows = refs[0].shape[0]
+    for i, ref in enumerate(refs[:-1]):
+        refs[-1][i * rows : (i + 1) * rows, :] = ref[...]
 
 
 def picked(rows, index):
@@ -161,7 +176,7 @@
     me = lax.axis_index("los")
     tall = g.column + SUB
     for near in range(g.plane):
-        ref, base = field_refs[near // 2], (near % 2) * tall
+        ref, base = field_refs[near % 2], (near // 2) * tall
         for far in range(g.planes):
             slab = slab_at(g, me, near, far)
             at = pl.ds(pl.multiple_of(slab * g.slab, SUB), g.slab)
@@ -227,6 +242,10 @@
         self.column = self.planes * self.slab
         self.window = rounded_up(self.slab + self.cols, SUB)
 
+    def far_peer(self, far, m):
+        even = self.planes & (self.planes - 1) == 0
+        return far ^ m if even else (far + m) % self.planes
+
 
 def on_device(
     part_cell,
@@ -260,7 +279,9 @@
         return lax.ppermute(block, "los", [(i ^ near, i) for i in range(g.slabs)])
 
     def from_far(block, m):
-        return passed_along(block, "los", -m * g.plane)
+        rest = [(i // g.plane, i % g.plane) for i in range(g.slabs)]
+        route = [(g.far_peer(far, m) * g.plane + near, far * g.plane + near) for far, near in rest]
+        return lax.ppermute(block, "los", route)
 
     given = (
         block_dest,
@@ -279,7 +300,7 @@
             pltpu.VMEM(part_cell.shape, jnp.int32),
             pltpu.VMEM(part_frac.shape, f32),
             pltpu.VMEM((g.blocks, g.deep), jnp.int32),
-            pltpu.VMEM((3 * g.slab + SUB, g.deep), f32),
+            pltpu.VMEM((2 * g.slab + SUB, g.deep), f32),
         ),
         in_specs=[pl.BlockSpec(memory_space=pltpu.HBM)] * len(given),
         out_specs=(vmem,) * 4,
@@ -307,45 +328,65 @@
         cost_estimate=pl.CostEstimate(flops=10**9, bytes_accessed=10**7, transcendentals=0),
         name="paint",
     )(place, frac, dest)
-    tables = [table] + [from_far(table, m) for m in range(1, g.planes)]
     quarters = g.plane // 2
     pair = (keep + to_near(send, 1)).reshape(quarters, g.column, g.deep)
-    column = pair[0] + sum(to_near(pair[j], 2 * j) for j in range(1, quarters))
+    column = pl.pallas_call(
+        functools.partial(column_kernel, g),
+        out_shape=tiled(g.column + 2 * g.slab + SUB),
+        in_specs=[vmem] * (quarters + 1),
+        out_specs=vmem,
+        compiler_params=small,
+        name="column",
+    )(pair[0], *(to_near(pair[j], 2 * j) for j in range(1, quarters)), table)
     parts = [column] + [from_far(column, m) for m in range(1, g.planes)]
     tall = g.column + SUB
     if sky_parts == 1:
         field = pl.pallas_call(
             functools.partial(field_kernel, g),
             out_shape=tiled(tall),
-            in_specs=[vmem] * (2 * g.planes),
+            in_specs=[vmem] * g.planes,
             out_specs=vmem,
             scratch_shapes=[pltpu.VMEM((g.column, g.deep), f32)],
             compiler_params=small,
             name="field",
-        )(*parts, *tables)
+        )(*parts)
     else:
-        start = jnp.mod(-(lax.axis_index("los") // g.plane), g.planes)
-        planes = lax.dynamic_slice_in_dim(jnp.stack(tables + tables), start, g.planes)
-        cells = planes[:, : 3 * g.slab].reshape(g.planes, 3, g.slab_rows, g.cols, g.deep)
-        core = sum(parts).reshape(g.planes, g.slab_rows, g.cols, g.deep)
+        here = lax.axis_index("los") // g.plane
+        stacked = jnp.stack(parts)
+        planes = jnp.zeros_like(stacked[:, g.column :])
+        for m in range(g.planes):
+            planes = lax.dynamic_update_index_in_dim(
+                planes, stacked[m, g.column :], g.far_peer(here, m), 0
+            )
+        cells = planes[:, : 2 * g.slab].reshape(g.planes, 2, g.slab_rows, g.cols, g.deep)
+        power = planes[:, 2 * g.slab, : g.slab_rows, None, None]
+        core = jnp.sum(stacked[:, : g.column], axis=0)
+        core = core.reshape(g.planes, g.slab_rows, g.cols, g.deep)
         edge = passed_along(core[:, :, g.width], "sky", 1)
         density = core[:, :, : g.width].at[:, :, 0].add(edge)
         near = cells[:, :, :, : g.width]
-        inner = cotangent_of(density, near[:, 0], near[:, 1], near[:, 2])
+        inner = cotangent_of(density, near[:, 0], near[:, 1], power)
         rim = passed_along(inner[:, :, 0], "sky", -1)
         rest = jnp.zeros((g.planes, g.slab_rows, g.cols - g.width - 1, g.deep), f32)
         inner = jnp.concatenate([inner, rim[:, :, None], rest], axis=2).reshape(g.column, g.deep)
-        rates = jnp.pad(planes[:, 3 * g.slab], ((0, SUB - g.planes), (0, 0)))
+        rates = jnp.pad(planes[:, 2 * g.slab + 1], ((0, SUB - g.planes), (0, 0)))
         field = jnp.concatenate([inner, rates])
-    both = jnp.concatenate([field, to_near(field, 1)])
-    fields = [both] + [to_near(both, 2 * j) for j in range(1, quarters)]
+    even = pl.pallas_call(
+        joined_kernel,
+        out_shape=tiled(quarters * tall),
+        in_specs=[vmem] * quarters,
+        out_specs=vmem,
+        compiler_params=small,
+        name="joined",
+    )(field, *(to_near(field, 2 * j) for j in range(1, quarters)))
+    fields = [even, to_near(even, 1)]
     grad_pos, grad_vel = pl.pallas_call(
         functools.partial(pull_kernel, g),
         out_shape=(
             jax.ShapeDtypeStruct(part_frac.shape, f32),
             jax.ShapeDtypeStruct((g.blocks, g.block), f32),
         ),
-        in_specs=[vmem] * (3 + quarters),
+        in_specs=[vmem] * 5,
         out_specs=(vmem, vmem),
         scratch_shapes=[pltpu.VMEM((padded, g.deep), f32), pltpu.VMEM((g.slabs, g.deep), f32)],
         compiler_params=small,

time: 35.2 us -> 30.4 us (0.86)
  starting transfers between devices: 20.4 us -> 13.1 us
  waiting for transfers between devices: 10.3 us -> 12.8 us
    ppermute x6 -> x3, starting transfers between devices: 11.8 us -> 4.45 us  [from_far(): return lax.ppermute(block, 'los', route)]
    ppermute x8, waiting for transfers between devices: 6.13 us -> 8.59 us  [to_near(): return lax.ppermute(block, 'los', [(i ^ near, i) for i in range(g.slabs)])]
    ppermute x6 -> x3, waiting for transfers between devices: 4.22 us -> 4.25 us  [from_far(): return lax.ppermute(block, 'los', route)]
  transfers between devices with their start and end apart: 14 -> 11, of which waited for: 6 -> 10; matrix products, arithmetic and copies ran while one was open for 0% -> 0% of each run, Pallas kernels for 0% -> 0%
where the time goes in v3:
time: 30.4 us; the launch traced here: 30.2 us
  starting transfers between devices  13.1 us (43%)
  waiting for transfers between devices  12.8 us (42%)
  Pallas kernels  3.57 us (12%)
  between operations  0.69 us (2%)
    ppermute x8, starting transfers between devices, to_near(): return lax.ppermute(block, 'los', [(i ^ near, i) for i in range(g.slabs)])  8.65 us
    ppermute x8, waiting for transfers between devices, to_near(): return lax.ppermute(block, 'los', [(i ^ near, i) for i in range(g.slabs)])  8.59 us
    ppermute x3, starting transfers between devices, from_far(): return lax.ppermute(block, 'los', route)  4.45 us
    ppermute x3, waiting for transfers between devices, from_far(): return lax.ppermute(block, 'los', route)  4.25 us
    pallas_call x1, Pallas kernels, on_device(): pl.pallas_call(functools.partial(pull_kernel, g), out_shape=(jax.ShapeDty...  1.37 us
    pallas_call x1, Pallas kernels, on_device(): pl.pallas_call(functools.partial(fetch_kernel, g), out_shape=(pltpu.VMEM(...  1.06 us
    pallas_call x1, Pallas kernels, on_device(): pl.pallas_call(functools.partial(paint_kernel, g), out_shape=(tiled(size...  1.01 us
  transfers between devices with their start and end apart: 11, of which 10 were waited for; matrix products, arithmetic and copies ran while one was open for 0% of the time, Pallas kernels for 0%

profile of v3, /device:TPU:0, one launch (start us, length us, event | category | flops | bytes accessed | tf_op | source)
XLA Modules:
  0.0 30.2 jit_solution(15136417951955454675)
XLA Ops:
  0.6 1.1 %fetch.1 = (s32[3,4096]{1,0:T(4,128)S(1)}, f32[3,4096]{1,0:T(4,128)S(1)}, s32[32,128]{1,0:T(8,128)S(1)}, f32[40,128]{1,0:T(8,128)S(1)}) custom-call(s32[32]{0:T(128)} %refs_0_.1, s32[32]{0:T(128)} %refs_1_.1, s32[3,4096]{1,0:T(4,128)} %refs_2_.1, f32[3,4096]{1,0:T(4,128)} %refs_3_.1, s32[32,128]{1,0:T(8,128)} %bitcast.2, f32[4,4,128]{2,1,0:T(4,128)} %refs_5_.1, ...), custom_call_target="tpu_custom_call" | custom-call | tf_op jit(solution)/shard_map/fetch/pallas_call | solution.py:297
  1.7 1.0 %paint.1 = (f32[256,128]{1,0:T(8,128)S(1)}, f32[256,128]{1,0:T(8,128)S(1)}) custom-call(s32[3,4096]{1,0:T(4,128)S(1)} %get-tuple-element.10.place_ref, f32[3,4096]{1,0:T(4,128)S(1)} %get-tuple-element.11.frac_ref, s32[32,128]{1,0:T(8,128)S(1)} %get-tuple-element.12.dest_ref), custom_call_target="tpu_custom_call" | custom-call | flops 1000000000 | bytes 10000000 | tf_op jit(solution)/shard_map/paint/pallas_call | solution.py:321
  2.7 0.5 %collective-permute-start = (f32[256,128]{1,0:T(8,128)S(1)}, f32[256,128]{1,0:T(8,128)S(1)}, u32[]{:S(2)}, u32[]{:S(2)}) collective-permute-start(f32[256,128]{1,0:T(8,128)S(1)} %get-tuple-element.14), channel_id=1, source_target_pairs={{1,0},{0,1},{3,2},{2,3},{5,4},{4,5},{7,6},{6,7},{9,8},{8,9},{11,10... | collective-permute-start | bytes 393224 | tf_op jit(solution)/shard_map/ppermute | solution.py:279
  3.2 1.0 %collective-permute-done = f32[256,128]{1,0:T(8,128)S(1)} collective-permute-done((f32[256,128]{1,0:T(8,128)S(1)}, f32[256,128]{1,0:T(8,128)S(1)}, u32[]{:S(2)}, u32[]{:S(2)}) %collective-permute-start) | collective-permute-done | bytes 131104 | tf_op jit(solution)/shard_map/ppermute | solution.py:279
  4.3 3.9 %collective-permute-start.3 = (f32[64,128]{1,0:T(8,128)S(1)}, f32[64,128]{1,0:T(8,128)S(1)}, u32[]{:S(2)}, u32[]{:S(2)}) collective-permute-start(f32[64,128]{1,0:T(8,128)S(1)} %get-tuple-element.18), channel_id=1, source_target_pairs={{6,0},{7,1},{4,2},{5,3},{2,4},{3,5},{0,6},{1,7},{14,8},{15,9},{12,... | collective-permute-start | bytes 98312 | tf_op jit(solution)/shard_map/ppermute | solution.py:279
  8.1 0.5 %collective-permute-start.2 = (f32[64,128]{1,0:T(8,128)S(1)}, f32[64,128]{1,0:T(8,128)S(1)}, u32[]{:S(2)}, u32[]{:S(2)}) collective-permute-start(f32[64,128]{1,0:T(8,128)S(1)} %get-tuple-element.19), channel_id=1, source_target_pairs={{4,0},{5,1},{6,2},{7,3},{0,4},{1,5},{2,6},{3,7},{12,8},{13,9},{14,... | collective-permute-start | bytes 98312 | tf_op jit(solution)/shard_map/ppermute | solution.py:279
  8.6 0.1 collective-permute-start.1
  8.8 1.3 %collective-permute-done.3.refs_2_ = f32[64,128]{1,0:T(8,128)S(1)} collective-permute-done((f32[64,128]{1,0:T(8,128)S(1)}, f32[64,128]{1,0:T(8,128)S(1)}, u32[]{:S(2)}, u32[]{:S(2)}) %collective-permute-start.3) | collective-permute-done | bytes 32800 | tf_op jit(solution)/shard_map/ppermute | solution.py:279
  10.0 2.0 %collective-permute-done.2.refs_1_ = f32[64,128]{1,0:T(8,128)S(1)} collective-permute-done((f32[64,128]{1,0:T(8,128)S(1)}, f32[64,128]{1,0:T(8,128)S(1)}, u32[]{:S(2)}, u32[]{:S(2)}) %collective-permute-start.2) | collective-permute-done | bytes 32800 | tf_op jit(solution)/shard_map/ppermute | solution.py:279
  12.0 0.5 %collective-permute-done.1.refs_0_ = f32[64,128]{1,0:T(8,128)S(1)} collective-permute-done((f32[64,128]{1,0:T(8,128)S(1)}, f32[64,128]{1,0:T(8,128)S(1)}, u32[]{:S(2)}, u32[]{:S(2)}) %collective-permute-start.1) | collective-permute-done | bytes 32800 | tf_op jit(solution)/shard_map/ppermute | solution.py:279
  12.6 3.7 %collective-permute-start.6 = (f32[104,128]{1,0:T(8,128)S(1)}, f32[104,128]{1,0:T(8,128)S(1)}, u32[]{:S(2)}, u32[]{:S(2)}) collective-permute-start(f32[104,128]{1,0:T(8,128)S(1)} %column.1.refs_0_), channel_id=1, source_target_pairs={{24,0},{25,1},{26,2},{27,3},{28,4},{29,5},{30,6},{31,7},{16,8},{17... | collective-permute-start | bytes 159752 | tf_op jit(solution)/shard_map/ppermute | solution.py:284
  16.2 0.0 collective-permute-start.5
  16.2 0.8 %collective-permute-start.4 = (f32[104,128]{1,0:T(8,128)S(1)}, f32[104,128]{1,0:T(8,128)S(1)}, u32[]{:S(2)}, u32[]{:S(2)}) collective-permute-start(f32[104,128]{1,0:T(8,128)S(1)} %column.1.refs_0_), channel_id=1, source_target_pairs={{8,0},{9,1},{10,2},{11,3},{12,4},{13,5},{14,6},{15,7},{0,8},{1,9},... | collective-permute-start | bytes 159752 | tf_op jit(solution)/shard_map/ppermute | solution.py:284
  17.0 1.6 %collective-permute-done.6.refs_3_ = f32[104,128]{1,0:T(8,128)S(1)} collective-permute-done((f32[104,128]{1,0:T(8,128)S(1)}, f32[104,128]{1,0:T(8,128)S(1)}, u32[]{:S(2)}, u32[]{:S(2)}) %collective-permute-start.6) | collective-permute-done | bytes 53280 | tf_op jit(solution)/shard_map/ppermute | solution.py:284
  18.7 2.6 %collective-permute-done.5.refs_2_ = f32[104,128]{1,0:T(8,128)S(1)} collective-permute-done((f32[104,128]{1,0:T(8,128)S(1)}, f32[104,128]{1,0:T(8,128)S(1)}, u32[]{:S(2)}, u32[]{:S(2)}) %collective-permute-start.5) | collective-permute-done | bytes 53280 | tf_op jit(solution)/shard_map/ppermute | solution.py:284
  21.3 0.0 collective-permute-done.4.refs_1_
  21.3 0.1 field.1.refs_0_
  21.4 1.6 %collective-permute-start.9 = (f32[72,128]{1,0:T(8,128)S(1)}, f32[72,128]{1,0:T(8,128)S(1)}, u32[]{:S(2)}, u32[]{:S(2)}) collective-permute-start(f32[72,128]{1,0:T(8,128)S(1)} %field.1.refs_0_), channel_id=1, source_target_pairs={{6,0},{7,1},{4,2},{5,3},{2,4},{3,5},{0,6},{1,7},{14,8},{15,9},{12,... | collective-permute-start | bytes 110600 | tf_op jit(solution)/shard_map/ppermute | solution.py:279
  22.9 0.5 %collective-permute-start.8 = (f32[72,128]{1,0:T(8,128)S(1)}, f32[72,128]{1,0:T(8,128)S(1)}, u32[]{:S(2)}, u32[]{:S(2)}) collective-permute-start(f32[72,128]{1,0:T(8,128)S(1)} %field.1.refs_0_), channel_id=1, source_target_pairs={{4,0},{5,1},{6,2},{7,3},{0,4},{1,5},{2,6},{3,7},{12,8},{13,9},{14,... | collective-permute-start | bytes 110600 | tf_op jit(solution)/shard_map/ppermute | solution.py:279
  23.4 1.5 %collective-permute-start.7 = (f32[72,128]{1,0:T(8,128)S(1)}, f32[72,128]{1,0:T(8,128)S(1)}, u32[]{:S(2)}, u32[]{:S(2)}) collective-permute-start(f32[72,128]{1,0:T(8,128)S(1)} %field.1.refs_0_), channel_id=1, source_target_pairs={{2,0},{3,1},{0,2},{1,3},{6,4},{7,5},{4,6},{5,7},{10,8},{11,9},{8,1... | collective-permute-start | bytes 110600 | tf_op jit(solution)/shard_map/ppermute | solution.py:279
  24.9 1.4 %collective-permute-done.9.refs_3_ = f32[72,128]{1,0:T(8,128)S(1)} collective-permute-done((f32[72,128]{1,0:T(8,128)S(1)}, f32[72,128]{1,0:T(8,128)S(1)}, u32[]{:S(2)}, u32[]{:S(2)}) %collective-permute-start.9) | collective-permute-done | bytes 36896 | tf_op jit(solution)/shard_map/ppermute | solution.py:279
  26.3 0.6 %collective-permute-done.8.refs_2_ = f32[72,128]{1,0:T(8,128)S(1)} collective-permute-done((f32[72,128]{1,0:T(8,128)S(1)}, f32[72,128]{1,0:T(8,128)S(1)}, u32[]{:S(2)}, u32[]{:S(2)}) %collective-permute-start.8) | collective-permute-done | bytes 36896 | tf_op jit(solution)/shard_map/ppermute | solution.py:279
  26.9 0.5 %collective-permute-done.7.refs_1_ = f32[72,128]{1,0:T(8,128)S(1)} collective-permute-done((f32[72,128]{1,0:T(8,128)S(1)}, f32[72,128]{1,0:T(8,128)S(1)}, u32[]{:S(2)}, u32[]{:S(2)}) %collective-permute-start.7) | collective-permute-done | bytes 36896 | tf_op jit(solution)/shard_map/ppermute | solution.py:279
  27.4 0.1 collective-permute-start.10
  27.5 1.4 %collective-permute-done.10.refs_1_ = f32[288,128]{1,0:T(8,128)S(1)} collective-permute-done((f32[288,128]{1,0:T(8,128)S(1)}, f32[288,128]{1,0:T(8,128)S(1)}, u32[]{:S(2)}, u32[]{:S(2)}) %collective-permute-start.10) | collective-permute-done | bytes 147488 | tf_op jit(solution)/shard_map/ppermute | solution.py:279
  28.9 1.4 %pull.1 = (f32[3,4096]{1,0:T(4,128)}, f32[32,128]{1,0:T(8,128)}) custom-call(s32[3,4096]{1,0:T(4,128)S(1)} %get-tuple-element.10.place_ref, f32[3,4096]{1,0:T(4,128)S(1)} %get-tuple-element.11.frac_ref, s32[32,128]{1,0:T(8,128)S(1)} %get-tuple-element.12.dest_ref, f32[288,128]{1,0:T(8,128)S(1)} %joined.1.refs_0_, f32[288,128]{1,0:T(8,128)S(1)} %collective-permute-done.10.refs_1_), custom_call_target="tpu_custom_call" | custom-call | tf_op jit(solution)/shard_map/pull/pallas_call | solution.py:383
  (4 shorter events, 0.1 us)
Async XLA Ops:
  2.7 1.5 %collective-permute-start = (f32[256,128]{1,0:T(8,128)S(1)}, f32[256,128]{1,0:T(8,128)S(1)}, u32[]{:S(2)}, u32[]{:S(2)}) collective-permute-start(f32[256,128]{1,0:T(8,128)S(1)} %get-tuple-element.14), channel_id=1, source_target_pairs={{1,0},{0,1},{3,2},{2,3},{5,4},{4,5},{7,6},{6,7},{9,8},{8,9},{11,10... | collective-permute-start | bytes 393224 | tf_op jit(solution)/shard_map/ppermute | solution.py:279
  4.3 5.8 %collective-permute-start.3 = (f32[64,128]{1,0:T(8,128)S(1)}, f32[64,128]{1,0:T(8,128)S(1)}, u32[]{:S(2)}, u32[]{:S(2)}) collective-permute-start(f32[64,128]{1,0:T(8,128)S(1)} %get-tuple-element.18), channel_id=1, source_target_pairs={{6,0},{7,1},{4,2},{5,3},{2,4},{3,5},{0,6},{1,7},{14,8},{15,9},{12,... | collective-permute-start | bytes 98312 | tf_op jit(solution)/shard_map/ppermute | solution.py:279
  8.1 3.9 %collective-permute-start.2 = (f32[64,128]{1,0:T(8,128)S(1)}, f32[64,128]{1,0:T(8,128)S(1)}, u32[]{:S(2)}, u32[]{:S(2)}) collective-permute-start(f32[64,128]{1,0:T(8,128)S(1)} %get-tuple-element.19), channel_id=1, source_target_pairs={{4,0},{5,1},{6,2},{7,3},{0,4},{1,5},{2,6},{3,7},{12,8},{13,9},{14,... | collective-permute-start | bytes 98312 | tf_op jit(solution)/shard_map/ppermute | solution.py:279
  8.6 3.9 %collective-permute-start.1 = (f32[64,128]{1,0:T(8,128)S(1)}, f32[64,128]{1,0:T(8,128)S(1)}, u32[]{:S(2)}, u32[]{:S(2)}) collective-permute-start(f32[64,128]{1,0:T(8,128)S(1)} %get-tuple-element.20), channel_id=1, source_target_pairs={{2,0},{3,1},{0,2},{1,3},{6,4},{7,5},{4,6},{5,7},{10,8},{11,9},{8,1... | collective-permute-start | bytes 98312 | tf_op jit(solution)/shard_map/ppermute | solution.py:279
  12.6 6.1 %collective-permute-start.6 = (f32[104,128]{1,0:T(8,128)S(1)}, f32[104,128]{1,0:T(8,128)S(1)}, u32[]{:S(2)}, u32[]{:S(2)}) collective-permute-start(f32[104,128]{1,0:T(8,128)S(1)} %column.1.refs_0_), channel_id=1, source_target_pairs={{24,0},{25,1},{26,2},{27,3},{28,4},{29,5},{30,6},{31,7},{16,8},{17... | collective-permute-start | bytes 159752 | tf_op jit(solution)/shard_map/ppermute | solution.py:284
  16.2 5.0 %collective-permute-start.5 = (f32[104,128]{1,0:T(8,128)S(1)}, f32[104,128]{1,0:T(8,128)S(1)}, u32[]{:S(2)}, u32[]{:S(2)}) collective-permute-start(f32[104,128]{1,0:T(8,128)S(1)} %column.1.refs_0_), channel_id=1, source_target_pairs={{16,0},{17,1},{18,2},{19,3},{20,4},{21,5},{22,6},{23,7},{24,8},{25... | collective-permute-start | bytes 159752 | tf_op jit(solution)/shard_map/ppermute | solution.py:284
  16.2 5.0 %collective-permute-start.4 = (f32[104,128]{1,0:T(8,128)S(1)}, f32[104,128]{1,0:T(8,128)S(1)}, u32[]{:S(2)}, u32[]{:S(2)}) collective-permute-start(f32[104,128]{1,0:T(8,128)S(1)} %column.1.refs_0_), channel_id=1, source_target_pairs={{8,0},{9,1},{10,2},{11,3},{12,4},{13,5},{14,6},{15,7},{0,8},{1,9},... | collective-permute-start | bytes 159752 | tf_op jit(solution)/shard_map/ppermute | solution.py:284
  21.4 4.9 %collective-permute-start.9 = (f32[72,128]{1,0:T(8,128)S(1)}, f32[72,128]{1,0:T(8,128)S(1)}, u32[]{:S(2)}, u32[]{:S(2)}) collective-permute-start(f32[72,128]{1,0:T(8,128)S(1)} %field.1.refs_0_), channel_id=1, source_target_pairs={{6,0},{7,1},{4,2},{5,3},{2,4},{3,5},{0,6},{1,7},{14,8},{15,9},{12,... | collective-permute-start | bytes 110600 | tf_op jit(solution)/shard_map/ppermute | solution.py:279
  22.9 4.0 %collective-permute-start.8 = (f32[72,128]{1,0:T(8,128)S(1)}, f32[72,128]{1,0:T(8,128)S(1)}, u32[]{:S(2)}, u32[]{:S(2)}) collective-permute-start(f32[72,128]{1,0:T(8,128)S(1)} %field.1.refs_0_), channel_id=1, source_target_pairs={{4,0},{5,1},{6,2},{7,3},{0,4},{1,5},{2,6},{3,7},{12,8},{13,9},{14,... | collective-permute-start | bytes 110600 | tf_op jit(solution)/shard_map/ppermute | solution.py:279
  23.4 4.0 %collective-permute-start.7 = (f32[72,128]{1,0:T(8,128)S(1)}, f32[72,128]{1,0:T(8,128)S(1)}, u32[]{:S(2)}, u32[]{:S(2)}) collective-permute-start(f32[72,128]{1,0:T(8,128)S(1)} %field.1.refs_0_), channel_id=1, source_target_pairs={{2,0},{3,1},{0,2},{1,3},{6,4},{7,5},{4,6},{5,7},{10,8},{11,9},{8,1... | collective-permute-start | bytes 110600 | tf_op jit(solution)/shard_map/ppermute | solution.py:279
  27.4 1.4 %collective-permute-start.10 = (f32[288,128]{1,0:T(8,128)S(1)}, f32[288,128]{1,0:T(8,128)S(1)}, u32[]{:S(2)}, u32[]{:S(2)}) collective-permute-start(f32[288,128]{1,0:T(8,128)S(1)} %joined.1.refs_0_), channel_id=1, source_target_pairs={{1,0},{0,1},{3,2},{2,3},{5,4},{4,5},{7,6},{6,7},{9,8},{8,9},{11,10... | collective-permute-start | bytes 442376 | tf_op jit(solution)/shard_map/ppermute | solution.py:279

commit v4 on v3

--- a/solution.py
+++ b/solution.py
@@ -48,41 +48,41 @@
     table_ref[2 * g.slab :, :] = rest
 
 
-def fetch_kernel(g, *refs):
-    far_refs, (place_ref, frac_ref, dest_ref, table_ref), near_refs = refs[:9], refs[9:13], refs[13:]
-    arrived = near_refs[-1]
-    near_refs = (*near_refs[:3], frac_ref, *near_refs[3:-1])
+def started(sources, targets, arrived):
     copies = [
         pltpu.make_async_copy(a, b, arrived.at[i])
-        for i, (a, b) in enumerate(zip(far_refs, near_refs, strict=True))
+        for i, (a, b) in enumerate(zip(sources, targets, strict=True))
     ]
     for copy in copies:
         copy.start()
+    return copies
+
+
+def dest_of(dest_ref, k):
+    return dest_ref[k : k + 1, 0:1][0, 0]
+
+
+def red_of(g, cell, offset):
+    even = g.slab_rows & (g.slab_rows - 1) == 0
+    return (cell + offset) & (g.slab_rows - 1) if even else jnp.mod(cell + offset, g.slab_rows)
+
+
+def paint_kernel(g, *refs):
+    far_refs, (cell_ref, frac_ref, offset_ref, keep_ref, send_ref), refs = refs[:5], refs[5:10], refs[10:]
+    dest_ref, count_ref, low_ref, high_ref, arrived = refs
+    copies = started(far_refs, (dest_ref, count_ref, cell_ref, frac_ref, offset_ref), arrived)
+    low_ref[...] = jnp.zeros_like(low_ref)
+    high_ref[...] = jnp.zeros_like(high_ref)
     for copy in copies:
         copy.wait()
-    blocks_ref, count_ref, cell_ref, frac_ref, offset_ref = near_refs[:5]
-    write_table(g, near_refs[5:], table_ref)
-    lane = lax.broadcasted_iota(jnp.int32, (1, g.block), 1)
-    for k in range(g.blocks):
-        lanes = slice(k * g.block, (k + 1) * g.block)
-        red = jnp.mod(cell_ref[0:1, lanes] + offset_ref[k : k + 1, :], g.slab_rows)
-        deep = jnp.where(lane < count_ref[k], cell_ref[2:3, lanes], -1)
-        place_ref[:, lanes] = jnp.concatenate([red, cell_ref[1:2, lanes], deep], axis=0)
-        dest_ref[k : k + 1, :] = jnp.full((1, g.deep), blocks_ref[k], jnp.int32)
-
-
-def dest_of(dest_ref, k):
-    return dest_ref[k : k + 1, 0:1][0, 0]
-
-
-def paint_kernel(g, place_ref, frac_ref, dest_ref, keep_ref, send_ref, low_ref, high_ref):
-    low_ref[...] = jnp.zeros_like(low_ref)
-    high_ref[...] = jnp.zeros_like(high_ref)
+    lane = lax.broadcasted_iota(jnp.int32, (SUB, g.block), 1)
     plane_iota, sky_iota = row_iotas(g.cols)
     deep_iota = lax.broadcasted_iota(jnp.int32, (g.deep, g.block), 0)
+    deep_iota = deep_iota.astype(jnp.float32).astype(g.cell_type)
     for k in range(g.blocks):
-        red = block_rows(place_ref, 0, k, g.block)
-        sky = block_rows(place_ref, 1, k, g.block)
+        offset = jnp.broadcast_to(offset_ref[k : k + 1, :], (SUB, g.block))
+        red = red_of(g, block_rows(cell_ref, 0, k, g.block), offset)
+        sky = block_rows(cell_ref, 1, k, g.block)
         sky_next = jnp.where(sky + 1 == g.sky_wrap, 0, sky + 1)
         frac_los = block_rows(frac_ref, 0, k, g.block)
         frac_sky = block_rows(frac_ref, 1, k, g.block)
@@ -90,6 +90,7 @@
         on_sky = jnp.where(
             sky_iota == sky, 1.0 - frac_sky, jnp.where(sky_iota == sky_next, frac_sky, 0.0)
         )
+        on_sky = jnp.where(lane < count_ref[k], on_sky, 0.0)
         rows = []
         for i in range(g.window // SUB):
             plane = plane_iota + i * g.planes_per_tile - red
@@ -102,8 +103,10 @@
         weight = jnp.concatenate([weight - upper, upper], axis=0)
         coarse = weight.astype(jnp.bfloat16)
         fine = (weight - coarse.astype(jnp.float32)).astype(jnp.bfloat16)
-        deep = jnp.broadcast_to(place_ref[2:3, k * g.block : (k + 1) * g.block], (g.deep, g.block))
-        hit = jnp.where(deep_iota == deep, 1.0, 0.0).astype(jnp.bfloat16)
+        deep = cell_ref[2:3, k * g.block : (k + 1) * g.block].astype(jnp.float32)
+        hit = deep_iota == jnp.broadcast_to(deep.astype(g.cell_type), (g.deep, g.block))
+        one, zero = jnp.ones_like(deep_iota), jnp.zeros_like(deep_iota)
+        hit = jnp.where(hit, one, zero).astype(jnp.bfloat16)
         got = lax.dot_general(
             jnp.concatenate([coarse, fine], axis=0),
             hit,
@@ -111,7 +114,7 @@
             preferred_element_type=jnp.float32,
         )
         got = got[: 2 * g.window] + got[2 * g.window :]
-        at = pl.ds(pl.multiple_of(dest_of(dest_ref, k) * g.slab, SUB), g.window)
+        at = pl.ds(pl.multiple_of(dest_ref[k] * g.slab, SUB), g.window)
         low_ref[at, :] += got[: g.window]
         high_ref[at, :] += got[g.window :]
     size = g.slabs * g.slab
@@ -150,8 +153,8 @@
     far = lax.axis_index("los") // g.plane
     plane = lax.broadcasted_iota(jnp.int32, (g.slab, g.deep), 0) // g.cols
     out_ref[g.column :, :] = jnp.zeros((SUB, g.deep), jnp.float32)
-    for m, ref in enumerate(part_refs):
-        there = g.far_peer(far, m)
+    for i, ref in enumerate(part_refs):
+        there = g.far_peer(far, i)
         at = pl.ds(pl.multiple_of(there * g.slab, SUB), g.slab)
         start = g.column + 2 * g.slab
         exponent = picked(jnp.broadcast_to(ref[start : start + 1, :], (g.slab, g.deep)), plane)
@@ -164,15 +167,64 @@
 def joined_kernel(*refs):
     rows = refs[0].shape[0]
     for i, ref in enumerate(refs[:-1]):
-        refs[-1][i * rows : (i + 1) * rows, :] = ref[...]
+        at = i * rows
+        refs[-1][at : at + rows, :] = ref[...]
 
 
 def picked(rows, index):
     return jnp.take_along_axis(rows, index, axis=1, mode="promise_in_bounds")
 
 
-def pull_kernel(g, place_ref, frac_ref, dest_ref, *refs):
-    field_refs, (pos_ref, vel_ref, whole_ref, rate_ref) = refs[:-4], refs[-4:]
+def ready_kernel(g, cell_ref, frac_ref, offset_ref, *refs):
+    far_refs, near_refs = refs[:6], refs[11:-1]
+    index_ref, weight_ref, info_ref, red_ref, table_ref = refs[6:11]
+    copies = started(far_refs, near_refs, refs[-1])
+    for copy in copies:
+        copy.wait()
+    dest_ref, count_ref = near_refs[:2]
+    write_table(g, near_refs[2:], table_ref)
+    plane_iota, sky_iota = row_iotas(g.cols)
+    lane = lax.broadcasted_iota(jnp.int32, (SUB, g.block), 1)
+    for k in range(g.blocks):
+        offset = jnp.broadcast_to(offset_ref[k : k + 1, :], (SUB, g.block))
+        live = lane < count_ref[k]
+        info_ref[k : k + 1, :] = jnp.full((1, g.deep), dest_ref[k], jnp.int32)
+        red = red_of(g, block_rows(cell_ref, 0, k, g.block), offset)
+        sky = block_rows(cell_ref, 1, k, g.block)
+        sky_next = jnp.where(sky + 1 == g.sky_wrap, 0, sky + 1)
+        deep = block_rows(cell_ref, 2, k, g.block)
+        frac_los = block_rows(frac_ref, 0, k, g.block)
+        frac_sky = block_rows(frac_ref, 1, k, g.block)
+        at_sky, at_next = (sky_iota == sky) & live, (sky_iota == sky_next) & live
+        on_sky = jnp.where(at_sky, 1.0 - frac_sky, jnp.where(at_next, frac_sky, 0.0))
+        slope_sky = jnp.where(at_next, 1.0, 0.0) - jnp.where(at_sky, 1.0, 0.0)
+        frac_deep = block_rows(frac_ref, 2, k, g.block)
+        deep_next = jnp.where(deep + 1 == g.deep, 0, deep + 1)
+        tiles = [on_sky, slope_sky, frac_deep]
+        for i in range(g.tiles):
+            plane = plane_iota + i * g.planes_per_tile - red
+            tiles.append(jnp.where(plane == 0, 1.0 - frac_los, jnp.where(plane == 1, frac_los, 0.0)))
+            tiles.append(jnp.where(plane == 1, 1.0, jnp.where(plane == 0, -1.0, 0.0)))
+        index_ref[k, 0] = deep
+        index_ref[k, 1] = deep_next
+        if g.twice:
+            first, top = plane_iota == 0, red == g.slab_rows - 1
+            slope_top = jnp.where(top, jnp.where(first, 1.0 - frac_deep, frac_deep), 0.0)
+            tiles.append(frac_los * slope_top)
+            tiles.append(jnp.where(top, jnp.where(first, -frac_los, frac_los), 0.0))
+            tiles.append(slope_top)
+            index_ref[k, 2] = jnp.where(first, deep, deep_next)
+        for j, tile in enumerate(tiles):
+            weight_ref[k, j] = tile
+        red_ref[k : k + 1, :] = red[0:1]
+
+
+def crossed(mask, first, second, distance):
+    return jnp.where(mask, first, second) + pltpu.roll(jnp.where(mask, second, first), distance, 0)
+
+
+def pull_kernel(g, info_ref, index_ref, weight_ref, red_ref, *refs):
+    field_refs, (pos_ref, vel_ref, whole_ref, top_ref, rate_ref, own_rate_ref) = refs[:-6], refs[-6:]
     me = lax.axis_index("los")
     tall = g.column + SUB
     for near in range(g.plane):
@@ -182,48 +234,47 @@
             at = pl.ds(pl.multiple_of(slab * g.slab, SUB), g.slab)
             start = base + far * g.slab
             whole_ref[at, :] = ref[start : start + g.slab, :]
+            if g.twice:
+                under = pl.multiple_of(lax.rem(slab + g.slabs - 1, g.slabs) * SUB, SUB)
+                rows = ref[start : start + g.cols, :]
+                top_ref[pl.ds(under, SUB), :] = jnp.concatenate([rows, rows], axis=0)
             start = base + g.column + far
             rate_ref[pl.ds(slab, 1), :] = ref[start : start + 1, :]
     spill = g.window - g.slab
     whole_ref[g.slabs * g.slab :, :] = whole_ref[:spill, :]
-    plane_iota, sky_iota = row_iotas(g.cols)
+    sub = lax.broadcasted_iota(jnp.int32, (SUB, g.block), 0)
+    in_even, in_first = sub % 2 == 0, sub % 4 < 2
     for k in range(g.blocks):
-        slab = dest_of(dest_ref, k)
-        red = block_rows(place_ref, 0, k, g.block)
-        sky = block_rows(place_ref, 1, k, g.block)
-        sky_next = jnp.where(sky + 1 == g.sky_wrap, 0, sky + 1)
-        deep = block_rows(place_ref, 2, k, g.block)
-        live = deep[0:1] >= 0
-        deep = jnp.maximum(deep, 0)
-        deep_next = jnp.where(deep + 1 == g.deep, 0, deep + 1)
-        frac_los = block_rows(frac_ref, 0, k, g.block)
-        frac_sky = block_rows(frac_ref, 1, k, g.block)
-        frac_deep = block_rows(frac_ref, 2, k, g.block)
-        at_sky, at_next = sky_iota == sky, sky_iota == sky_next
-        on_sky = jnp.where(at_sky, 1.0 - frac_sky, jnp.where(at_next, frac_sky, 0.0))
-        slope_sky = jnp.where(at_next, 1.0, 0.0) - jnp.where(at_sky, 1.0, 0.0)
+        slab = dest_of(info_ref, k)
+        deep, deep_next = index_ref[k, 0], index_ref[k, 1]
+        on_sky, slope_sky, frac_deep = weight_ref[k, 0], weight_ref[k, 1], weight_ref[k, 2]
         sum_val, sum_los, sum_deep = 0.0, 0.0, 0.0
-        for i in range(g.window // SUB):
+        for i in range(g.tiles):
             at = pl.ds(pl.multiple_of(slab * g.slab, SUB) + i * SUB, SUB)
             rows = whole_ref[at, :]
             below = picked(rows, deep)
             step = picked(rows, deep_next) - below
             value = below + frac_deep * step
-            plane = plane_iota + i * g.planes_per_tile - red
-            at_plane, at_above = plane == 0, plane == 1
-            on_los = jnp.where(at_plane, 1.0 - frac_los, jnp.where(at_above, frac_los, 0.0))
+            on_los, slope_los = weight_ref[k, 3 + 2 * i], weight_ref[k, 4 + 2 * i]
             sum_val += on_los * value
             sum_deep += on_los * step
-            sum_los += jnp.where(at_above, value, jnp.where(at_plane, -value, 0.0))
+            sum_los += slope_los * value
+        if g.twice:
+            rows = picked(top_ref[pl.ds(pl.multiple_of(slab * SUB, SUB), SUB), :], index_ref[k, 2])
+            sum_val += weight_ref[k, 3 + 2 * g.tiles] * rows
+            sum_deep += weight_ref[k, 4 + 2 * g.tiles] * rows
+            sum_los += weight_ref[k, 5 + 2 * g.tiles] * rows
         lanes = slice(k * g.block, (k + 1) * g.block)
-        rate = picked(jnp.broadcast_to(rate_ref[pl.ds(slab, 1), :], (SUB, g.deep)), red)
-        grad_los = jnp.where(live, jnp.sum(on_sky * sum_los, axis=0, keepdims=True), 0.0)
-        grad_sky = jnp.where(live, jnp.sum(slope_sky * sum_val, axis=0, keepdims=True), 0.0)
-        grad_deep = jnp.where(live, jnp.sum(on_sky * sum_deep, axis=0, keepdims=True), 0.0)
-        pos_ref[0:1, lanes] = grad_los
-        pos_ref[1:2, lanes] = grad_sky
-        pos_ref[2:3, lanes] = grad_deep
-        vel_ref[k : k + 1, :] = rate[0:1] * grad_los
+        own_rate_ref[k : k + 1, :] = rate_ref[pl.ds(slab, 1), :]
+        pair = crossed(in_even, on_sky * sum_los, slope_sky * sum_val, 1)
+        other = on_sky * sum_deep
+        four = crossed(in_first, pair, other + pltpu.roll(other, 1, 0), 2)
+        grads = four + pltpu.roll(four, 4, 0)
+        pos_ref[:, lanes] = grads[:3]
+        vel_ref[k : k + 1, :] = grads[0:1]
+    for k in range(0, g.blocks, SUB):
+        rows = slice(k, k + SUB)
+        vel_ref[rows, :] = vel_ref[rows, :] * picked(own_rate_ref[rows, :], red_ref[rows, :])
 
 
 class Geometry:
@@ -236,11 +287,15 @@
         need = self.width + (sky_parts > 1)
         self.cols = next(c for c in (1, 2, 4, 8) if c >= need and c * self.slab_rows % SUB == 0)
         self.planes_per_tile = SUB // self.cols
+        self.cell_type = jnp.bfloat16 if self.deep <= 256 else jnp.float32
         self.slab = self.slab_rows * self.cols
         self.plane = 8
         self.planes = slabs // self.plane
         self.column = self.planes * self.slab
         self.window = rounded_up(self.slab + self.cols, SUB)
+
+        self.twice = self.planes_per_tile == 2 and self.slab % SUB == 0
+        self.tiles = (self.slab if self.twice else self.window) // SUB
 
     def far_peer(self, far, m):
         even = self.planes & (self.planes - 1) == 0
@@ -278,56 +333,71 @@
     def to_near(block, near):
         return lax.ppermute(block, "los", [(i ^ near, i) for i in range(g.slabs)])
 
+    def spread(move, blocks):
+        return [move(block, j) for j, block in enumerate(blocks, 1)]
+
     def from_far(block, m):
         rest = [(i // g.plane, i % g.plane) for i in range(g.slabs)]
         route = [(g.far_peer(far, m) * g.plane + near, far * g.plane + near) for far, near in rest]
         return lax.ppermute(block, "los", route)
 
-    given = (
-        block_dest,
-        block_count,
-        part_cell,
-        part_frac,
-        offsets,
-        selection,
-        galaxy_counts,
-        bias_exp,
-        rsd_factor,
-    )
-    place, frac, dest, table = pl.pallas_call(
-        functools.partial(fetch_kernel, g),
+    def held(*arrays):
+        return [pltpu.with_memory_space_constraint(x, pltpu.HBM) for x in arrays]
+
+    far = pl.BlockSpec(memory_space=pltpu.HBM)
+    scalars = [
+        pltpu.SMEM(block_dest.shape, jnp.int32),
+        pltpu.SMEM(block_count.shape, jnp.int32),
+    ]
+    cell, frac, offset, keep, send = pl.pallas_call(
+        functools.partial(paint_kernel, g),
         out_shape=(
             pltpu.VMEM(part_cell.shape, jnp.int32),
             pltpu.VMEM(part_frac.shape, f32),
+            pltpu.VMEM(offsets.shape, jnp.int32),
+            pltpu.VMEM((size // 2, g.deep), f32),
+            pltpu.VMEM((size // 2, g.deep), f32),
+        ),
+        in_specs=[far] * 5,
+        out_specs=(vmem,) * 5,
+        scratch_shapes=[
+            *scalars,
+            pltpu.VMEM((padded, g.deep), f32),
+            pltpu.VMEM((padded, g.deep), f32),
+            pltpu.SemaphoreType.DMA((5,)),
+        ],
+        compiler_params=small,
+        name="paint",
+    )(*held(block_dest, block_count, part_cell, part_frac, offsets))
+    tiles = (g.blocks, 3 + 2 * g.tiles + 3 * g.twice, SUB, g.block)
+    index, weight, info, red, table = pl.pallas_call(
+        functools.partial(ready_kernel, g),
+        out_shape=(
+            pltpu.VMEM((g.blocks, 3, SUB, g.block), jnp.int32),
+            pltpu.VMEM(tiles, f32),
             pltpu.VMEM((g.blocks, g.deep), jnp.int32),
+            pltpu.VMEM((g.blocks, g.block), jnp.int32),
             pltpu.VMEM((2 * g.slab + SUB, g.deep), f32),
         ),
-        in_specs=[pl.BlockSpec(memory_space=pltpu.HBM)] * len(given),
-        out_specs=(vmem,) * 4,
+        in_specs=[vmem] * 3 + [far] * 6,
+        out_specs=(vmem,) * 5,
         scratch_shapes=[
-            pltpu.SMEM(block_dest.shape, jnp.int32),
-            pltpu.SMEM(block_count.shape, jnp.int32),
-            pltpu.VMEM(part_cell.shape, jnp.int32),
-            pltpu.VMEM(offsets.shape, jnp.int32),
+            *scalars,
             pltpu.VMEM(selection.shape, f32),
             pltpu.VMEM(galaxy_counts.shape, jnp.int32),
             pltpu.SMEM(bias_exp.shape, f32),
             pltpu.SMEM(rsd_factor.shape, f32),
-            pltpu.SemaphoreType.DMA((len(given),)),
+            pltpu.SemaphoreType.DMA((6,)),
         ],
         compiler_params=small,
-        name="fetch",
-    )(*(pltpu.with_memory_space_constraint(x, pltpu.HBM) for x in given))
-    keep, send = pl.pallas_call(
-        functools.partial(paint_kernel, g),
-        out_shape=(tiled(size // 2), tiled(size // 2)),
-        in_specs=[vmem] * 3,
-        out_specs=(vmem, vmem),
-        scratch_shapes=[pltpu.VMEM((padded, g.deep), f32), pltpu.VMEM((padded, g.deep), f32)],
-        compiler_params=small,
-        cost_estimate=pl.CostEstimate(flops=10**9, bytes_accessed=10**7, transcendentals=0),
-        name="paint",
-    )(place, frac, dest)
+        cost_estimate=pl.CostEstimate(flops=10**6, bytes_accessed=4 * 10**6, transcendentals=0),
+        name="ready",
+    )(
+        cell,
+        frac,
+        offset,
+        *held(block_dest, block_count, selection, galaxy_counts, bias_exp, rsd_factor),
+    )
     quarters = g.plane // 2
     pair = (keep + to_near(send, 1)).reshape(quarters, g.column, g.deep)
     column = pl.pallas_call(
@@ -337,8 +407,8 @@
         out_specs=vmem,
         compiler_params=small,
         name="column",
-    )(pair[0], *(to_near(pair[j], 2 * j) for j in range(1, quarters)), table)
-    parts = [column] + [from_far(column, m) for m in range(1, g.planes)]
+    )(pair[0], *spread(lambda block, j: to_near(block, 2 * j), list(pair[1:])), table)
+    parts = [column] + spread(from_far, [column] * (g.planes - 1))
     tall = g.column + SUB
     if sky_parts == 1:
         field = pl.pallas_call(
@@ -378,7 +448,7 @@
         out_specs=vmem,
         compiler_params=small,
         name="joined",
-    )(field, *(to_near(field, 2 * j) for j in range(1, quarters)))
+    )(field, *spread(lambda block, j: to_near(block, 2 * j), [field] * (quarters - 1)))
     fields = [even, to_near(even, 1)]
     grad_pos, grad_vel = pl.pallas_call(
         functools.partial(pull_kernel, g),
@@ -386,12 +456,17 @@
             jax.ShapeDtypeStruct(part_frac.shape, f32),
             jax.ShapeDtypeStruct((g.blocks, g.block), f32),
         ),
-        in_specs=[vmem] * 5,
+        in_specs=[vmem] * 6,
         out_specs=(vmem, vmem),
-        scratch_shapes=[pltpu.VMEM((padded, g.deep), f32), pltpu.VMEM((g.slabs, g.deep), f32)],
+        scratch_shapes=[
+            pltpu.VMEM((padded, g.deep), f32),
+            pltpu.VMEM((g.slabs * SUB, g.deep), f32),
+            pltpu.VMEM((g.slabs, g.deep), f32),
+            pltpu.VMEM((g.blocks, g.deep), f32),
+        ],
         compiler_params=small,
         name="pull",
-    )(place, frac, dest, *fields)
+    )(info, index, weight, red, *fields)
     return grad_pos, grad_vel.reshape(-1)
 
 

time: 30.4 us -> 30.1 us (level)
  waiting for transfers between devices: 12.8 us -> 11.8 us
  Pallas kernels: 3.57 us -> 4.27 us
    ppermute x8, waiting for transfers between devices: 8.59 us -> 7.52 us  [to_near(): return lax.ppermute(block, 'los', [(i ^ near, i) for i in range(g.slabs)])]
    pallas_call x2, Pallas kernels: 2.07 us -> 2.97 us  [the longest x1 1.91 us: on_device(): pl.pallas_call(functools.partial(paint_kernel, g), out_shape=(pltpu.VMEM(...]
  transfers between devices with their start and end apart: 11 -> 11, of which waited for: 10 -> 10; matrix products, arithmetic and copies ran while one was open for 0% -> 0% of each run, Pallas kernels for 0% -> 4%
where the time goes in v4:
time: 30.1 us; the launch traced here: 29.9 us
  starting transfers between devices  13.1 us (44%)
  waiting for transfers between devices  11.8 us (39%)
  Pallas kernels  4.27 us (14%)
  between operations  0.69 us (2%)
    ppermute x8, starting transfers between devices, to_near(): return lax.ppermute(block, 'los', [(i ^ near, i) for i in range(g.slabs)])  8.65 us
    ppermute x8, waiting for transfers between devices, to_near(): return lax.ppermute(block, 'los', [(i ^ near, i) for i in range(g.slabs)])  7.52 us
    ppermute x3, starting transfers between devices, from_far(): return lax.ppermute(block, 'los', route)  4.45 us
    ppermute x3, waiting for transfers between devices, from_far(): return lax.ppermute(block, 'los', route)  4.25 us
    pallas_call x1, Pallas kernels, on_device(): pl.pallas_call(functools.partial(paint_kernel, g), out_shape=(pltpu.VMEM(...  1.91 us
    pallas_call x1, Pallas kernels, on_device(): pl.pallas_call(functools.partial(pull_kernel, g), out_shape=(jax.ShapeDty...  1.18 us
    pallas_call x1, Pallas kernels, on_device(): pl.pallas_call(functools.partial(ready_kernel, g), out_shape=(pltpu.VMEM(...  1.06 us
  transfers between devices with their start and end apart: 11, of which 10 were waited for; matrix products, arithmetic and copies ran while one was open for 0% of the time, Pallas kernels for 4%

profile of v4, /device:TPU:0, one launch (start us, length us, event | category | flops | bytes accessed | tf_op | source)
XLA Modules:
  0.0 29.9 jit_solution(842788762274140508)
XLA Ops:
  0.6 1.9 %paint.1 = (s32[3,4096]{1,0:T(4,128)S(1)}, f32[3,4096]{1,0:T(4,128)S(1)}, s32[32,128]{1,0:T(8,128)S(1)}, f32[256,128]{1,0:T(8,128)S(1)}, f32[256,128]{1,0:T(8,128)S(1)}) custom-call(s32[32]{0:T(128)} %refs_0_.3, s32[32]{0:T(128)} %refs_1_.3, s32[3,4096]{1,0:T(4,128)} %refs_2_.2, f32[3,4096]{1,0:T(4,128)} %refs_3_.2, s32[32,128]{1,0:T(8,128)} %bitcast.2), custom_call_target="tpu_custom_call" | custom-call | tf_op jit(solution)/shard_map/paint/pallas_call | solution.py:352
  2.5 0.5 %collective-permute-start = (f32[256,128]{1,0:T(8,128)S(1)}, f32[256,128]{1,0:T(8,128)S(1)}, u32[]{:S(2)}, u32[]{:S(2)}) collective-permute-start(f32[256,128]{1,0:T(8,128)S(1)} %get-tuple-element.22), channel_id=1, source_target_pairs={{1,0},{0,1},{3,2},{2,3},{5,4},{4,5},{7,6},{6,7},{9,8},{8,9},{11,10... | collective-permute-start | bytes 393224 | tf_op jit(solution)/shard_map/ppermute | solution.py:334
  3.1 1.0 %collective-permute-done = f32[256,128]{1,0:T(8,128)S(1)} collective-permute-done((f32[256,128]{1,0:T(8,128)S(1)}, f32[256,128]{1,0:T(8,128)S(1)}, u32[]{:S(2)}, u32[]{:S(2)}) %collective-permute-start) | collective-permute-done | bytes 131104 | tf_op jit(solution)/shard_map/ppermute | solution.py:334
  4.1 3.9 %collective-permute-start.3 = (f32[64,128]{1,0:T(8,128)S(1)}, f32[64,128]{1,0:T(8,128)S(1)}, u32[]{:S(2)}, u32[]{:S(2)}) collective-permute-start(f32[64,128]{1,0:T(8,128)S(1)} %get-tuple-element.26), channel_id=1, source_target_pairs={{6,0},{7,1},{4,2},{5,3},{2,4},{3,5},{0,6},{1,7},{14,8},{15,9},{12,... | collective-permute-start | bytes 98312 | tf_op jit(solution)/shard_map/ppermute | solution.py:334
  8.0 0.5 %collective-permute-start.2 = (f32[64,128]{1,0:T(8,128)S(1)}, f32[64,128]{1,0:T(8,128)S(1)}, u32[]{:S(2)}, u32[]{:S(2)}) collective-permute-start(f32[64,128]{1,0:T(8,128)S(1)} %get-tuple-element.27), channel_id=1, source_target_pairs={{4,0},{5,1},{6,2},{7,3},{0,4},{1,5},{2,6},{3,7},{12,8},{13,9},{14,... | collective-permute-start | bytes 98312 | tf_op jit(solution)/shard_map/ppermute | solution.py:334
  8.5 0.1 collective-permute-start.1
  8.6 1.1 %ready.1 = (s32[32,3,8,128]{3,2,1,0:T(8,128)S(1)}, f32[32,10,8,128]{3,2,1,0:T(8,128)S(1)}, s32[32,128]{1,0:T(8,128)S(1)}, s32[32,128]{1,0:T(8,128)S(1)}, f32[40,128]{1,0:T(8,128)S(1)}) custom-call(s32[3,4096]{1,0:T(4,128)S(1)} %get-tuple-element.14.cell_ref, f32[3,4096]{1,0:T(4,128)S(1)} %get-tuple-element.15.frac_ref, ...), custom_call_target="tpu_custom_call" | custom-call | flops 1000000 | bytes 4000000 | tf_op jit(solution)/shard_map/ready/pallas_call | solution.py:373
  9.7 0.2 collective-permute-done.3.refs_2_
  9.8 2.0 %collective-permute-done.2.refs_1_ = f32[64,128]{1,0:T(8,128)S(1)} collective-permute-done((f32[64,128]{1,0:T(8,128)S(1)}, f32[64,128]{1,0:T(8,128)S(1)}, u32[]{:S(2)}, u32[]{:S(2)}) %collective-permute-start.2) | collective-permute-done | bytes 32800 | tf_op jit(solution)/shard_map/ppermute | solution.py:334
  11.9 0.5 %collective-permute-done.1.refs_0_ = f32[64,128]{1,0:T(8,128)S(1)} collective-permute-done((f32[64,128]{1,0:T(8,128)S(1)}, f32[64,128]{1,0:T(8,128)S(1)}, u32[]{:S(2)}, u32[]{:S(2)}) %collective-permute-start.1) | collective-permute-done | bytes 32800 | tf_op jit(solution)/shard_map/ppermute | solution.py:334
  12.4 3.7 %collective-permute-start.6 = (f32[104,128]{1,0:T(8,128)S(1)}, f32[104,128]{1,0:T(8,128)S(1)}, u32[]{:S(2)}, u32[]{:S(2)}) collective-permute-start(f32[104,128]{1,0:T(8,128)S(1)} %column.1.refs_0_), channel_id=1, source_target_pairs={{24,0},{25,1},{26,2},{27,3},{28,4},{29,5},{30,6},{31,7},{16,8},{17... | collective-permute-start | bytes 159752 | tf_op jit(solution)/shard_map/ppermute | solution.py:342
  16.1 0.0 collective-permute-start.5
  16.1 0.8 %collective-permute-start.4 = (f32[104,128]{1,0:T(8,128)S(1)}, f32[104,128]{1,0:T(8,128)S(1)}, u32[]{:S(2)}, u32[]{:S(2)}) collective-permute-start(f32[104,128]{1,0:T(8,128)S(1)} %column.1.refs_0_), channel_id=1, source_target_pairs={{8,0},{9,1},{10,2},{11,3},{12,4},{13,5},{14,6},{15,7},{0,8},{1,9},... | collective-permute-start | bytes 159752 | tf_op jit(solution)/shard_map/ppermute | solution.py:342
  16.8 1.6 %collective-permute-done.6.refs_3_ = f32[104,128]{1,0:T(8,128)S(1)} collective-permute-done((f32[104,128]{1,0:T(8,128)S(1)}, f32[104,128]{1,0:T(8,128)S(1)}, u32[]{:S(2)}, u32[]{:S(2)}) %collective-permute-start.6) | collective-permute-done | bytes 53280 | tf_op jit(solution)/shard_map/ppermute | solution.py:342
  18.5 2.6 %collective-permute-done.5.refs_2_ = f32[104,128]{1,0:T(8,128)S(1)} collective-permute-done((f32[104,128]{1,0:T(8,128)S(1)}, f32[104,128]{1,0:T(8,128)S(1)}, u32[]{:S(2)}, u32[]{:S(2)}) %collective-permute-start.5) | collective-permute-done | bytes 53280 | tf_op jit(solution)/shard_map/ppermute | solution.py:342
  21.1 0.0 collective-permute-done.4.refs_1_
  21.1 0.1 field.1.refs_0_
  21.2 1.6 %collective-permute-start.9 = (f32[72,128]{1,0:T(8,128)S(1)}, f32[72,128]{1,0:T(8,128)S(1)}, u32[]{:S(2)}, u32[]{:S(2)}) collective-permute-start(f32[72,128]{1,0:T(8,128)S(1)} %field.1.refs_0_), channel_id=1, source_target_pairs={{6,0},{7,1},{4,2},{5,3},{2,4},{3,5},{0,6},{1,7},{14,8},{15,9},{12,... | collective-permute-start | bytes 110600 | tf_op jit(solution)/shard_map/ppermute | solution.py:334
  22.8 0.5 %collective-permute-start.8 = (f32[72,128]{1,0:T(8,128)S(1)}, f32[72,128]{1,0:T(8,128)S(1)}, u32[]{:S(2)}, u32[]{:S(2)}) collective-permute-start(f32[72,128]{1,0:T(8,128)S(1)} %field.1.refs_0_), channel_id=1, source_target_pairs={{4,0},{5,1},{6,2},{7,3},{0,4},{1,5},{2,6},{3,7},{12,8},{13,9},{14,... | collective-permute-start | bytes 110600 | tf_op jit(solution)/shard_map/ppermute | solution.py:334
  23.3 1.5 %collective-permute-start.7 = (f32[72,128]{1,0:T(8,128)S(1)}, f32[72,128]{1,0:T(8,128)S(1)}, u32[]{:S(2)}, u32[]{:S(2)}) collective-permute-start(f32[72,128]{1,0:T(8,128)S(1)} %field.1.refs_0_), channel_id=1, source_target_pairs={{2,0},{3,1},{0,2},{1,3},{6,4},{7,5},{4,6},{5,7},{10,8},{11,9},{8,1... | collective-permute-start | bytes 110600 | tf_op jit(solution)/shard_map/ppermute | solution.py:334
  24.8 1.4 %collective-permute-done.9.refs_3_ = f32[72,128]{1,0:T(8,128)S(1)} collective-permute-done((f32[72,128]{1,0:T(8,128)S(1)}, f32[72,128]{1,0:T(8,128)S(1)}, u32[]{:S(2)}, u32[]{:S(2)}) %collective-permute-start.9) | collective-permute-done | bytes 36896 | tf_op jit(solution)/shard_map/ppermute | solution.py:334
  26.1 0.6 %collective-permute-done.8.refs_2_ = f32[72,128]{1,0:T(8,128)S(1)} collective-permute-done((f32[72,128]{1,0:T(8,128)S(1)}, f32[72,128]{1,0:T(8,128)S(1)}, u32[]{:S(2)}, u32[]{:S(2)}) %collective-permute-start.8) | collective-permute-done | bytes 36896 | tf_op jit(solution)/shard_map/ppermute | solution.py:334
  26.7 0.5 %collective-permute-done.7.refs_1_ = f32[72,128]{1,0:T(8,128)S(1)} collective-permute-done((f32[72,128]{1,0:T(8,128)S(1)}, f32[72,128]{1,0:T(8,128)S(1)}, u32[]{:S(2)}, u32[]{:S(2)}) %collective-permute-start.7) | collective-permute-done | bytes 36896 | tf_op jit(solution)/shard_map/ppermute | solution.py:334
  27.2 0.1 collective-permute-start.10
  27.3 1.4 %collective-permute-done.10.refs_1_ = f32[288,128]{1,0:T(8,128)S(1)} collective-permute-done((f32[288,128]{1,0:T(8,128)S(1)}, f32[288,128]{1,0:T(8,128)S(1)}, u32[]{:S(2)}, u32[]{:S(2)}) %collective-permute-start.10) | collective-permute-done | bytes 147488 | tf_op jit(solution)/shard_map/ppermute | solution.py:334
  28.7 1.2 %pull.1 = (f32[3,4096]{1,0:T(4,128)}, f32[32,128]{1,0:T(8,128)}) custom-call(s32[32,128]{1,0:T(8,128)S(1)} %get-tuple-element.17.info_ref, s32[32,3,8,128]{3,2,1,0:T(8,128)S(1)} %get-tuple-element.18.index_ref, f32[32,10,8,128]{3,2,1,0:T(8,128)S(1)} %get-tuple-element.19.weight_ref, s32[32,128]{1,0:T(8,128)S(1)} %get-tuple-element.20.red_ref, ...), custom_call_target="tpu_custom_call" | custom-call | tf_op jit(solution)/shard_map/pull/pallas_call | solution.py:453
  (4 shorter events, 0.0 us)
Async XLA Ops:
  2.5 1.5 %collective-permute-start = (f32[256,128]{1,0:T(8,128)S(1)}, f32[256,128]{1,0:T(8,128)S(1)}, u32[]{:S(2)}, u32[]{:S(2)}) collective-permute-start(f32[256,128]{1,0:T(8,128)S(1)} %get-tuple-element.22), channel_id=1, source_target_pairs={{1,0},{0,1},{3,2},{2,3},{5,4},{4,5},{7,6},{6,7},{9,8},{8,9},{11,10... | collective-permute-start | bytes 393224 | tf_op jit(solution)/shard_map/ppermute | solution.py:334
  4.1 5.8 %collective-permute-start.3 = (f32[64,128]{1,0:T(8,128)S(1)}, f32[64,128]{1,0:T(8,128)S(1)}, u32[]{:S(2)}, u32[]{:S(2)}) collective-permute-start(f32[64,128]{1,0:T(8,128)S(1)} %get-tuple-element.26), channel_id=1, source_target_pairs={{6,0},{7,1},{4,2},{5,3},{2,4},{3,5},{0,6},{1,7},{14,8},{15,9},{12,... | collective-permute-start | bytes 98312 | tf_op jit(solution)/shard_map/ppermute | solution.py:334
  8.0 3.9 %collective-permute-start.2 = (f32[64,128]{1,0:T(8,128)S(1)}, f32[64,128]{1,0:T(8,128)S(1)}, u32[]{:S(2)}, u32[]{:S(2)}) collective-permute-start(f32[64,128]{1,0:T(8,128)S(1)} %get-tuple-element.27), channel_id=1, source_target_pairs={{4,0},{5,1},{6,2},{7,3},{0,4},{1,5},{2,6},{3,7},{12,8},{13,9},{14,... | collective-permute-start | bytes 98312 | tf_op jit(solution)/shard_map/ppermute | solution.py:334
  8.5 3.9 %collective-permute-start.1 = (f32[64,128]{1,0:T(8,128)S(1)}, f32[64,128]{1,0:T(8,128)S(1)}, u32[]{:S(2)}, u32[]{:S(2)}) collective-permute-start(f32[64,128]{1,0:T(8,128)S(1)} %get-tuple-element.28), channel_id=1, source_target_pairs={{2,0},{3,1},{0,2},{1,3},{6,4},{7,5},{4,6},{5,7},{10,8},{11,9},{8,1... | collective-permute-start | bytes 98312 | tf_op jit(solution)/shard_map/ppermute | solution.py:334
  12.4 6.1 %collective-permute-start.6 = (f32[104,128]{1,0:T(8,128)S(1)}, f32[104,128]{1,0:T(8,128)S(1)}, u32[]{:S(2)}, u32[]{:S(2)}) collective-permute-start(f32[104,128]{1,0:T(8,128)S(1)} %column.1.refs_0_), channel_id=1, source_target_pairs={{24,0},{25,1},{26,2},{27,3},{28,4},{29,5},{30,6},{31,7},{16,8},{17... | collective-permute-start | bytes 159752 | tf_op jit(solution)/shard_map/ppermute | solution.py:342
  16.1 5.0 %collective-permute-start.5 = (f32[104,128]{1,0:T(8,128)S(1)}, f32[104,128]{1,0:T(8,128)S(1)}, u32[]{:S(2)}, u32[]{:S(2)}) collective-permute-start(f32[104,128]{1,0:T(8,128)S(1)} %column.1.refs_0_), channel_id=1, source_target_pairs={{16,0},{17,1},{18,2},{19,3},{20,4},{21,5},{22,6},{23,7},{24,8},{25... | collective-permute-start | bytes 159752 | tf_op jit(solution)/shard_map/ppermute | solution.py:342
  16.1 5.0 %collective-permute-start.4 = (f32[104,128]{1,0:T(8,128)S(1)}, f32[104,128]{1,0:T(8,128)S(1)}, u32[]{:S(2)}, u32[]{:S(2)}) collective-permute-start(f32[104,128]{1,0:T(8,128)S(1)} %column.1.refs_0_), channel_id=1, source_target_pairs={{8,0},{9,1},{10,2},{11,3},{12,4},{13,5},{14,6},{15,7},{0,8},{1,9},... | collective-permute-start | bytes 159752 | tf_op jit(solution)/shard_map/ppermute | solution.py:342
  21.2 4.9 %collective-permute-start.9 = (f32[72,128]{1,0:T(8,128)S(1)}, f32[72,128]{1,0:T(8,128)S(1)}, u32[]{:S(2)}, u32[]{:S(2)}) collective-permute-start(f32[72,128]{1,0:T(8,128)S(1)} %field.1.refs_0_), channel_id=1, source_target_pairs={{6,0},{7,1},{4,2},{5,3},{2,4},{3,5},{0,6},{1,7},{14,8},{15,9},{12,... | collective-permute-start | bytes 110600 | tf_op jit(solution)/shard_map/ppermute | solution.py:334
  22.8 4.0 %collective-permute-start.8 = (f32[72,128]{1,0:T(8,128)S(1)}, f32[72,128]{1,0:T(8,128)S(1)}, u32[]{:S(2)}, u32[]{:S(2)}) collective-permute-start(f32[72,128]{1,0:T(8,128)S(1)} %field.1.refs_0_), channel_id=1, source_target_pairs={{4,0},{5,1},{6,2},{7,3},{0,4},{1,5},{2,6},{3,7},{12,8},{13,9},{14,... | collective-permute-start | bytes 110600 | tf_op jit(solution)/shard_map/ppermute | solution.py:334
  23.3 4.0 %collective-permute-start.7 = (f32[72,128]{1,0:T(8,128)S(1)}, f32[72,128]{1,0:T(8,128)S(1)}, u32[]{:S(2)}, u32[]{:S(2)}) collective-permute-start(f32[72,128]{1,0:T(8,128)S(1)} %field.1.refs_0_), channel_id=1, source_target_pairs={{2,0},{3,1},{0,2},{1,3},{6,4},{7,5},{4,6},{5,7},{10,8},{11,9},{8,1... | collective-permute-start | bytes 110600 | tf_op jit(solution)/shard_map/ppermute | solution.py:334
  27.2 1.4 %collective-permute-start.10 = (f32[288,128]{1,0:T(8,128)S(1)}, f32[288,128]{1,0:T(8,128)S(1)}, u32[]{:S(2)}, u32[]{:S(2)}) collective-permute-start(f32[288,128]{1,0:T(8,128)S(1)} %joined.1.refs_0_), channel_id=1, source_target_pairs={{1,0},{0,1},{3,2},{2,3},{5,4},{4,5},{7,6},{6,7},{9,8},{8,9},{11,10... | collective-permute-start | bytes 442376 | tf_op jit(solution)/shard_map/ppermute | solution.py:334

commit v5 on v4

--- a/solution.py
+++ b/solution.py
@@ -69,16 +69,23 @@
 
 def paint_kernel(g, *refs):
     far_refs, (cell_ref, frac_ref, offset_ref, keep_ref, send_ref), refs = refs[:5], refs[5:10], refs[10:]
-    dest_ref, count_ref, low_ref, high_ref, arrived = refs
+    dest_ref, count_ref, sum_ref, turn_ref, arrived = refs
     copies = started(far_refs, (dest_ref, count_ref, cell_ref, frac_ref, offset_ref), arrived)
-    low_ref[...] = jnp.zeros_like(low_ref)
-    high_ref[...] = jnp.zeros_like(high_ref)
-    for copy in copies:
-        copy.wait()
+    sum_ref[...] = jnp.zeros_like(sum_ref)
     lane = lax.broadcasted_iota(jnp.int32, (SUB, g.block), 1)
     plane_iota, sky_iota = row_iotas(g.cols)
-    deep_iota = lax.broadcasted_iota(jnp.int32, (g.deep, g.block), 0)
-    deep_iota = deep_iota.astype(jnp.float32).astype(g.cell_type)
+    deep_iota = lax.broadcasted_iota(jnp.int32, (g.block, g.deep), 1)
+    under_iota = jnp.where(deep_iota == 0, g.deep - 1, deep_iota - 1)
+    cell_type = jnp.bfloat16 if g.deep <= 256 else jnp.float32
+    both_iota = jnp.concatenate([deep_iota, under_iota], axis=0).astype(jnp.float32).astype(cell_type)
+    one, zero = jnp.ones_like(both_iota), jnp.zeros_like(both_iota)
+    for copy in copies[2:]:
+        copy.wait()
+    for k in range(g.blocks):
+        turn_ref[k : k + 1, :] = cell_ref[2:3, k * g.block : (k + 1) * g.block].astype(jnp.float32)
+    turned = turn_ref[...].T
+    for copy in copies[:2]:
+        copy.wait()
     for k in range(g.blocks):
         offset = jnp.broadcast_to(offset_ref[k : k + 1, :], (SUB, g.block))
         red = red_of(g, block_rows(cell_ref, 0, k, g.block), offset)
@@ -100,34 +107,27 @@
             rows.append(on_los * on_sky)
         weight = jnp.concatenate(rows, axis=0)
         upper = weight * jnp.concatenate([frac_deep] * (g.window // SUB), axis=0)
-        weight = jnp.concatenate([weight - upper, upper], axis=0)
-        coarse = weight.astype(jnp.bfloat16)
-        fine = (weight - coarse.astype(jnp.float32)).astype(jnp.bfloat16)
-        deep = cell_ref[2:3, k * g.block : (k + 1) * g.block].astype(jnp.float32)
-        hit = deep_iota == jnp.broadcast_to(deep.astype(g.cell_type), (g.deep, g.block))
-        one, zero = jnp.ones_like(deep_iota), jnp.zeros_like(deep_iota)
-        hit = jnp.where(hit, one, zero).astype(jnp.bfloat16)
-        got = lax.dot_general(
-            jnp.concatenate([coarse, fine], axis=0),
-            hit,
-            (((1,), (1,)), ((), ())),
+        weight = jnp.concatenate([weight - upper, upper], axis=1)
+        coarse = weight.astype(jnp.bfloat16).astype(jnp.float32)
+        split = jnp.concatenate([coarse, weight - coarse], axis=0).astype(jnp.bfloat16)
+        deep = jnp.broadcast_to(turned[:, k : k + 1], (g.block, g.deep)).astype(cell_type)
+        hit = jnp.where(both_iota == jnp.concatenate([deep, deep], axis=0), one, zero)
+        got = jnp.dot(
+            split,
+            hit.astype(jnp.bfloat16),
             preferred_element_type=jnp.float32,
         )
-        got = got[: 2 * g.window] + got[2 * g.window :]
         at = pl.ds(pl.multiple_of(dest_ref[k] * g.slab, SUB), g.window)
-        low_ref[at, :] += got[: g.window]
-        high_ref[at, :] += got[g.window :]
+        sum_ref[at, :] += got[: g.window] + got[g.window :]
     size = g.slabs * g.slab
     spill = g.window - g.slab
-    low_ref[:spill, :] += low_ref[size:, :]
-    high_ref[:spill, :] += high_ref[size:, :]
+    sum_ref[:spill, :] += sum_ref[size:, :]
     me = lax.axis_index("los")
     for near in range(g.plane):
         for far in range(g.planes):
             at = pl.ds(pl.multiple_of(slab_at(g, me, near, far) * g.slab, SUB), g.slab)
             start = (near // 2) * g.column + far * g.slab
-            rows = low_ref[at, :] + pltpu.roll(high_ref[at, :], 1, 1)
-            (send_ref if near % 2 else keep_ref)[start : start + g.slab, :] = rows
+            (send_ref if near % 2 else keep_ref)[start : start + g.slab, :] = sum_ref[at, :]
 
 
 def cotangent_of(density, selection, counts, exponent):
@@ -287,7 +287,6 @@
         need = self.width + (sky_parts > 1)
         self.cols = next(c for c in (1, 2, 4, 8) if c >= need and c * self.slab_rows % SUB == 0)
         self.planes_per_tile = SUB // self.cols
-        self.cell_type = jnp.bfloat16 if self.deep <= 256 else jnp.float32
         self.slab = self.slab_rows * self.cols
         self.plane = 8
         self.planes = slabs // self.plane
@@ -363,7 +362,7 @@
         scratch_shapes=[
             *scalars,
             pltpu.VMEM((padded, g.deep), f32),
-            pltpu.VMEM((padded, g.deep), f32),
+            pltpu.VMEM((rounded_up(g.blocks, SUB), g.block), f32),
             pltpu.SemaphoreType.DMA((5,)),
         ],
         compiler_params=small,

time: 30.1 us -> 29.9 us (level)
  no operation moved by 1% of the time
where the time goes in v5:
time: 29.9 us; the launch traced here: 29.7 us
  starting transfers between devices  13.1 us (44%)
  waiting for transfers between devices  11.8 us (39%)
  Pallas kernels  4.15 us (14%)
  between operations  0.69 us (2%)
    ppermute x8, starting transfers between devices, to_near(): return lax.ppermute(block, 'los', [(i ^ near, i) for i in range(g.slabs)])  8.65 us
    ppermute x8, waiting for transfers between devices, to_near(): return lax.ppermute(block, 'los', [(i ^ near, i) for i in range(g.slabs)])  7.53 us
    ppermute x3, starting transfers between devices, from_far(): return lax.ppermute(block, 'los', route)  4.45 us
    ppermute x3, waiting for transfers between devices, from_far(): return lax.ppermute(block, 'los', route)  4.25 us
    pallas_call x1, Pallas kernels, on_device(): pl.pallas_call(functools.partial(paint_kernel, g), out_shape=(pltpu.VMEM(...  1.78 us
    pallas_call x1, Pallas kernels, on_device(): pl.pallas_call(functools.partial(pull_kernel, g), out_shape=(jax.ShapeDty...  1.18 us
    pallas_call x1, Pallas kernels, on_device(): pl.pallas_call(functools.partial(ready_kernel, g), out_shape=(pltpu.VMEM(...  1.06 us
  transfers between devices with their start and end apart: 11, of which 10 were waited for; matrix products, arithmetic and copies ran while one was open for 0% of the time, Pallas kernels for 4%

profile of v5, /device:TPU:0, one launch (start us, length us, event | category | flops | bytes accessed | tf_op | source)
XLA Modules:
  0.0 29.7 jit_solution(11460556054728722962)
XLA Ops:
  0.6 1.8 %paint.1 = (s32[3,4096]{1,0:T(4,128)S(1)}, f32[3,4096]{1,0:T(4,128)S(1)}, s32[32,128]{1,0:T(8,128)S(1)}, f32[256,128]{1,0:T(8,128)S(1)}, f32[256,128]{1,0:T(8,128)S(1)}) custom-call(s32[32]{0:T(128)} %refs_0_.3, s32[32]{0:T(128)} %refs_1_.3, s32[3,4096]{1,0:T(4,128)} %refs_2_.2, f32[3,4096]{1,0:T(4,128)} %refs_3_.2, s32[32,128]{1,0:T(8,128)} %bitcast.2), custom_call_target="tpu_custom_call" | custom-call | tf_op jit(solution)/shard_map/paint/pallas_call | solution.py:351
  2.4 0.5 %collective-permute-start = (f32[256,128]{1,0:T(8,128)S(1)}, f32[256,128]{1,0:T(8,128)S(1)}, u32[]{:S(2)}, u32[]{:S(2)}) collective-permute-start(f32[256,128]{1,0:T(8,128)S(1)} %get-tuple-element.22), channel_id=1, source_target_pairs={{1,0},{0,1},{3,2},{2,3},{5,4},{4,5},{7,6},{6,7},{9,8},{8,9},{11,10... | collective-permute-start | bytes 393224 | tf_op jit(solution)/shard_map/ppermute | solution.py:333
  2.9 1.0 %collective-permute-done = f32[256,128]{1,0:T(8,128)S(1)} collective-permute-done((f32[256,128]{1,0:T(8,128)S(1)}, f32[256,128]{1,0:T(8,128)S(1)}, u32[]{:S(2)}, u32[]{:S(2)}) %collective-permute-start) | collective-permute-done | bytes 131104 | tf_op jit(solution)/shard_map/ppermute | solution.py:333
  4.0 3.9 %collective-permute-start.3 = (f32[64,128]{1,0:T(8,128)S(1)}, f32[64,128]{1,0:T(8,128)S(1)}, u32[]{:S(2)}, u32[]{:S(2)}) collective-permute-start(f32[64,128]{1,0:T(8,128)S(1)} %get-tuple-element.26), channel_id=1, source_target_pairs={{6,0},{7,1},{4,2},{5,3},{2,4},{3,5},{0,6},{1,7},{14,8},{15,9},{12,... | collective-permute-start | bytes 98312 | tf_op jit(solution)/shard_map/ppermute | solution.py:333
  7.8 0.5 %collective-permute-start.2 = (f32[64,128]{1,0:T(8,128)S(1)}, f32[64,128]{1,0:T(8,128)S(1)}, u32[]{:S(2)}, u32[]{:S(2)}) collective-permute-start(f32[64,128]{1,0:T(8,128)S(1)} %get-tuple-element.27), channel_id=1, source_target_pairs={{4,0},{5,1},{6,2},{7,3},{0,4},{1,5},{2,6},{3,7},{12,8},{13,9},{14,... | collective-permute-start | bytes 98312 | tf_op jit(solution)/shard_map/ppermute | solution.py:333
  8.3 0.1 collective-permute-start.1
  8.5 1.1 %ready.1 = (s32[32,3,8,128]{3,2,1,0:T(8,128)S(1)}, f32[32,10,8,128]{3,2,1,0:T(8,128)S(1)}, s32[32,128]{1,0:T(8,128)S(1)}, s32[32,128]{1,0:T(8,128)S(1)}, f32[40,128]{1,0:T(8,128)S(1)}) custom-call(s32[3,4096]{1,0:T(4,128)S(1)} %get-tuple-element.14.cell_ref, f32[3,4096]{1,0:T(4,128)S(1)} %get-tuple-element.15.frac_ref, ...), custom_call_target="tpu_custom_call" | custom-call | flops 1000000 | bytes 4000000 | tf_op jit(solution)/shard_map/ready/pallas_call | solution.py:372
  9.5 0.2 collective-permute-done.3.refs_2_
  9.7 2.0 %collective-permute-done.2.refs_1_ = f32[64,128]{1,0:T(8,128)S(1)} collective-permute-done((f32[64,128]{1,0:T(8,128)S(1)}, f32[64,128]{1,0:T(8,128)S(1)}, u32[]{:S(2)}, u32[]{:S(2)}) %collective-permute-start.2) | collective-permute-done | bytes 32800 | tf_op jit(solution)/shard_map/ppermute | solution.py:333
  11.7 0.5 %collective-permute-done.1.refs_0_ = f32[64,128]{1,0:T(8,128)S(1)} collective-permute-done((f32[64,128]{1,0:T(8,128)S(1)}, f32[64,128]{1,0:T(8,128)S(1)}, u32[]{:S(2)}, u32[]{:S(2)}) %collective-permute-start.1) | collective-permute-done | bytes 32800 | tf_op jit(solution)/shard_map/ppermute | solution.py:333
  12.3 3.7 %collective-permute-start.6 = (f32[104,128]{1,0:T(8,128)S(1)}, f32[104,128]{1,0:T(8,128)S(1)}, u32[]{:S(2)}, u32[]{:S(2)}) collective-permute-start(f32[104,128]{1,0:T(8,128)S(1)} %column.1.refs_0_), channel_id=1, source_target_pairs={{24,0},{25,1},{26,2},{27,3},{28,4},{29,5},{30,6},{31,7},{16,8},{17... | collective-permute-start | bytes 159752 | tf_op jit(solution)/shard_map/ppermute | solution.py:341
  15.9 0.0 collective-permute-start.5
  15.9 0.8 %collective-permute-start.4 = (f32[104,128]{1,0:T(8,128)S(1)}, f32[104,128]{1,0:T(8,128)S(1)}, u32[]{:S(2)}, u32[]{:S(2)}) collective-permute-start(f32[104,128]{1,0:T(8,128)S(1)} %column.1.refs_0_), channel_id=1, source_target_pairs={{8,0},{9,1},{10,2},{11,3},{12,4},{13,5},{14,6},{15,7},{0,8},{1,9},... | collective-permute-start | bytes 159752 | tf_op jit(solution)/shard_map/ppermute | solution.py:341
  16.7 1.6 %collective-permute-done.6.refs_3_ = f32[104,128]{1,0:T(8,128)S(1)} collective-permute-done((f32[104,128]{1,0:T(8,128)S(1)}, f32[104,128]{1,0:T(8,128)S(1)}, u32[]{:S(2)}, u32[]{:S(2)}) %collective-permute-start.6) | collective-permute-done | bytes 53280 | tf_op jit(solution)/shard_map/ppermute | solution.py:341
  18.4 2.6 %collective-permute-done.5.refs_2_ = f32[104,128]{1,0:T(8,128)S(1)} collective-permute-done((f32[104,128]{1,0:T(8,128)S(1)}, f32[104,128]{1,0:T(8,128)S(1)}, u32[]{:S(2)}, u32[]{:S(2)}) %collective-permute-start.5) | collective-permute-done | bytes 53280 | tf_op jit(solution)/shard_map/ppermute | solution.py:341
  21.0 0.0 collective-permute-done.4.refs_1_
  21.0 0.1 field.1.refs_0_
  21.1 1.6 %collective-permute-start.9 = (f32[72,128]{1,0:T(8,128)S(1)}, f32[72,128]{1,0:T(8,128)S(1)}, u32[]{:S(2)}, u32[]{:S(2)}) collective-permute-start(f32[72,128]{1,0:T(8,128)S(1)} %field.1.refs_0_), channel_id=1, source_target_pairs={{6,0},{7,1},{4,2},{5,3},{2,4},{3,5},{0,6},{1,7},{14,8},{15,9},{12,... | collective-permute-start | bytes 110600 | tf_op jit(solution)/shard_map/ppermute | solution.py:333
  22.6 0.5 %collective-permute-start.8 = (f32[72,128]{1,0:T(8,128)S(1)}, f32[72,128]{1,0:T(8,128)S(1)}, u32[]{:S(2)}, u32[]{:S(2)}) collective-permute-start(f32[72,128]{1,0:T(8,128)S(1)} %field.1.refs_0_), channel_id=1, source_target_pairs={{4,0},{5,1},{6,2},{7,3},{0,4},{1,5},{2,6},{3,7},{12,8},{13,9},{14,... | collective-permute-start | bytes 110600 | tf_op jit(solution)/shard_map/ppermute | solution.py:333
  23.1 1.5 %collective-permute-start.7 = (f32[72,128]{1,0:T(8,128)S(1)}, f32[72,128]{1,0:T(8,128)S(1)}, u32[]{:S(2)}, u32[]{:S(2)}) collective-permute-start(f32[72,128]{1,0:T(8,128)S(1)} %field.1.refs_0_), channel_id=1, source_target_pairs={{2,0},{3,1},{0,2},{1,3},{6,4},{7,5},{4,6},{5,7},{10,8},{11,9},{8,1... | collective-permute-start | bytes 110600 | tf_op jit(solution)/shard_map/ppermute | solution.py:333
  24.6 1.4 %collective-permute-done.9.refs_3_ = f32[72,128]{1,0:T(8,128)S(1)} collective-permute-done((f32[72,128]{1,0:T(8,128)S(1)}, f32[72,128]{1,0:T(8,128)S(1)}, u32[]{:S(2)}, u32[]{:S(2)}) %collective-permute-start.9) | collective-permute-done | bytes 36896 | tf_op jit(solution)/shard_map/ppermute | solution.py:333
  26.0 0.6 %collective-permute-done.8.refs_2_ = f32[72,128]{1,0:T(8,128)S(1)} collective-permute-done((f32[72,128]{1,0:T(8,128)S(1)}, f32[72,128]{1,0:T(8,128)S(1)}, u32[]{:S(2)}, u32[]{:S(2)}) %collective-permute-start.8) | collective-permute-done | bytes 36896 | tf_op jit(solution)/shard_map/ppermute | solution.py:333
  26.6 0.5 %collective-permute-done.7.refs_1_ = f32[72,128]{1,0:T(8,128)S(1)} collective-permute-done((f32[72,128]{1,0:T(8,128)S(1)}, f32[72,128]{1,0:T(8,128)S(1)}, u32[]{:S(2)}, u32[]{:S(2)}) %collective-permute-start.7) | collective-permute-done | bytes 36896 | tf_op jit(solution)/shard_map/ppermute | solution.py:333
  27.1 0.1 collective-permute-start.10
  27.2 1.4 %collective-permute-done.10.refs_1_ = f32[288,128]{1,0:T(8,128)S(1)} collective-permute-done((f32[288,128]{1,0:T(8,128)S(1)}, f32[288,128]{1,0:T(8,128)S(1)}, u32[]{:S(2)}, u32[]{:S(2)}) %collective-permute-start.10) | collective-permute-done | bytes 147488 | tf_op jit(solution)/shard_map/ppermute | solution.py:333
  28.6 1.2 %pull.1 = (f32[3,4096]{1,0:T(4,128)}, f32[32,128]{1,0:T(8,128)}) custom-call(s32[32,128]{1,0:T(8,128)S(1)} %get-tuple-element.17.info_ref, s32[32,3,8,128]{3,2,1,0:T(8,128)S(1)} %get-tuple-element.18.index_ref, f32[32,10,8,128]{3,2,1,0:T(8,128)S(1)} %get-tuple-element.19.weight_ref, s32[32,128]{1,0:T(8,128)S(1)} %get-tuple-element.20.red_ref, ...), custom_call_target="tpu_custom_call" | custom-call | tf_op jit(solution)/shard_map/pull/pallas_call | solution.py:452
  (4 shorter events, 0.0 us)
Async XLA Ops:
  2.4 1.5 %collective-permute-start = (f32[256,128]{1,0:T(8,128)S(1)}, f32[256,128]{1,0:T(8,128)S(1)}, u32[]{:S(2)}, u32[]{:S(2)}) collective-permute-start(f32[256,128]{1,0:T(8,128)S(1)} %get-tuple-element.22), channel_id=1, source_target_pairs={{1,0},{0,1},{3,2},{2,3},{5,4},{4,5},{7,6},{6,7},{9,8},{8,9},{11,10... | collective-permute-start | bytes 393224 | tf_op jit(solution)/shard_map/ppermute | solution.py:333
  4.0 5.8 %collective-permute-start.3 = (f32[64,128]{1,0:T(8,128)S(1)}, f32[64,128]{1,0:T(8,128)S(1)}, u32[]{:S(2)}, u32[]{:S(2)}) collective-permute-start(f32[64,128]{1,0:T(8,128)S(1)} %get-tuple-element.26), channel_id=1, source_target_pairs={{6,0},{7,1},{4,2},{5,3},{2,4},{3,5},{0,6},{1,7},{14,8},{15,9},{12,... | collective-permute-start | bytes 98312 | tf_op jit(solution)/shard_map/ppermute | solution.py:333
  7.8 3.9 %collective-permute-start.2 = (f32[64,128]{1,0:T(8,128)S(1)}, f32[64,128]{1,0:T(8,128)S(1)}, u32[]{:S(2)}, u32[]{:S(2)}) collective-permute-start(f32[64,128]{1,0:T(8,128)S(1)} %get-tuple-element.27), channel_id=1, source_target_pairs={{4,0},{5,1},{6,2},{7,3},{0,4},{1,5},{2,6},{3,7},{12,8},{13,9},{14,... | collective-permute-start | bytes 98312 | tf_op jit(solution)/shard_map/ppermute | solution.py:333
  8.3 3.9 %collective-permute-start.1 = (f32[64,128]{1,0:T(8,128)S(1)}, f32[64,128]{1,0:T(8,128)S(1)}, u32[]{:S(2)}, u32[]{:S(2)}) collective-permute-start(f32[64,128]{1,0:T(8,128)S(1)} %get-tuple-element.28), channel_id=1, source_target_pairs={{2,0},{3,1},{0,2},{1,3},{6,4},{7,5},{4,6},{5,7},{10,8},{11,9},{8,1... | collective-permute-start | bytes 98312 | tf_op jit(solution)/shard_map/ppermute | solution.py:333
  12.3 6.1 %collective-permute-start.6 = (f32[104,128]{1,0:T(8,128)S(1)}, f32[104,128]{1,0:T(8,128)S(1)}, u32[]{:S(2)}, u32[]{:S(2)}) collective-permute-start(f32[104,128]{1,0:T(8,128)S(1)} %column.1.refs_0_), channel_id=1, source_target_pairs={{24,0},{25,1},{26,2},{27,3},{28,4},{29,5},{30,6},{31,7},{16,8},{17... | collective-permute-start | bytes 159752 | tf_op jit(solution)/shard_map/ppermute | solution.py:341
  15.9 5.0 %collective-permute-start.5 = (f32[104,128]{1,0:T(8,128)S(1)}, f32[104,128]{1,0:T(8,128)S(1)}, u32[]{:S(2)}, u32[]{:S(2)}) collective-permute-start(f32[104,128]{1,0:T(8,128)S(1)} %column.1.refs_0_), channel_id=1, source_target_pairs={{16,0},{17,1},{18,2},{19,3},{20,4},{21,5},{22,6},{23,7},{24,8},{25... | collective-permute-start | bytes 159752 | tf_op jit(solution)/shard_map/ppermute | solution.py:341
  15.9 5.0 %collective-permute-start.4 = (f32[104,128]{1,0:T(8,128)S(1)}, f32[104,128]{1,0:T(8,128)S(1)}, u32[]{:S(2)}, u32[]{:S(2)}) collective-permute-start(f32[104,128]{1,0:T(8,128)S(1)} %column.1.refs_0_), channel_id=1, source_target_pairs={{8,0},{9,1},{10,2},{11,3},{12,4},{13,5},{14,6},{15,7},{0,8},{1,9},... | collective-permute-start | bytes 159752 | tf_op jit(solution)/shard_map/ppermute | solution.py:341
  21.1 4.9 %collective-permute-start.9 = (f32[72,128]{1,0:T(8,128)S(1)}, f32[72,128]{1,0:T(8,128)S(1)}, u32[]{:S(2)}, u32[]{:S(2)}) collective-permute-start(f32[72,128]{1,0:T(8,128)S(1)} %field.1.refs_0_), channel_id=1, source_target_pairs={{6,0},{7,1},{4,2},{5,3},{2,4},{3,5},{0,6},{1,7},{14,8},{15,9},{12,... | collective-permute-start | bytes 110600 | tf_op jit(solution)/shard_map/ppermute | solution.py:333
  22.6 4.0 %collective-permute-start.8 = (f32[72,128]{1,0:T(8,128)S(1)}, f32[72,128]{1,0:T(8,128)S(1)}, u32[]{:S(2)}, u32[]{:S(2)}) collective-permute-start(f32[72,128]{1,0:T(8,128)S(1)} %field.1.refs_0_), channel_id=1, source_target_pairs={{4,0},{5,1},{6,2},{7,3},{0,4},{1,5},{2,6},{3,7},{12,8},{13,9},{14,... | collective-permute-start | bytes 110600 | tf_op jit(solution)/shard_map/ppermute | solution.py:333
  23.1 4.0 %collective-permute-start.7 = (f32[72,128]{1,0:T(8,128)S(1)}, f32[72,128]{1,0:T(8,128)S(1)}, u32[]{:S(2)}, u32[]{:S(2)}) collective-permute-start(f32[72,128]{1,0:T(8,128)S(1)} %field.1.refs_0_), channel_id=1, source_target_pairs={{2,0},{3,1},{0,2},{1,3},{6,4},{7,5},{4,6},{5,7},{10,8},{11,9},{8,1... | collective-permute-start | bytes 110600 | tf_op jit(solution)/shard_map/ppermute | solution.py:333
  27.1 1.4 %collective-permute-start.10 = (f32[288,128]{1,0:T(8,128)S(1)}, f32[288,128]{1,0:T(8,128)S(1)}, u32[]{:S(2)}, u32[]{:S(2)}) collective-permute-start(f32[288,128]{1,0:T(8,128)S(1)} %joined.1.refs_0_), channel_id=1, source_target_pairs={{1,0},{0,1},{3,2},{2,3},{5,4},{4,5},{7,6},{6,7},{9,8},{8,9},{11,10... | collective-permute-start | bytes 442376 | tf_op jit(solution)/shard_map/ppermute | solution.py:333

commit v6 on v5

--- a/solution.py
+++ b/solution.py
@@ -68,7 +68,7 @@
 
 
 def paint_kernel(g, *refs):
-    far_refs, (cell_ref, frac_ref, offset_ref, keep_ref, send_ref), refs = refs[:5], refs[5:10], refs[10:]
+    far_refs, (cell_ref, frac_ref, offset_ref), part_refs, refs = refs[:5], refs[5:8], refs[8:12], refs[12:]
     dest_ref, count_ref, sum_ref, turn_ref, arrived = refs
     copies = started(far_refs, (dest_ref, count_ref, cell_ref, frac_ref, offset_ref), arrived)
     sum_ref[...] = jnp.zeros_like(sum_ref)
@@ -126,8 +126,9 @@
     for near in range(g.plane):
         for far in range(g.planes):
             at = pl.ds(pl.multiple_of(slab_at(g, me, near, far) * g.slab, SUB), g.slab)
-            start = (near // 2) * g.column + far * g.slab
-            (send_ref if near % 2 else keep_ref)[start : start + g.slab, :] = sum_ref[at, :]
+            last = near // 2 == g.plane // 2 - 1
+            start = (0 if last else near // 2) * g.column + far * g.slab
+            part_refs[near % 2 + 2 * last][start : start + g.slab, :] = sum_ref[at, :]
 
 
 def cotangent_of(density, selection, counts, exponent):
@@ -228,7 +229,8 @@
     me = lax.axis_index("los")
     tall = g.column + SUB
     for near in range(g.plane):
-        ref, base = field_refs[near % 2], (near // 2) * tall
+        ref = field_refs[near % 2 + 2 * (near > 1)]
+        base = max(near // 2 - 1, 0) * tall
         for far in range(g.planes):
             slab = slab_at(g, me, near, far)
             at = pl.ds(pl.multiple_of(slab * g.slab, SUB), g.slab)
@@ -348,17 +350,20 @@
         pltpu.SMEM(block_dest.shape, jnp.int32),
         pltpu.SMEM(block_count.shape, jnp.int32),
     ]
-    cell, frac, offset, keep, send = pl.pallas_call(
+    rest_rows = size // 2 - g.column
+    cell, frac, offset, keep, send, keep_last, send_last = pl.pallas_call(
         functools.partial(paint_kernel, g),
         out_shape=(
             pltpu.VMEM(part_cell.shape, jnp.int32),
             pltpu.VMEM(part_frac.shape, f32),
             pltpu.VMEM(offsets.shape, jnp.int32),
-            pltpu.VMEM((size // 2, g.deep), f32),
-            pltpu.VMEM((size // 2, g.deep), f32),
+            pltpu.VMEM((rest_rows, g.deep), f32),
+            pltpu.VMEM((rest_rows, g.deep), f32),
+            pltpu.VMEM((g.column, g.deep), f32),
+            pltpu.VMEM((g.column, g.deep), f32),
         ),
         in_specs=[far] * 5,
-        out_specs=(vmem,) * 5,
+        out_specs=(vmem,) * 7,
         scratch_shapes=[
             *scalars,
             pltpu.VMEM((padded, g.deep), f32),
@@ -398,7 +403,9 @@
         *held(block_dest, block_count, selection, galaxy_counts, bias_exp, rsd_factor),
     )
     quarters = g.plane // 2
-    pair = (keep + to_near(send, 1)).reshape(quarters, g.column, g.deep)
+    last = keep_last + to_near(send_last, 1)
+    pair = (keep + to_near(send, 1)).reshape(quarters - 1, g.column, g.deep)
+    pair = [*pair, last]
     column = pl.pallas_call(
         functools.partial(column_kernel, g),
         out_shape=tiled(g.column + 2 * g.slab + SUB),
@@ -406,7 +413,7 @@
         out_specs=vmem,
         compiler_params=small,
         name="column",
-    )(pair[0], *spread(lambda block, j: to_near(block, 2 * j), list(pair[1:])), table)
+    )(pair[0], *spread(lambda block, j: to_near(block, 2 * j), pair[1:]), table)
     parts = [column] + spread(from_far, [column] * (g.planes - 1))
     tall = g.column + SUB
     if sky_parts == 1:
@@ -440,22 +447,24 @@
         inner = jnp.concatenate([inner, rim[:, :, None], rest], axis=2).reshape(g.column, g.deep)
         rates = jnp.pad(planes[:, 2 * g.slab + 1], ((0, SUB - g.planes), (0, 0)))
         field = jnp.concatenate([inner, rates])
-    even = pl.pallas_call(
+    around = spread(lambda block, j: to_near(block, 2 * j), [field] * (quarters - 1))
+    own = [field, to_near(field, 1)]
+    joined = pl.pallas_call(
         joined_kernel,
-        out_shape=tiled(quarters * tall),
-        in_specs=[vmem] * quarters,
+        out_shape=tiled((quarters - 1) * tall),
+        in_specs=[vmem] * (quarters - 1),
         out_specs=vmem,
         compiler_params=small,
         name="joined",
-    )(field, *spread(lambda block, j: to_near(block, 2 * j), [field] * (quarters - 1)))
-    fields = [even, to_near(even, 1)]
+    )(*around)
+    fields = [*own, joined, to_near(joined, 1)]
     grad_pos, grad_vel = pl.pallas_call(
         functools.partial(pull_kernel, g),
         out_shape=(
             jax.ShapeDtypeStruct(part_frac.shape, f32),
             jax.ShapeDtypeStruct((g.blocks, g.block), f32),
         ),
-        in_specs=[vmem] * 6,
+        in_specs=[vmem] * 8,
         out_specs=(vmem, vmem),
         scratch_shapes=[
             pltpu.VMEM((padded, g.deep), f32),

time: 29.9 us -> 30 us (level)
  starting transfers between devices: 13.1 us -> 13.4 us
  waiting for transfers between devices: 11.8 us -> 11.5 us
    ppermute x8 -> x10, starting transfers between devices: 8.65 us -> 9 us  [to_near(): return lax.ppermute(block, 'los', [(i ^ near, i) for i in range(g.slabs)])]
    ppermute x8 -> x10, waiting for transfers between devices: 7.53 us -> 7.21 us  [to_near(): return lax.ppermute(block, 'los', [(i ^ near, i) for i in range(g.slabs)])]
  transfers between devices with their start and end apart: 11 -> 13, of which waited for: 10 -> 10; matrix products, arithmetic and copies ran while one was open for 0% -> 0% of each run, Pallas kernels for 4% -> 4%
where the time goes in v6:
time: 30 us; the launch traced here: 29.8 us
  starting transfers between devices  13.4 us (45%)
  waiting for transfers between devices  11.5 us (38%)
  Pallas kernels  4.15 us (14%)
  between operations  0.69 us (2%)
    ppermute x10, starting transfers between devices, to_near(): return lax.ppermute(block, 'los', [(i ^ near, i) for i in range(g.slabs)])  9 us
    ppermute x10, waiting for transfers between devices, to_near(): return lax.ppermute(block, 'los', [(i ^ near, i) for i in range(g.slabs)])  7.21 us
    ppermute x3, starting transfers between devices, from_far(): return lax.ppermute(block, 'los', route)  4.45 us
    ppermute x3, waiting for transfers between devices, from_far(): return lax.ppermute(block, 'los', route)  4.25 us
    pallas_call x1, Pallas kernels, on_device(): pl.pallas_call(functools.partial(paint_kernel, g), out_shape=(pltpu.VMEM(...  1.78 us
    pallas_call x1, Pallas kernels, on_device(): pl.pallas_call(functools.partial(pull_kernel, g), out_shape=(jax.ShapeDty...  1.18 us
    pallas_call x1, Pallas kernels, on_device(): pl.pallas_call(functools.partial(ready_kernel, g), out_shape=(pltpu.VMEM(...  1.06 us
  transfers between devices with their start and end apart: 13, of which 10 were waited for; matrix products, arithmetic and copies ran while one was open for 0% of the time, Pallas kernels for 4%

profile of v6, /device:TPU:0, one launch (start us, length us, event | category | flops | bytes accessed | tf_op | source)
XLA Modules:
  0.0 29.8 jit_solution(13798911667522248215)
XLA Ops:
  0.6 1.8 %paint.1 = (s32[3,4096]{1,0:T(4,128)S(1)}, f32[3,4096]{1,0:T(4,128)S(1)}, s32[32,128]{1,0:T(8,128)S(1)}, f32[192,128]{1,0:T(8,128)S(1)}, f32[192,128]{1,0:T(8,12...) custom-call(s32[32]{0:T(128)} %refs_0_.3, s32[32]{0:T(128)} %refs_1_.3, s32[3,4096]{1,0:T(4,128)} %refs_2_.2, ...), custom_call_target="tpu_custom_call" | custom-call | tf_op jit(solution)/shard_map/paint/pallas_call | solution.py:354
  2.4 0.5 %collective-permute-start = (f32[192,128]{1,0:T(8,128)S(1)}, f32[192,128]{1,0:T(8,128)S(1)}, u32[]{:S(2)}, u32[]{:S(2)}) collective-permute-start(f32[192,128]{1,0:T(8,128)S(1)} %get-tuple-element.24), channel_id=1, source_target_pairs={{1,0},{0,1},{3,2},{2,3},{5,4},{4,5},{7,6},{6,7},{9,8},{8,9},{11,10... | collective-permute-start | bytes 294920 | tf_op jit(solution)/shard_map/ppermute | solution.py:335
  2.9 0.1 collective-permute-start.3
  3.0 1.1 %collective-permute-done.3 = f32[64,128]{1,0:T(8,128)S(1)} collective-permute-done((f32[64,128]{1,0:T(8,128)S(1)}, f32[64,128]{1,0:T(8,128)S(1)}, u32[]{:S(2)}, u32[]{:S(2)}) %collective-permute-start.3) | collective-permute-done | bytes 32800 | tf_op jit(solution)/shard_map/ppermute | solution.py:335
  4.1 3.6 %collective-permute-start.4 = (f32[64,128]{1,0:T(8,128)S(1)}, f32[64,128]{1,0:T(8,128)S(1)}, u32[]{:S(2)}, u32[]{:S(2)}) collective-permute-start(f32[64,128]{1,0:T(8,128)S(1)} %add.7), channel_id=1, source_target_pairs={{6,0},{7,1},{4,2},{5,3},{2,4},{3,5},{0,6},{1,7},{14,8},{15,9},{12,... | collective-permute-start | bytes 98312 | tf_op jit(solution)/shard_map/ppermute | solution.py:335
  7.8 0.0 collective-permute-done
  7.8 0.6 %collective-permute-start.2 = (f32[64,128]{1,0:T(8,128)S(1)}, f32[64,128]{1,0:T(8,128)S(1)}, u32[]{:S(2)}, u32[]{:S(2)}) collective-permute-start(f32[64,128]{1,0:T(8,128)S(1)} %get-tuple-element.30), channel_id=1, source_target_pairs={{4,0},{5,1},{6,2},{7,3},{0,4},{1,5},{2,6},{3,7},{12,8},{13,9},{14,... | collective-permute-start | bytes 98312 | tf_op jit(solution)/shard_map/ppermute | solution.py:335
  8.4 0.1 collective-permute-start.1
  8.5 1.1 %ready.1 = (s32[32,3,8,128]{3,2,1,0:T(8,128)S(1)}, f32[32,10,8,128]{3,2,1,0:T(8,128)S(1)}, s32[32,128]{1,0:T(8,128)S(1)}, s32[32,128]{1,0:T(8,128)S(1)}, f32[40,128]{1,0:T(8,128)S(1)}) custom-call(s32[3,4096]{1,0:T(4,128)S(1)} %get-tuple-element.16.cell_ref, f32[3,4096]{1,0:T(4,128)S(1)} %get-tuple-element.17.frac_ref, ...), custom_call_target="tpu_custom_call" | custom-call | flops 1000000 | bytes 4000000 | tf_op jit(solution)/shard_map/ready/pallas_call | solution.py:377
  9.5 0.1 collective-permute-done.4.refs_2_
  9.7 2.1 %collective-permute-done.2.refs_1_ = f32[64,128]{1,0:T(8,128)S(1)} collective-permute-done((f32[64,128]{1,0:T(8,128)S(1)}, f32[64,128]{1,0:T(8,128)S(1)}, u32[]{:S(2)}, u32[]{:S(2)}) %collective-permute-start.2) | collective-permute-done | bytes 32800 | tf_op jit(solution)/shard_map/ppermute | solution.py:335
  11.8 0.5 %collective-permute-done.1.refs_0_ = f32[64,128]{1,0:T(8,128)S(1)} collective-permute-done((f32[64,128]{1,0:T(8,128)S(1)}, f32[64,128]{1,0:T(8,128)S(1)}, u32[]{:S(2)}, u32[]{:S(2)}) %collective-permute-start.1) | collective-permute-done | bytes 32800 | tf_op jit(solution)/shard_map/ppermute | solution.py:335
  12.3 3.7 %collective-permute-start.7 = (f32[104,128]{1,0:T(8,128)S(1)}, f32[104,128]{1,0:T(8,128)S(1)}, u32[]{:S(2)}, u32[]{:S(2)}) collective-permute-start(f32[104,128]{1,0:T(8,128)S(1)} %column.1.refs_0_), channel_id=1, source_target_pairs={{24,0},{25,1},{26,2},{27,3},{28,4},{29,5},{30,6},{31,7},{16,8},{17... | collective-permute-start | bytes 159752 | tf_op jit(solution)/shard_map/ppermute | solution.py:343
  16.0 0.0 collective-permute-start.6
  16.0 0.8 %collective-permute-start.5 = (f32[104,128]{1,0:T(8,128)S(1)}, f32[104,128]{1,0:T(8,128)S(1)}, u32[]{:S(2)}, u32[]{:S(2)}) collective-permute-start(f32[104,128]{1,0:T(8,128)S(1)} %column.1.refs_0_), channel_id=1, source_target_pairs={{8,0},{9,1},{10,2},{11,3},{12,4},{13,5},{14,6},{15,7},{0,8},{1,9},... | collective-permute-start | bytes 159752 | tf_op jit(solution)/shard_map/ppermute | solution.py:343
  16.7 1.5 %collective-permute-done.7.refs_3_ = f32[104,128]{1,0:T(8,128)S(1)} collective-permute-done((f32[104,128]{1,0:T(8,128)S(1)}, f32[104,128]{1,0:T(8,128)S(1)}, u32[]{:S(2)}, u32[]{:S(2)}) %collective-permute-start.7) | collective-permute-done | bytes 53280 | tf_op jit(solution)/shard_map/ppermute | solution.py:343
  18.3 2.7 %collective-permute-done.6.refs_2_ = f32[104,128]{1,0:T(8,128)S(1)} collective-permute-done((f32[104,128]{1,0:T(8,128)S(1)}, f32[104,128]{1,0:T(8,128)S(1)}, u32[]{:S(2)}, u32[]{:S(2)}) %collective-permute-start.6) | collective-permute-done | bytes 53280 | tf_op jit(solution)/shard_map/ppermute | solution.py:343
  21.0 0.0 collective-permute-done.5.refs_1_
  21.0 0.1 field.1.refs_0_
  21.1 1.6 %collective-permute-start.11 = (f32[72,128]{1,0:T(8,128)S(1)}, f32[72,128]{1,0:T(8,128)S(1)}, u32[]{:S(2)}, u32[]{:S(2)}) collective-permute-start(f32[72,128]{1,0:T(8,128)S(1)} %field.1.refs_0_), channel_id=1, source_target_pairs={{6,0},{7,1},{4,2},{5,3},{2,4},{3,5},{0,6},{1,7},{14,8},{15,9},{12,... | collective-permute-start | bytes 110600 | tf_op jit(solution)/shard_map/ppermute | solution.py:335
  22.7 0.5 %collective-permute-start.10 = (f32[72,128]{1,0:T(8,128)S(1)}, f32[72,128]{1,0:T(8,128)S(1)}, u32[]{:S(2)}, u32[]{:S(2)}) collective-permute-start(f32[72,128]{1,0:T(8,128)S(1)} %field.1.refs_0_), channel_id=1, source_target_pairs={{4,0},{5,1},{6,2},{7,3},{0,4},{1,5},{2,6},{3,7},{12,8},{13,9},{14,... | collective-permute-start | bytes 110600 | tf_op jit(solution)/shard_map/ppermute | solution.py:335
  23.2 1.5 %collective-permute-start.9 = (f32[72,128]{1,0:T(8,128)S(1)}, f32[72,128]{1,0:T(8,128)S(1)}, u32[]{:S(2)}, u32[]{:S(2)}) collective-permute-start(f32[72,128]{1,0:T(8,128)S(1)} %field.1.refs_0_), channel_id=1, source_target_pairs={{2,0},{3,1},{0,2},{1,3},{6,4},{7,5},{4,6},{5,7},{10,8},{11,9},{8,1... | collective-permute-start | bytes 110600 | tf_op jit(solution)/shard_map/ppermute | solution.py:335
  24.7 1.4 %collective-permute-done.11.refs_2_ = f32[72,128]{1,0:T(8,128)S(1)} collective-permute-done((f32[72,128]{1,0:T(8,128)S(1)}, f32[72,128]{1,0:T(8,128)S(1)}, u32[]{:S(2)}, u32[]{:S(2)}) %collective-permute-start.11) | collective-permute-done | bytes 36896 | tf_op jit(solution)/shard_map/ppermute | solution.py:335
  26.0 0.6 %collective-permute-done.10.refs_1_ = f32[72,128]{1,0:T(8,128)S(1)} collective-permute-done((f32[72,128]{1,0:T(8,128)S(1)}, f32[72,128]{1,0:T(8,128)S(1)}, u32[]{:S(2)}, u32[]{:S(2)}) %collective-permute-start.10) | collective-permute-done | bytes 36896 | tf_op jit(solution)/shard_map/ppermute | solution.py:335
  26.6 0.5 %collective-permute-done.9.refs_0_ = f32[72,128]{1,0:T(8,128)S(1)} collective-permute-done((f32[72,128]{1,0:T(8,128)S(1)}, f32[72,128]{1,0:T(8,128)S(1)}, u32[]{:S(2)}, u32[]{:S(2)}) %collective-permute-start.9) | collective-permute-done | bytes 36896 | tf_op jit(solution)/shard_map/ppermute | solution.py:335
  27.1 0.1 collective-permute-start.12
  27.2 0.5 %collective-permute-start.8 = (f32[72,128]{1,0:T(8,128)S(1)}, f32[72,128]{1,0:T(8,128)S(1)}, u32[]{:S(2)}, u32[]{:S(2)}) collective-permute-start(f32[72,128]{1,0:T(8,128)S(1)} %field.1.refs_0_), channel_id=1, source_target_pairs={{1,0},{0,1},{3,2},{2,3},{5,4},{4,5},{7,6},{6,7},{9,8},{8,9},{11,10... | collective-permute-start | bytes 110600 | tf_op jit(solution)/shard_map/ppermute | solution.py:335
  27.7 0.9 %collective-permute-done.8.refs_1_ = f32[72,128]{1,0:T(8,128)S(1)} collective-permute-done((f32[72,128]{1,0:T(8,128)S(1)}, f32[72,128]{1,0:T(8,128)S(1)}, u32[]{:S(2)}, u32[]{:S(2)}) %collective-permute-start.8) | collective-permute-done | bytes 36896 | tf_op jit(solution)/shard_map/ppermute | solution.py:335
  28.6 0.0 collective-permute-done.12.refs_3_
  28.6 1.2 %pull.1 = (f32[3,4096]{1,0:T(4,128)}, f32[32,128]{1,0:T(8,128)}) custom-call(s32[32,128]{1,0:T(8,128)S(1)} %get-tuple-element.19.info_ref, s32[32,3,8,128]{3,2,1,0:T(8,128)S(1)} %get-tuple-element.20.index_ref, f32[32,10,8,128]{3,2,1,0:T(8,128)S(1)} %get-tuple-element.21.weight_ref, s32[32,128]{1,0:T(8,128)S(1)} %get-tuple-element.22.red_ref, ...), custom_call_target="tpu_custom_call" | custom-call | tf_op jit(solution)/shard_map/pull/pallas_call | solution.py:461
  (5 shorter events, 0.0 us)
Async XLA Ops:
  2.4 5.3 %collective-permute-start = (f32[192,128]{1,0:T(8,128)S(1)}, f32[192,128]{1,0:T(8,128)S(1)}, u32[]{:S(2)}, u32[]{:S(2)}) collective-permute-start(f32[192,128]{1,0:T(8,128)S(1)} %get-tuple-element.24), channel_id=1, source_target_pairs={{1,0},{0,1},{3,2},{2,3},{5,4},{4,5},{7,6},{6,7},{9,8},{8,9},{11,10... | collective-permute-start | bytes 294920 | tf_op jit(solution)/shard_map/ppermute | solution.py:335
  2.9 1.2 %collective-permute-start.3 = (f32[64,128]{1,0:T(8,128)S(1)}, f32[64,128]{1,0:T(8,128)S(1)}, u32[]{:S(2)}, u32[]{:S(2)}) collective-permute-start(f32[64,128]{1,0:T(8,128)S(1)} %get-tuple-element.26), channel_id=1, source_target_pairs={{1,0},{0,1},{3,2},{2,3},{5,4},{4,5},{7,6},{6,7},{9,8},{8,9},{11,10... | collective-permute-start | bytes 98312 | tf_op jit(solution)/shard_map/ppermute | solution.py:335
  4.1 5.5 %collective-permute-start.4 = (f32[64,128]{1,0:T(8,128)S(1)}, f32[64,128]{1,0:T(8,128)S(1)}, u32[]{:S(2)}, u32[]{:S(2)}) collective-permute-start(f32[64,128]{1,0:T(8,128)S(1)} %add.7), channel_id=1, source_target_pairs={{6,0},{7,1},{4,2},{5,3},{2,4},{3,5},{0,6},{1,7},{14,8},{15,9},{12,... | collective-permute-start | bytes 98312 | tf_op jit(solution)/shard_map/ppermute | solution.py:335
  7.8 4.0 %collective-permute-start.2 = (f32[64,128]{1,0:T(8,128)S(1)}, f32[64,128]{1,0:T(8,128)S(1)}, u32[]{:S(2)}, u32[]{:S(2)}) collective-permute-start(f32[64,128]{1,0:T(8,128)S(1)} %get-tuple-element.30), channel_id=1, source_target_pairs={{4,0},{5,1},{6,2},{7,3},{0,4},{1,5},{2,6},{3,7},{12,8},{13,9},{14,... | collective-permute-start | bytes 98312 | tf_op jit(solution)/shard_map/ppermute | solution.py:335
  8.4 3.9 %collective-permute-start.1 = (f32[64,128]{1,0:T(8,128)S(1)}, f32[64,128]{1,0:T(8,128)S(1)}, u32[]{:S(2)}, u32[]{:S(2)}) collective-permute-start(f32[64,128]{1,0:T(8,128)S(1)} %get-tuple-element.31), channel_id=1, source_target_pairs={{2,0},{3,1},{0,2},{1,3},{6,4},{7,5},{4,6},{5,7},{10,8},{11,9},{8,1... | collective-permute-start | bytes 98312 | tf_op jit(solution)/shard_map/ppermute | solution.py:335
  12.3 6.0 %collective-permute-start.7 = (f32[104,128]{1,0:T(8,128)S(1)}, f32[104,128]{1,0:T(8,128)S(1)}, u32[]{:S(2)}, u32[]{:S(2)}) collective-permute-start(f32[104,128]{1,0:T(8,128)S(1)} %column.1.refs_0_), channel_id=1, source_target_pairs={{24,0},{25,1},{26,2},{27,3},{28,4},{29,5},{30,6},{31,7},{16,8},{17... | collective-permute-start | bytes 159752 | tf_op jit(solution)/shard_map/ppermute | solution.py:343
  16.0 5.0 %collective-permute-start.6 = (f32[104,128]{1,0:T(8,128)S(1)}, f32[104,128]{1,0:T(8,128)S(1)}, u32[]{:S(2)}, u32[]{:S(2)}) collective-permute-start(f32[104,128]{1,0:T(8,128)S(1)} %column.1.refs_0_), channel_id=1, source_target_pairs={{16,0},{17,1},{18,2},{19,3},{20,4},{21,5},{22,6},{23,7},{24,8},{25... | collective-permute-start | bytes 159752 | tf_op jit(solution)/shard_map/ppermute | solution.py:343
  16.0 5.0 %collective-permute-start.5 = (f32[104,128]{1,0:T(8,128)S(1)}, f32[104,128]{1,0:T(8,128)S(1)}, u32[]{:S(2)}, u32[]{:S(2)}) collective-permute-start(f32[104,128]{1,0:T(8,128)S(1)} %column.1.refs_0_), channel_id=1, source_target_pairs={{8,0},{9,1},{10,2},{11,3},{12,4},{13,5},{14,6},{15,7},{0,8},{1,9},... | collective-permute-start | bytes 159752 | tf_op jit(solution)/shard_map/ppermute | solution.py:343
  21.1 4.9 %collective-permute-start.11 = (f32[72,128]{1,0:T(8,128)S(1)}, f32[72,128]{1,0:T(8,128)S(1)}, u32[]{:S(2)}, u32[]{:S(2)}) collective-permute-start(f32[72,128]{1,0:T(8,128)S(1)} %field.1.refs_0_), channel_id=1, source_target_pairs={{6,0},{7,1},{4,2},{5,3},{2,4},{3,5},{0,6},{1,7},{14,8},{15,9},{12,... | collective-permute-start | bytes 110600 | tf_op jit(solution)/shard_map/ppermute | solution.py:335
  22.7 4.0 %collective-permute-start.10 = (f32[72,128]{1,0:T(8,128)S(1)}, f32[72,128]{1,0:T(8,128)S(1)}, u32[]{:S(2)}, u32[]{:S(2)}) collective-permute-start(f32[72,128]{1,0:T(8,128)S(1)} %field.1.refs_0_), channel_id=1, source_target_pairs={{4,0},{5,1},{6,2},{7,3},{0,4},{1,5},{2,6},{3,7},{12,8},{13,9},{14,... | collective-permute-start | bytes 110600 | tf_op jit(solution)/shard_map/ppermute | solution.py:335
  23.2 4.0 %collective-permute-start.9 = (f32[72,128]{1,0:T(8,128)S(1)}, f32[72,128]{1,0:T(8,128)S(1)}, u32[]{:S(2)}, u32[]{:S(2)}) collective-permute-start(f32[72,128]{1,0:T(8,128)S(1)} %field.1.refs_0_), channel_id=1, source_target_pairs={{2,0},{3,1},{0,2},{1,3},{6,4},{7,5},{4,6},{5,7},{10,8},{11,9},{8,1... | collective-permute-start | bytes 110600 | tf_op jit(solution)/shard_map/ppermute | solution.py:335
  27.1 1.4 %collective-permute-start.12 = (f32[216,128]{1,0:T(8,128)S(1)}, f32[216,128]{1,0:T(8,128)S(1)}, u32[]{:S(2)}, u32[]{:S(2)}) collective-permute-start(f32[216,128]{1,0:T(8,128)S(1)} %joined.1.refs_2_), channel_id=1, source_target_pairs={{1,0},{0,1},{3,2},{2,3},{5,4},{4,5},{7,6},{6,7},{9,8},{8,9},{11,10... | collective-permute-start | bytes 331784 | tf_op jit(solution)/shard_map/ppermute | solution.py:335
  27.2 1.4 %collective-permute-start.8 = (f32[72,128]{1,0:T(8,128)S(1)}, f32[72,128]{1,0:T(8,128)S(1)}, u32[]{:S(2)}, u32[]{:S(2)}) collective-permute-start(f32[72,128]{1,0:T(8,128)S(1)} %field.1.refs_0_), channel_id=1, source_target_pairs={{1,0},{0,1},{3,2},{2,3},{5,4},{4,5},{7,6},{6,7},{9,8},{8,9},{11,10... | collective-permute-start | bytes 110600 | tf_op jit(solution)/shard_map/ppermute | solution.py:335

commit v7 on v6

--- a/solution.py
+++ b/solution.py
@@ -229,8 +229,7 @@
     me = lax.axis_index("los")
     tall = g.column + SUB
     for near in range(g.plane):
-        ref = field_refs[near % 2 + 2 * (near > 1)]
-        base = max(near // 2 - 1, 0) * tall
+        ref, base = field_refs[near % 2], (near // 2) * tall
         for far in range(g.planes):
             slab = slab_at(g, me, near, far)
             at = pl.ds(pl.multiple_of(slab * g.slab, SUB), g.slab)
@@ -447,24 +446,22 @@
         inner = jnp.concatenate([inner, rim[:, :, None], rest], axis=2).reshape(g.column, g.deep)
         rates = jnp.pad(planes[:, 2 * g.slab + 1], ((0, SUB - g.planes), (0, 0)))
         field = jnp.concatenate([inner, rates])
-    around = spread(lambda block, j: to_near(block, 2 * j), [field] * (quarters - 1))
-    own = [field, to_near(field, 1)]
-    joined = pl.pallas_call(
+    even = pl.pallas_call(
         joined_kernel,
-        out_shape=tiled((quarters - 1) * tall),
-        in_specs=[vmem] * (quarters - 1),
+        out_shape=tiled(quarters * tall),
+        in_specs=[vmem] * quarters,
         out_specs=vmem,
         compiler_params=small,
         name="joined",
-    )(*around)
-    fields = [*own, joined, to_near(joined, 1)]
+    )(field, *spread(lambda block, j: to_near(block, 2 * j), [field] * (quarters - 1)))
+    fields = [even, to_near(even, 1)]
     grad_pos, grad_vel = pl.pallas_call(
         functools.partial(pull_kernel, g),
         out_shape=(
             jax.ShapeDtypeStruct(part_frac.shape, f32),
             jax.ShapeDtypeStruct((g.blocks, g.block), f32),
         ),
-        in_specs=[vmem] * 8,
+        in_specs=[vmem] * 6,
         out_specs=(vmem, vmem),
         scratch_shapes=[
             pltpu.VMEM((padded, g.deep), f32),

time: 30 us -> 30 us (level)
  waiting for transfers between devices: 11.5 us -> 12 us
  starting transfers between devices: 13.4 us -> 13 us
    ppermute x10 -> x9, waiting for transfers between devices: 7.21 us -> 7.72 us  [to_near(): return lax.ppermute(block, 'los', [(i ^ near, i) for i in range(g.slabs)])]
    ppermute x10 -> x9, starting transfers between devices: 9 us -> 8.5 us  [to_near(): return lax.ppermute(block, 'los', [(i ^ near, i) for i in range(g.slabs)])]
  transfers between devices with their start and end apart: 13 -> 12, of which waited for: 10 -> 10; matrix products, arithmetic and copies ran while one was open for 0% -> 0% of each run, Pallas kernels for 4% -> 4%
where the time goes in v7:
time: 30 us; the launch traced here: 29.8 us
  starting transfers between devices  13 us (43%)
  waiting for transfers between devices  12 us (40%)
  Pallas kernels  4.15 us (14%)
  between operations  0.69 us (2%)
    ppermute x9, starting transfers between devices, to_near(): return lax.ppermute(block, 'los', [(i ^ near, i) for i in range(g.slabs)])  8.5 us
    ppermute x9, waiting for transfers between devices, to_near(): return lax.ppermute(block, 'los', [(i ^ near, i) for i in range(g.slabs)])  7.72 us
    ppermute x3, starting transfers between devices, from_far(): return lax.ppermute(block, 'los', route)  4.45 us
    ppermute x3, waiting for transfers between devices, from_far(): return lax.ppermute(block, 'los', route)  4.25 us
    pallas_call x1, Pallas kernels, on_device(): pl.pallas_call(functools.partial(paint_kernel, g), out_shape=(pltpu.VMEM(...  1.78 us
    pallas_call x1, Pallas kernels, on_device(): pl.pallas_call(functools.partial(pull_kernel, g), out_shape=(jax.ShapeDty...  1.18 us
    pallas_call x1, Pallas kernels, on_device(): pl.pallas_call(functools.partial(ready_kernel, g), out_shape=(pltpu.VMEM(...  1.06 us
  transfers between devices with their start and end apart: 12, of which 10 were waited for; matrix products, arithmetic and copies ran while one was open for 0% of the time, Pallas kernels for 4%

profile of v7, /device:TPU:0, one launch (start us, length us, event | category | flops | bytes accessed | tf_op | source)
XLA Modules:
  0.0 29.8 jit_solution(3427790508147374041)
XLA Ops:
  0.6 1.8 %paint.1 = (s32[3,4096]{1,0:T(4,128)S(1)}, f32[3,4096]{1,0:T(4,128)S(1)}, s32[32,128]{1,0:T(8,128)S(1)}, f32[192,128]{1,0:T(8,128)S(1)}, f32[192,128]{1,0:T(8,12...) custom-call(s32[32]{0:T(128)} %refs_0_.3, s32[32]{0:T(128)} %refs_1_.3, s32[3,4096]{1,0:T(4,128)} %refs_2_.2, ...), custom_call_target="tpu_custom_call" | custom-call | tf_op jit(solution)/shard_map/paint/pallas_call | solution.py:353
  2.4 0.5 %collective-permute-start = (f32[192,128]{1,0:T(8,128)S(1)}, f32[192,128]{1,0:T(8,128)S(1)}, u32[]{:S(2)}, u32[]{:S(2)}) collective-permute-start(f32[192,128]{1,0:T(8,128)S(1)} %get-tuple-element.24), channel_id=1, source_target_pairs={{1,0},{0,1},{3,2},{2,3},{5,4},{4,5},{7,6},{6,7},{9,8},{8,9},{11,10... | collective-permute-start | bytes 294920 | tf_op jit(solution)/shard_map/ppermute | solution.py:334
  2.9 0.1 collective-permute-start.3
  3.0 1.1 %collective-permute-done.3 = f32[64,128]{1,0:T(8,128)S(1)} collective-permute-done((f32[64,128]{1,0:T(8,128)S(1)}, f32[64,128]{1,0:T(8,128)S(1)}, u32[]{:S(2)}, u32[]{:S(2)}) %collective-permute-start.3) | collective-permute-done | bytes 32800 | tf_op jit(solution)/shard_map/ppermute | solution.py:334
  4.1 3.6 %collective-permute-start.4 = (f32[64,128]{1,0:T(8,128)S(1)}, f32[64,128]{1,0:T(8,128)S(1)}, u32[]{:S(2)}, u32[]{:S(2)}) collective-permute-start(f32[64,128]{1,0:T(8,128)S(1)} %add.7), channel_id=1, source_target_pairs={{6,0},{7,1},{4,2},{5,3},{2,4},{3,5},{0,6},{1,7},{14,8},{15,9},{12,... | collective-permute-start | bytes 98312 | tf_op jit(solution)/shard_map/ppermute | solution.py:334
  7.8 0.0 collective-permute-done
  7.8 0.6 %collective-permute-start.2 = (f32[64,128]{1,0:T(8,128)S(1)}, f32[64,128]{1,0:T(8,128)S(1)}, u32[]{:S(2)}, u32[]{:S(2)}) collective-permute-start(f32[64,128]{1,0:T(8,128)S(1)} %get-tuple-element.30), channel_id=1, source_target_pairs={{4,0},{5,1},{6,2},{7,3},{0,4},{1,5},{2,6},{3,7},{12,8},{13,9},{14,... | collective-permute-start | bytes 98312 | tf_op jit(solution)/shard_map/ppermute | solution.py:334
  8.4 0.1 collective-permute-start.1
  8.5 1.1 %ready.1 = (s32[32,3,8,128]{3,2,1,0:T(8,128)S(1)}, f32[32,10,8,128]{3,2,1,0:T(8,128)S(1)}, s32[32,128]{1,0:T(8,128)S(1)}, s32[32,128]{1,0:T(8,128)S(1)}, f32[40,128]{1,0:T(8,128)S(1)}) custom-call(s32[3,4096]{1,0:T(4,128)S(1)} %get-tuple-element.16.cell_ref, f32[3,4096]{1,0:T(4,128)S(1)} %get-tuple-element.17.frac_ref, ...), custom_call_target="tpu_custom_call" | custom-call | flops 1000000 | bytes 4000000 | tf_op jit(solution)/shard_map/ready/pallas_call | solution.py:376
  9.5 0.1 collective-permute-done.4.refs_2_
  9.7 2.1 %collective-permute-done.2.refs_1_ = f32[64,128]{1,0:T(8,128)S(1)} collective-permute-done((f32[64,128]{1,0:T(8,128)S(1)}, f32[64,128]{1,0:T(8,128)S(1)}, u32[]{:S(2)}, u32[]{:S(2)}) %collective-permute-start.2) | collective-permute-done | bytes 32800 | tf_op jit(solution)/shard_map/ppermute | solution.py:334
  11.8 0.5 %collective-permute-done.1.refs_0_ = f32[64,128]{1,0:T(8,128)S(1)} collective-permute-done((f32[64,128]{1,0:T(8,128)S(1)}, f32[64,128]{1,0:T(8,128)S(1)}, u32[]{:S(2)}, u32[]{:S(2)}) %collective-permute-start.1) | collective-permute-done | bytes 32800 | tf_op jit(solution)/shard_map/ppermute | solution.py:334
  12.3 3.7 %collective-permute-start.7 = (f32[104,128]{1,0:T(8,128)S(1)}, f32[104,128]{1,0:T(8,128)S(1)}, u32[]{:S(2)}, u32[]{:S(2)}) collective-permute-start(f32[104,128]{1,0:T(8,128)S(1)} %column.1.refs_0_), channel_id=1, source_target_pairs={{24,0},{25,1},{26,2},{27,3},{28,4},{29,5},{30,6},{31,7},{16,8},{17... | collective-permute-start | bytes 159752 | tf_op jit(solution)/shard_map/ppermute | solution.py:342
  16.0 0.0 collective-permute-start.6
  16.0 0.8 %collective-permute-start.5 = (f32[104,128]{1,0:T(8,128)S(1)}, f32[104,128]{1,0:T(8,128)S(1)}, u32[]{:S(2)}, u32[]{:S(2)}) collective-permute-start(f32[104,128]{1,0:T(8,128)S(1)} %column.1.refs_0_), channel_id=1, source_target_pairs={{8,0},{9,1},{10,2},{11,3},{12,4},{13,5},{14,6},{15,7},{0,8},{1,9},... | collective-permute-start | bytes 159752 | tf_op jit(solution)/shard_map/ppermute | solution.py:342
  16.7 1.6 %collective-permute-done.7.refs_3_ = f32[104,128]{1,0:T(8,128)S(1)} collective-permute-done((f32[104,128]{1,0:T(8,128)S(1)}, f32[104,128]{1,0:T(8,128)S(1)}, u32[]{:S(2)}, u32[]{:S(2)}) %collective-permute-start.7) | collective-permute-done | bytes 53280 | tf_op jit(solution)/shard_map/ppermute | solution.py:342
  18.3 2.7 %collective-permute-done.6.refs_2_ = f32[104,128]{1,0:T(8,128)S(1)} collective-permute-done((f32[104,128]{1,0:T(8,128)S(1)}, f32[104,128]{1,0:T(8,128)S(1)}, u32[]{:S(2)}, u32[]{:S(2)}) %collective-permute-start.6) | collective-permute-done | bytes 53280 | tf_op jit(solution)/shard_map/ppermute | solution.py:342
  21.0 0.0 collective-permute-done.5.refs_1_
  21.0 0.1 field.1.refs_0_
  21.1 1.6 %collective-permute-start.10 = (f32[72,128]{1,0:T(8,128)S(1)}, f32[72,128]{1,0:T(8,128)S(1)}, u32[]{:S(2)}, u32[]{:S(2)}) collective-permute-start(f32[72,128]{1,0:T(8,128)S(1)} %field.1.refs_0_), channel_id=1, source_target_pairs={{6,0},{7,1},{4,2},{5,3},{2,4},{3,5},{0,6},{1,7},{14,8},{15,9},{12,... | collective-permute-start | bytes 110600 | tf_op jit(solution)/shard_map/ppermute | solution.py:334
  22.7 0.5 %collective-permute-start.9 = (f32[72,128]{1,0:T(8,128)S(1)}, f32[72,128]{1,0:T(8,128)S(1)}, u32[]{:S(2)}, u32[]{:S(2)}) collective-permute-start(f32[72,128]{1,0:T(8,128)S(1)} %field.1.refs_0_), channel_id=1, source_target_pairs={{4,0},{5,1},{6,2},{7,3},{0,4},{1,5},{2,6},{3,7},{12,8},{13,9},{14,... | collective-permute-start | bytes 110600 | tf_op jit(solution)/shard_map/ppermute | solution.py:334
  23.2 1.5 %collective-permute-start.8 = (f32[72,128]{1,0:T(8,128)S(1)}, f32[72,128]{1,0:T(8,128)S(1)}, u32[]{:S(2)}, u32[]{:S(2)}) collective-permute-start(f32[72,128]{1,0:T(8,128)S(1)} %field.1.refs_0_), channel_id=1, source_target_pairs={{2,0},{3,1},{0,2},{1,3},{6,4},{7,5},{4,6},{5,7},{10,8},{11,9},{8,1... | collective-permute-start | bytes 110600 | tf_op jit(solution)/shard_map/ppermute | solution.py:334
  24.7 1.4 %collective-permute-done.10.refs_3_ = f32[72,128]{1,0:T(8,128)S(1)} collective-permute-done((f32[72,128]{1,0:T(8,128)S(1)}, f32[72,128]{1,0:T(8,128)S(1)}, u32[]{:S(2)}, u32[]{:S(2)}) %collective-permute-start.10) | collective-permute-done | bytes 36896 | tf_op jit(solution)/shard_map/ppermute | solution.py:334
  26.0 0.6 %collective-permute-done.9.refs_2_ = f32[72,128]{1,0:T(8,128)S(1)} collective-permute-done((f32[72,128]{1,0:T(8,128)S(1)}, f32[72,128]{1,0:T(8,128)S(1)}, u32[]{:S(2)}, u32[]{:S(2)}) %collective-permute-start.9) | collective-permute-done | bytes 36896 | tf_op jit(solution)/shard_map/ppermute | solution.py:334
  26.6 0.5 %collective-permute-done.8.refs_1_ = f32[72,128]{1,0:T(8,128)S(1)} collective-permute-done((f32[72,128]{1,0:T(8,128)S(1)}, f32[72,128]{1,0:T(8,128)S(1)}, u32[]{:S(2)}, u32[]{:S(2)}) %collective-permute-start.8) | collective-permute-done | bytes 36896 | tf_op jit(solution)/shard_map/ppermute | solution.py:334
  27.2 0.1 collective-permute-start.11
  27.2 1.4 %collective-permute-done.11.refs_1_ = f32[288,128]{1,0:T(8,128)S(1)} collective-permute-done((f32[288,128]{1,0:T(8,128)S(1)}, f32[288,128]{1,0:T(8,128)S(1)}, u32[]{:S(2)}, u32[]{:S(2)}) %collective-permute-start.11) | collective-permute-done | bytes 147488 | tf_op jit(solution)/shard_map/ppermute | solution.py:334
  28.6 1.2 %pull.1 = (f32[3,4096]{1,0:T(4,128)}, f32[32,128]{1,0:T(8,128)}) custom-call(s32[32,128]{1,0:T(8,128)S(1)} %get-tuple-element.19.info_ref, s32[32,3,8,128]{3,2,1,0:T(8,128)S(1)} %get-tuple-element.20.index_ref, f32[32,10,8,128]{3,2,1,0:T(8,128)S(1)} %get-tuple-element.21.weight_ref, s32[32,128]{1,0:T(8,128)S(1)} %get-tuple-element.22.red_ref, ...), custom_call_target="tpu_custom_call" | custom-call | tf_op jit(solution)/shard_map/pull/pallas_call | solution.py:458
  (5 shorter events, 0.0 us)
Async XLA Ops:
  2.4 5.3 %collective-permute-start = (f32[192,128]{1,0:T(8,128)S(1)}, f32[192,128]{1,0:T(8,128)S(1)}, u32[]{:S(2)}, u32[]{:S(2)}) collective-permute-start(f32[192,128]{1,0:T(8,128)S(1)} %get-tuple-element.24), channel_id=1, source_target_pairs={{1,0},{0,1},{3,2},{2,3},{5,4},{4,5},{7,6},{6,7},{9,8},{8,9},{11,10... | collective-permute-start | bytes 294920 | tf_op jit(solution)/shard_map/ppermute | solution.py:334
  2.9 1.2 %collective-permute-start.3 = (f32[64,128]{1,0:T(8,128)S(1)}, f32[64,128]{1,0:T(8,128)S(1)}, u32[]{:S(2)}, u32[]{:S(2)}) collective-permute-start(f32[64,128]{1,0:T(8,128)S(1)} %get-tuple-element.26), channel_id=1, source_target_pairs={{1,0},{0,1},{3,2},{2,3},{5,4},{4,5},{7,6},{6,7},{9,8},{8,9},{11,10... | collective-permute-start | bytes 98312 | tf_op jit(solution)/shard_map/ppermute | solution.py:334
  4.1 5.5 %collective-permute-start.4 = (f32[64,128]{1,0:T(8,128)S(1)}, f32[64,128]{1,0:T(8,128)S(1)}, u32[]{:S(2)}, u32[]{:S(2)}) collective-permute-start(f32[64,128]{1,0:T(8,128)S(1)} %add.7), channel_id=1, source_target_pairs={{6,0},{7,1},{4,2},{5,3},{2,4},{3,5},{0,6},{1,7},{14,8},{15,9},{12,... | collective-permute-start | bytes 98312 | tf_op jit(solution)/shard_map/ppermute | solution.py:334
  7.8 4.0 %collective-permute-start.2 = (f32[64,128]{1,0:T(8,128)S(1)}, f32[64,128]{1,0:T(8,128)S(1)}, u32[]{:S(2)}, u32[]{:S(2)}) collective-permute-start(f32[64,128]{1,0:T(8,128)S(1)} %get-tuple-element.30), channel_id=1, source_target_pairs={{4,0},{5,1},{6,2},{7,3},{0,4},{1,5},{2,6},{3,7},{12,8},{13,9},{14,... | collective-permute-start | bytes 98312 | tf_op jit(solution)/shard_map/ppermute | solution.py:334
  8.4 3.9 %collective-permute-start.1 = (f32[64,128]{1,0:T(8,128)S(1)}, f32[64,128]{1,0:T(8,128)S(1)}, u32[]{:S(2)}, u32[]{:S(2)}) collective-permute-start(f32[64,128]{1,0:T(8,128)S(1)} %get-tuple-element.31), channel_id=1, source_target_pairs={{2,0},{3,1},{0,2},{1,3},{6,4},{7,5},{4,6},{5,7},{10,8},{11,9},{8,1... | collective-permute-start | bytes 98312 | tf_op jit(solution)/shard_map/ppermute | solution.py:334
  12.3 6.0 %collective-permute-start.7 = (f32[104,128]{1,0:T(8,128)S(1)}, f32[104,128]{1,0:T(8,128)S(1)}, u32[]{:S(2)}, u32[]{:S(2)}) collective-permute-start(f32[104,128]{1,0:T(8,128)S(1)} %column.1.refs_0_), channel_id=1, source_target_pairs={{24,0},{25,1},{26,2},{27,3},{28,4},{29,5},{30,6},{31,7},{16,8},{17... | collective-permute-start | bytes 159752 | tf_op jit(solution)/shard_map/ppermute | solution.py:342
  16.0 5.0 %collective-permute-start.6 = (f32[104,128]{1,0:T(8,128)S(1)}, f32[104,128]{1,0:T(8,128)S(1)}, u32[]{:S(2)}, u32[]{:S(2)}) collective-permute-start(f32[104,128]{1,0:T(8,128)S(1)} %column.1.refs_0_), channel_id=1, source_target_pairs={{16,0},{17,1},{18,2},{19,3},{20,4},{21,5},{22,6},{23,7},{24,8},{25... | collective-permute-start | bytes 159752 | tf_op jit(solution)/shard_map/ppermute | solution.py:342
  16.0 5.0 %collective-permute-start.5 = (f32[104,128]{1,0:T(8,128)S(1)}, f32[104,128]{1,0:T(8,128)S(1)}, u32[]{:S(2)}, u32[]{:S(2)}) collective-permute-start(f32[104,128]{1,0:T(8,128)S(1)} %column.1.refs_0_), channel_id=1, source_target_pairs={{8,0},{9,1},{10,2},{11,3},{12,4},{13,5},{14,6},{15,7},{0,8},{1,9},... | collective-permute-start | bytes 159752 | tf_op jit(solution)/shard_map/ppermute | solution.py:342
  21.1 4.9 %collective-permute-start.10 = (f32[72,128]{1,0:T(8,128)S(1)}, f32[72,128]{1,0:T(8,128)S(1)}, u32[]{:S(2)}, u32[]{:S(2)}) collective-permute-start(f32[72,128]{1,0:T(8,128)S(1)} %field.1.refs_0_), channel_id=1, source_target_pairs={{6,0},{7,1},{4,2},{5,3},{2,4},{3,5},{0,6},{1,7},{14,8},{15,9},{12,... | collective-permute-start | bytes 110600 | tf_op jit(solution)/shard_map/ppermute | solution.py:334
  22.7 4.0 %collective-permute-start.9 = (f32[72,128]{1,0:T(8,128)S(1)}, f32[72,128]{1,0:T(8,128)S(1)}, u32[]{:S(2)}, u32[]{:S(2)}) collective-permute-start(f32[72,128]{1,0:T(8,128)S(1)} %field.1.refs_0_), channel_id=1, source_target_pairs={{4,0},{5,1},{6,2},{7,3},{0,4},{1,5},{2,6},{3,7},{12,8},{13,9},{14,... | collective-permute-start | bytes 110600 | tf_op jit(solution)/shard_map/ppermute | solution.py:334
  23.2 4.0 %collective-permute-start.8 = (f32[72,128]{1,0:T(8,128)S(1)}, f32[72,128]{1,0:T(8,128)S(1)}, u32[]{:S(2)}, u32[]{:S(2)}) collective-permute-start(f32[72,128]{1,0:T(8,128)S(1)} %field.1.refs_0_), channel_id=1, source_target_pairs={{2,0},{3,1},{0,2},{1,3},{6,4},{7,5},{4,6},{5,7},{10,8},{11,9},{8,1... | collective-permute-start | bytes 110600 | tf_op jit(solution)/shard_map/ppermute | solution.py:334
  27.2 1.4 %collective-permute-start.11 = (f32[288,128]{1,0:T(8,128)S(1)}, f32[288,128]{1,0:T(8,128)S(1)}, u32[]{:S(2)}, u32[]{:S(2)}) collective-permute-start(f32[288,128]{1,0:T(8,128)S(1)} %joined.1.refs_0_), channel_id=1, source_target_pairs={{1,0},{0,1},{3,2},{2,3},{5,4},{4,5},{7,6},{6,7},{9,8},{8,9},{11,10... | collective-permute-start | bytes 442376 | tf_op jit(solution)/shard_map/ppermute | solution.py:334

commit v8 on v4

--- a/solution.py
+++ b/solution.py
@@ -153,8 +153,8 @@
     far = lax.axis_index("los") // g.plane
     plane = lax.broadcasted_iota(jnp.int32, (g.slab, g.deep), 0) // g.cols
     out_ref[g.column :, :] = jnp.zeros((SUB, g.deep), jnp.float32)
-    for i, ref in enumerate(part_refs):
-        there = g.far_peer(far, i)
+    for m, ref in zip(g.turns, part_refs, strict=True):
+        there = g.far_peer(far, m)
         at = pl.ds(pl.multiple_of(there * g.slab, SUB), g.slab)
         start = g.column + 2 * g.slab
         exponent = picked(jnp.broadcast_to(ref[start : start + 1, :], (g.slab, g.deep)), plane)
@@ -292,6 +292,8 @@
         self.plane = 8
         self.planes = slabs // self.plane
         self.column = self.planes * self.slab
+        turns = (2, 1, 3) if self.planes == 4 else range(1, self.planes)
+        self.turns = (0, *turns)
         self.window = rounded_up(self.slab + self.cols, SUB)
 
         self.twice = self.planes_per_tile == 2 and self.slab % SUB == 0
@@ -408,7 +410,7 @@
         compiler_params=small,
         name="column",
     )(pair[0], *spread(lambda block, j: to_near(block, 2 * j), list(pair[1:])), table)
-    parts = [column] + spread(from_far, [column] * (g.planes - 1))
+    parts = [column] + [from_far(column, m) for m in g.turns[1:]]
     tall = g.column + SUB
     if sky_parts == 1:
         field = pl.pallas_call(
@@ -424,9 +426,9 @@
         here = lax.axis_index("los") // g.plane
         stacked = jnp.stack(parts)
         planes = jnp.zeros_like(stacked[:, g.column :])
-        for m in range(g.planes):
+        for i, m in enumerate(g.turns):
             planes = lax.dynamic_update_index_in_dim(
-                planes, stacked[m, g.column :], g.far_peer(here, m), 0
+                planes, stacked[i, g.column :], g.far_peer(here, m), 0
             )
         cells = planes[:, : 2 * g.slab].reshape(g.planes, 2, g.slab_rows, g.cols, g.deep)
         power = planes[:, 2 * g.slab, : g.slab_rows, None, None]

time: 30.1 us -> 30.1 us (level)
  transfers between devices with their start and end apart: 11 -> 11, of which waited for: 10 -> 11; matrix products, arithmetic and copies ran while one was open for 0% -> 0% of each run, Pallas kernels for 4% -> 4%
where the time goes in v8:
time: 30.1 us; the launch traced here: 29.9 us
  starting transfers between devices  13.1 us (44%)
  waiting for transfers between devices  11.8 us (39%)
  Pallas kernels  4.27 us (14%)
  between operations  0.69 us (2%)
    ppermute x8, starting transfers between devices, to_near(): return lax.ppermute(block, 'los', [(i ^ near, i) for i in range(g.slabs)])  8.65 us
    ppermute x8, waiting for transfers between devices, to_near(): return lax.ppermute(block, 'los', [(i ^ near, i) for i in range(g.slabs)])  7.52 us
    ppermute x3, starting transfers between devices, from_far(): return lax.ppermute(block, 'los', route)  4.45 us
    ppermute x3, waiting for transfers between devices, from_far(): return lax.ppermute(block, 'los', route)  4.25 us
    pallas_call x1, Pallas kernels, on_device(): pl.pallas_call(functools.partial(paint_kernel, g), out_shape=(pltpu.VMEM(...  1.9 us
    pallas_call x1, Pallas kernels, on_device(): pl.pallas_call(functools.partial(pull_kernel, g), out_shape=(jax.ShapeDty...  1.18 us
    pallas_call x1, Pallas kernels, on_device(): pl.pallas_call(functools.partial(ready_kernel, g), out_shape=(pltpu.VMEM(...  1.06 us
  transfers between devices with their start and end apart: 11, of which 11 were waited for; matrix products, arithmetic and copies ran while one was open for 0% of the time, Pallas kernels for 4%

profile of v8, /device:TPU:0, one launch (start us, length us, event | category | flops | bytes accessed | tf_op | source)
XLA Modules:
  0.0 29.9 jit_solution(14452592402240059458)
XLA Ops:
  0.6 1.9 %paint.1 = (s32[3,4096]{1,0:T(4,128)S(1)}, f32[3,4096]{1,0:T(4,128)S(1)}, s32[32,128]{1,0:T(8,128)S(1)}, f32[256,128]{1,0:T(8,128)S(1)}, f32[256,128]{1,0:T(8,128)S(1)}) custom-call(s32[32]{0:T(128)} %refs_0_.3, s32[32]{0:T(128)} %refs_1_.3, s32[3,4096]{1,0:T(4,128)} %refs_2_.2, f32[3,4096]{1,0:T(4,128)} %refs_3_.2, s32[32,128]{1,0:T(8,128)} %bitcast.2), custom_call_target="tpu_custom_call" | custom-call | tf_op jit(solution)/shard_map/paint/pallas_call | solution.py:354
  2.5 0.5 %collective-permute-start = (f32[256,128]{1,0:T(8,128)S(1)}, f32[256,128]{1,0:T(8,128)S(1)}, u32[]{:S(2)}, u32[]{:S(2)}) collective-permute-start(f32[256,128]{1,0:T(8,128)S(1)} %get-tuple-element.22), channel_id=1, source_target_pairs={{1,0},{0,1},{3,2},{2,3},{5,4},{4,5},{7,6},{6,7},{9,8},{8,9},{11,10... | collective-permute-start | bytes 393224 | tf_op jit(solution)/shard_map/ppermute | solution.py:336
  3.1 1.0 %collective-permute-done = f32[256,128]{1,0:T(8,128)S(1)} collective-permute-done((f32[256,128]{1,0:T(8,128)S(1)}, f32[256,128]{1,0:T(8,128)S(1)}, u32[]{:S(2)}, u32[]{:S(2)}) %collective-permute-start) | collective-permute-done | bytes 131104 | tf_op jit(solution)/shard_map/ppermute | solution.py:336
  4.1 3.9 %collective-permute-start.3 = (f32[64,128]{1,0:T(8,128)S(1)}, f32[64,128]{1,0:T(8,128)S(1)}, u32[]{:S(2)}, u32[]{:S(2)}) collective-permute-start(f32[64,128]{1,0:T(8,128)S(1)} %get-tuple-element.26), channel_id=1, source_target_pairs={{6,0},{7,1},{4,2},{5,3},{2,4},{3,5},{0,6},{1,7},{14,8},{15,9},{12,... | collective-permute-start | bytes 98312 | tf_op jit(solution)/shard_map/ppermute | solution.py:336
  8.0 0.5 %collective-permute-start.2 = (f32[64,128]{1,0:T(8,128)S(1)}, f32[64,128]{1,0:T(8,128)S(1)}, u32[]{:S(2)}, u32[]{:S(2)}) collective-permute-start(f32[64,128]{1,0:T(8,128)S(1)} %get-tuple-element.27), channel_id=1, source_target_pairs={{4,0},{5,1},{6,2},{7,3},{0,4},{1,5},{2,6},{3,7},{12,8},{13,9},{14,... | collective-permute-start | bytes 98312 | tf_op jit(solution)/shard_map/ppermute | solution.py:336
  8.5 0.1 collective-permute-start.1
  8.6 1.1 %ready.1 = (s32[32,3,8,128]{3,2,1,0:T(8,128)S(1)}, f32[32,10,8,128]{3,2,1,0:T(8,128)S(1)}, s32[32,128]{1,0:T(8,128)S(1)}, s32[32,128]{1,0:T(8,128)S(1)}, f32[40,128]{1,0:T(8,128)S(1)}) custom-call(s32[3,4096]{1,0:T(4,128)S(1)} %get-tuple-element.14.cell_ref, f32[3,4096]{1,0:T(4,128)S(1)} %get-tuple-element.15.frac_ref, ...), custom_call_target="tpu_custom_call" | custom-call | flops 1000000 | bytes 4000000 | tf_op jit(solution)/shard_map/ready/pallas_call | solution.py:375
  9.7 0.2 collective-permute-done.3.refs_2_
  9.8 2.0 %collective-permute-done.2.refs_1_ = f32[64,128]{1,0:T(8,128)S(1)} collective-permute-done((f32[64,128]{1,0:T(8,128)S(1)}, f32[64,128]{1,0:T(8,128)S(1)}, u32[]{:S(2)}, u32[]{:S(2)}) %collective-permute-start.2) | collective-permute-done | bytes 32800 | tf_op jit(solution)/shard_map/ppermute | solution.py:336
  11.9 0.5 %collective-permute-done.1.refs_0_ = f32[64,128]{1,0:T(8,128)S(1)} collective-permute-done((f32[64,128]{1,0:T(8,128)S(1)}, f32[64,128]{1,0:T(8,128)S(1)}, u32[]{:S(2)}, u32[]{:S(2)}) %collective-permute-start.1) | collective-permute-done | bytes 32800 | tf_op jit(solution)/shard_map/ppermute | solution.py:336
  12.4 3.7 %collective-permute-start.6 = (f32[104,128]{1,0:T(8,128)S(1)}, f32[104,128]{1,0:T(8,128)S(1)}, u32[]{:S(2)}, u32[]{:S(2)}) collective-permute-start(f32[104,128]{1,0:T(8,128)S(1)} %column.1.refs_0_), channel_id=1, source_target_pairs={{24,0},{25,1},{26,2},{27,3},{28,4},{29,5},{30,6},{31,7},{16,8},{17... | collective-permute-start | bytes 159752 | tf_op jit(solution)/shard_map/ppermute | solution.py:344
  16.1 0.0 collective-permute-start.5
  16.1 0.8 %collective-permute-start.4 = (f32[104,128]{1,0:T(8,128)S(1)}, f32[104,128]{1,0:T(8,128)S(1)}, u32[]{:S(2)}, u32[]{:S(2)}) collective-permute-start(f32[104,128]{1,0:T(8,128)S(1)} %column.1.refs_0_), channel_id=1, source_target_pairs={{16,0},{17,1},{18,2},{19,3},{20,4},{21,5},{22,6},{23,7},{24,8},{25... | collective-permute-start | bytes 159752 | tf_op jit(solution)/shard_map/ppermute | solution.py:344
  16.8 1.6 %collective-permute-done.6.refs_3_ = f32[104,128]{1,0:T(8,128)S(1)} collective-permute-done((f32[104,128]{1,0:T(8,128)S(1)}, f32[104,128]{1,0:T(8,128)S(1)}, u32[]{:S(2)}, u32[]{:S(2)}) %collective-permute-start.6) | collective-permute-done | bytes 53280 | tf_op jit(solution)/shard_map/ppermute | solution.py:344
  18.5 1.7 %collective-permute-done.5.refs_2_ = f32[104,128]{1,0:T(8,128)S(1)} collective-permute-done((f32[104,128]{1,0:T(8,128)S(1)}, f32[104,128]{1,0:T(8,128)S(1)}, u32[]{:S(2)}, u32[]{:S(2)}) %collective-permute-start.5) | collective-permute-done | bytes 53280 | tf_op jit(solution)/shard_map/ppermute | solution.py:344
  20.2 0.9 %collective-permute-done.4.refs_1_ = f32[104,128]{1,0:T(8,128)S(1)} collective-permute-done((f32[104,128]{1,0:T(8,128)S(1)}, f32[104,128]{1,0:T(8,128)S(1)}, u32[]{:S(2)}, u32[]{:S(2)}) %collective-permute-start.4) | collective-permute-done | bytes 53280 | tf_op jit(solution)/shard_map/ppermute | solution.py:344
  21.1 0.1 field.1.refs_0_
  21.2 1.6 %collective-permute-start.9 = (f32[72,128]{1,0:T(8,128)S(1)}, f32[72,128]{1,0:T(8,128)S(1)}, u32[]{:S(2)}, u32[]{:S(2)}) collective-permute-start(f32[72,128]{1,0:T(8,128)S(1)} %field.1.refs_0_), channel_id=1, source_target_pairs={{6,0},{7,1},{4,2},{5,3},{2,4},{3,5},{0,6},{1,7},{14,8},{15,9},{12,... | collective-permute-start | bytes 110600 | tf_op jit(solution)/shard_map/ppermute | solution.py:336
  22.8 0.5 %collective-permute-start.8 = (f32[72,128]{1,0:T(8,128)S(1)}, f32[72,128]{1,0:T(8,128)S(1)}, u32[]{:S(2)}, u32[]{:S(2)}) collective-permute-start(f32[72,128]{1,0:T(8,128)S(1)} %field.1.refs_0_), channel_id=1, source_target_pairs={{4,0},{5,1},{6,2},{7,3},{0,4},{1,5},{2,6},{3,7},{12,8},{13,9},{14,... | collective-permute-start | bytes 110600 | tf_op jit(solution)/shard_map/ppermute | solution.py:336
  23.3 1.5 %collective-permute-start.7 = (f32[72,128]{1,0:T(8,128)S(1)}, f32[72,128]{1,0:T(8,128)S(1)}, u32[]{:S(2)}, u32[]{:S(2)}) collective-permute-start(f32[72,128]{1,0:T(8,128)S(1)} %field.1.refs_0_), channel_id=1, source_target_pairs={{2,0},{3,1},{0,2},{1,3},{6,4},{7,5},{4,6},{5,7},{10,8},{11,9},{8,1... | collective-permute-start | bytes 110600 | tf_op jit(solution)/shard_map/ppermute | solution.py:336
  24.8 1.4 %collective-permute-done.9.refs_3_ = f32[72,128]{1,0:T(8,128)S(1)} collective-permute-done((f32[72,128]{1,0:T(8,128)S(1)}, f32[72,128]{1,0:T(8,128)S(1)}, u32[]{:S(2)}, u32[]{:S(2)}) %collective-permute-start.9) | collective-permute-done | bytes 36896 | tf_op jit(solution)/shard_map/ppermute | solution.py:336
  26.1 0.6 %collective-permute-done.8.refs_2_ = f32[72,128]{1,0:T(8,128)S(1)} collective-permute-done((f32[72,128]{1,0:T(8,128)S(1)}, f32[72,128]{1,0:T(8,128)S(1)}, u32[]{:S(2)}, u32[]{:S(2)}) %collective-permute-start.8) | collective-permute-done | bytes 36896 | tf_op jit(solution)/shard_map/ppermute | solution.py:336
  26.7 0.5 %collective-permute-done.7.refs_1_ = f32[72,128]{1,0:T(8,128)S(1)} collective-permute-done((f32[72,128]{1,0:T(8,128)S(1)}, f32[72,128]{1,0:T(8,128)S(1)}, u32[]{:S(2)}, u32[]{:S(2)}) %collective-permute-start.7) | collective-permute-done | bytes 36896 | tf_op jit(solution)/shard_map/ppermute | solution.py:336
  27.2 0.1 collective-permute-start.10
  27.3 1.4 %collective-permute-done.10.refs_1_ = f32[288,128]{1,0:T(8,128)S(1)} collective-permute-done((f32[288,128]{1,0:T(8,128)S(1)}, f32[288,128]{1,0:T(8,128)S(1)}, u32[]{:S(2)}, u32[]{:S(2)}) %collective-permute-start.10) | collective-permute-done | bytes 147488 | tf_op jit(solution)/shard_map/ppermute | solution.py:336
  28.7 1.2 %pull.1 = (f32[3,4096]{1,0:T(4,128)}, f32[32,128]{1,0:T(8,128)}) custom-call(s32[32,128]{1,0:T(8,128)S(1)} %get-tuple-element.17.info_ref, s32[32,3,8,128]{3,2,1,0:T(8,128)S(1)} %get-tuple-element.18.index_ref, f32[32,10,8,128]{3,2,1,0:T(8,128)S(1)} %get-tuple-element.19.weight_ref, s32[32,128]{1,0:T(8,128)S(1)} %get-tuple-element.20.red_ref, ...), custom_call_target="tpu_custom_call" | custom-call | tf_op jit(solution)/shard_map/pull/pallas_call | solution.py:455
  (4 shorter events, 0.0 us)
Async XLA Ops:
  2.5 1.5 %collective-permute-start = (f32[256,128]{1,0:T(8,128)S(1)}, f32[256,128]{1,0:T(8,128)S(1)}, u32[]{:S(2)}, u32[]{:S(2)}) collective-permute-start(f32[256,128]{1,0:T(8,128)S(1)} %get-tuple-element.22), channel_id=1, source_target_pairs={{1,0},{0,1},{3,2},{2,3},{5,4},{4,5},{7,6},{6,7},{9,8},{8,9},{11,10... | collective-permute-start | bytes 393224 | tf_op jit(solution)/shard_map/ppermute | solution.py:336
  4.1 5.8 %collective-permute-start.3 = (f32[64,128]{1,0:T(8,128)S(1)}, f32[64,128]{1,0:T(8,128)S(1)}, u32[]{:S(2)}, u32[]{:S(2)}) collective-permute-start(f32[64,128]{1,0:T(8,128)S(1)} %get-tuple-element.26), channel_id=1, source_target_pairs={{6,0},{7,1},{4,2},{5,3},{2,4},{3,5},{0,6},{1,7},{14,8},{15,9},{12,... | collective-permute-start | bytes 98312 | tf_op jit(solution)/shard_map/ppermute | solution.py:336
  8.0 3.9 %collective-permute-start.2 = (f32[64,128]{1,0:T(8,128)S(1)}, f32[64,128]{1,0:T(8,128)S(1)}, u32[]{:S(2)}, u32[]{:S(2)}) collective-permute-start(f32[64,128]{1,0:T(8,128)S(1)} %get-tuple-element.27), channel_id=1, source_target_pairs={{4,0},{5,1},{6,2},{7,3},{0,4},{1,5},{2,6},{3,7},{12,8},{13,9},{14,... | collective-permute-start | bytes 98312 | tf_op jit(solution)/shard_map/ppermute | solution.py:336
  8.5 3.9 %collective-permute-start.1 = (f32[64,128]{1,0:T(8,128)S(1)}, f32[64,128]{1,0:T(8,128)S(1)}, u32[]{:S(2)}, u32[]{:S(2)}) collective-permute-start(f32[64,128]{1,0:T(8,128)S(1)} %get-tuple-element.28), channel_id=1, source_target_pairs={{2,0},{3,1},{0,2},{1,3},{6,4},{7,5},{4,6},{5,7},{10,8},{11,9},{8,1... | collective-permute-start | bytes 98312 | tf_op jit(solution)/shard_map/ppermute | solution.py:336
  12.4 6.1 %collective-permute-start.6 = (f32[104,128]{1,0:T(8,128)S(1)}, f32[104,128]{1,0:T(8,128)S(1)}, u32[]{:S(2)}, u32[]{:S(2)}) collective-permute-start(f32[104,128]{1,0:T(8,128)S(1)} %column.1.refs_0_), channel_id=1, source_target_pairs={{24,0},{25,1},{26,2},{27,3},{28,4},{29,5},{30,6},{31,7},{16,8},{17... | collective-permute-start | bytes 159752 | tf_op jit(solution)/shard_map/ppermute | solution.py:344
  16.1 4.1 %collective-permute-start.5 = (f32[104,128]{1,0:T(8,128)S(1)}, f32[104,128]{1,0:T(8,128)S(1)}, u32[]{:S(2)}, u32[]{:S(2)}) collective-permute-start(f32[104,128]{1,0:T(8,128)S(1)} %column.1.refs_0_), channel_id=1, source_target_pairs={{8,0},{9,1},{10,2},{11,3},{12,4},{13,5},{14,6},{15,7},{0,8},{1,9},... | collective-permute-start | bytes 159752 | tf_op jit(solution)/shard_map/ppermute | solution.py:344
  16.1 5.0 %collective-permute-start.4 = (f32[104,128]{1,0:T(8,128)S(1)}, f32[104,128]{1,0:T(8,128)S(1)}, u32[]{:S(2)}, u32[]{:S(2)}) collective-permute-start(f32[104,128]{1,0:T(8,128)S(1)} %column.1.refs_0_), channel_id=1, source_target_pairs={{16,0},{17,1},{18,2},{19,3},{20,4},{21,5},{22,6},{23,7},{24,8},{25... | collective-permute-start | bytes 159752 | tf_op jit(solution)/shard_map/ppermute | solution.py:344
  21.2 4.9 %collective-permute-start.9 = (f32[72,128]{1,0:T(8,128)S(1)}, f32[72,128]{1,0:T(8,128)S(1)}, u32[]{:S(2)}, u32[]{:S(2)}) collective-permute-start(f32[72,128]{1,0:T(8,128)S(1)} %field.1.refs_0_), channel_id=1, source_target_pairs={{6,0},{7,1},{4,2},{5,3},{2,4},{3,5},{0,6},{1,7},{14,8},{15,9},{12,... | collective-permute-start | bytes 110600 | tf_op jit(solution)/shard_map/ppermute | solution.py:336
  22.8 4.0 %collective-permute-start.8 = (f32[72,128]{1,0:T(8,128)S(1)}, f32[72,128]{1,0:T(8,128)S(1)}, u32[]{:S(2)}, u32[]{:S(2)}) collective-permute-start(f32[72,128]{1,0:T(8,128)S(1)} %field.1.refs_0_), channel_id=1, source_target_pairs={{4,0},{5,1},{6,2},{7,3},{0,4},{1,5},{2,6},{3,7},{12,8},{13,9},{14,... | collective-permute-start | bytes 110600 | tf_op jit(solution)/shard_map/ppermute | solution.py:336
  23.3 4.0 %collective-permute-start.7 = (f32[72,128]{1,0:T(8,128)S(1)}, f32[72,128]{1,0:T(8,128)S(1)}, u32[]{:S(2)}, u32[]{:S(2)}) collective-permute-start(f32[72,128]{1,0:T(8,128)S(1)} %field.1.refs_0_), channel_id=1, source_target_pairs={{2,0},{3,1},{0,2},{1,3},{6,4},{7,5},{4,6},{5,7},{10,8},{11,9},{8,1... | collective-permute-start | bytes 110600 | tf_op jit(solution)/shard_map/ppermute | solution.py:336
  27.2 1.4 %collective-permute-start.10 = (f32[288,128]{1,0:T(8,128)S(1)}, f32[288,128]{1,0:T(8,128)S(1)}, u32[]{:S(2)}, u32[]{:S(2)}) collective-permute-start(f32[288,128]{1,0:T(8,128)S(1)} %joined.1.refs_0_), channel_id=1, source_target_pairs={{1,0},{0,1},{3,2},{2,3},{5,4},{4,5},{7,6},{6,7},{9,8},{8,9},{11,10... | collective-permute-start | bytes 442376 | tf_op jit(solution)/shard_map/ppermute | solution.py:336
